TPU v7x, 32 devices: a whole 2x2x4 slice. The times are simulated.
32 devices in a mesh: row: 16 (over z, x, core), head: 2 (over y).
Axes of the slice: x: 2, y: 2, z: 4, core: 2. Of those that a mesh axis runs over, the one named last changes fastest.
Arguments:
- single: bfloat16 [2, 384, 384], replicated, may hold values from -6 to 6
- residue_index: int32 [2, 384], replicated, may hold values from 1 to 768, as said below
- chain_index: int32 [2, 384], replicated, may hold values from 0 to 1, as said below
- token_mask: int32 [2, 384], replicated, may hold values from 0 to 1, as said below
- pair_valid: int32 [2, 384, 384], P(None, 'row', 'head'), may hold values from 0 to 1
- target_bins: int32 [2, 384, 384], P(None, 'row', 'head'), may hold values from 0 to 63
- relative_table: float32 [66, 128], replicated, may hold values from -6 to 6
- single_weight: float32 [384, 256], replicated, may hold values from -0.3125 to 0.3125
- triangle_input: float32 [2, 2, 128, 640], replicated, may hold values from -0.5 to 0.5
- triangle_output: float32 [2, 2, 128, 128], replicated, may hold values from -0.5 to 0.5
- expand_weight: float32 [2, 128, 1024], replicated, may hold values from -0.5 to 0.5
- reduce_weight: float32 [2, 512, 128], replicated, may hold values from -0.25 to 0.25
- distogram_weight: float32 [128, 64], replicated, may hold values from -1 to 1
- norm_gains: float32 [11, 128], replicated, may hold values from 0.5 to 1.5
- first_table: float32 [66, 128], replicated, may hold values from -1.4305115e-06 to 1.4305115e-06
- second_table: float32 [66, 128], replicated, may hold values from 4.4307387e-15 to 1.7722955e-14
- first_single: float32 [384, 256], replicated, may hold values from -1.4305115e-06 to 1.4305115e-06
- second_single: float32 [384, 256], replicated, may hold values from 4.4307387e-15 to 1.7722955e-14
- first_input: float32 [2, 2, 128, 640], replicated, may hold values from -1.4305115e-06 to 1.4305115e-06
- second_input: float32 [2, 2, 128, 640], replicated, may hold values from 4.4307387e-15 to 1.7722955e-14
- first_output: float32 [2, 2, 128, 128], replicated, may hold values from -1.4305115e-06 to 1.4305115e-06
- second_output: float32 [2, 2, 128, 128], replicated, may hold values from 4.4307387e-15 to 1.7722955e-14
- first_expand: float32 [2, 128, 1024], replicated, may hold values from -1.4305115e-06 to 1.4305115e-06
- second_expand: float32 [2, 128, 1024], replicated, may hold values from 4.4307387e-15 to 1.7722955e-14
- first_reduce: float32 [2, 512, 128], replicated, may hold values from -1.4305115e-06 to 1.4305115e-06
- second_reduce: float32 [2, 512, 128], replicated, may hold values from 4.4307387e-15 to 1.7722955e-14
- first_logits: float32 [128, 64], replicated, may hold values from -1.4305115e-06 to 1.4305115e-06
- second_logits: float32 [128, 64], replicated, may hold values from 4.4307387e-15 to 1.7722955e-14
- first_gains: float32 [11, 128], replicated, may hold values from -6.67572e-06 to 6.67572e-06
- second_gains: float32 [11, 128], replicated, may hold values from 1.1076847e-13 to 4.4307388e-13
Outputs:
- loss_sum: float32 [], replicated
- valid_count: float32 [], replicated
- gradient_norm: float32 [], replicated
- table_moment: float32 [66, 128], replicated
- table_square: float32 [66, 128], replicated
- table_master: float32 [66, 128], replicated
- single_moment: float32 [384, 256], replicated
- single_square: float32 [384, 256], replicated
- single_master: float32 [384, 256], replicated
- input_moment: float32 [2, 2, 128, 640], replicated
- input_square: float32 [2, 2, 128, 640], replicated
- input_master: float32 [2, 2, 128, 640], replicated
- output_moment: float32 [2, 2, 128, 128], replicated
- output_square: float32 [2, 2, 128, 128], replicated
- output_master: float32 [2, 2, 128, 128], replicated
- expand_moment: float32 [2, 128, 1024], replicated
- expand_square: float32 [2, 128, 1024], replicated
- expand_master: float32 [2, 128, 1024], replicated
- reduce_moment: float32 [2, 512, 128], replicated
- reduce_square: float32 [2, 512, 128], replicated
- reduce_master: float32 [2, 512, 128], replicated
- logits_moment: float32 [128, 64], replicated
- logits_square: float32 [128, 64], replicated
- logits_master: float32 [128, 64], replicated
- gains_moment: float32 [11, 128], replicated
- gains_square: float32 [11, 128], replicated
- gains_master: float32 [11, 128], replicated
Inputs may be any that keep to these rules, and one draw needn't show every extreme that they name: token_mask is 1 on a prefix of each crop of 192 tokens or more; one crop, drawn from the seed, is whole. chain_index is 0 on a prefix of each crop and 1 on the rest, both present. residue_index rises along each crop, from 1 at its first token to 768 at its last.
All inputs are finite; a program needn't handle non-finite values.
Results may differ from a plain program's by a relative error of at most 0.0069.
Values may be sent and summed in bfloat16 or wider, within the bound.
A program may use at most 832 MiB of HBM per device.

v0:
```python
import jax
import jax.numpy as jnp
from jax import lax
from jax.sharding import PartitionSpec as P

STEP = 10


EPS = 1e-05
BETA_ONE = 0.9
BETA_TWO = 0.999
ADAM_EPS = 1e-08
WEIGHT_RATE = 0.1
GAIN_RATE = 0.5
WEIGHT_DECAY = 0.01
CLIP_NORM = 0.002


def normalize(value):
    mean = jnp.mean(value, axis=-1, keepdims=True)
    centred = value - mean
    scale = lax.rsqrt(jnp.mean(centred * centred, axis=-1, keepdims=True) + EPS)
    return (centred * scale, scale)


def norm_back(grad_out, unit, scale, gain):
    scaled = grad_out * gain
    first_mean = jnp.mean(scaled, axis=-1, keepdims=True)
    second_mean = jnp.mean(scaled * unit, axis=-1, keepdims=True)
    grad_in = scale * (scaled - first_mean - unit * second_mean)
    grad_gain = jnp.sum(grad_out * unit, axis=tuple(range(grad_out.ndim - 1)))
    return (grad_in, grad_gain)


def project(value, weight):
    return jnp.einsum("...c,cd->...d", value, weight, preferred_element_type=jnp.float32)


def project_back(grad, weight):
    return jnp.einsum("...d,cd->...c", grad, weight, preferred_element_type=jnp.float32)


def weight_grad(value, grad):
    return jnp.einsum("bijc,bijd->cd", value, grad, preferred_element_type=jnp.float32)


def triangle_forward(state, weight_in, weight_out, gains, pair_mask, incoming):
    hidden = weight_out.shape[0]
    pair_unit, pair_scale = normalize(state)
    normed = (pair_unit * gains[0]).astype(jnp.bfloat16)
    mixed = project(normed, weight_in)
    mask = pair_mask[..., None]
    left = (mask * jax.nn.sigmoid(mixed[..., :hidden]) * mixed[..., hidden : 2 * hidden]).astype(
        jnp.bfloat16
    )
    right = (
        mask
        * jax.nn.sigmoid(mixed[..., 2 * hidden : 3 * hidden])
        * mixed[..., 3 * hidden : 4 * hidden]
    ).astype(jnp.bfloat16)
    left_cols, right_cols = (
        lax.all_to_all(left, "head", split_axis=3, concat_axis=2, tiled=True),
        lax.all_to_all(right, "head", split_axis=3, concat_axis=2, tiled=True),
    )
    if incoming:
        left_cols, right_cols = (
            lax.all_to_all(left_cols, "row", split_axis=2, concat_axis=1, tiled=True),
            lax.all_to_all(right_cols, "row", split_axis=2, concat_axis=1, tiled=True),
        )
        left_cols = jnp.swapaxes(left_cols, 1, 2)
        right_cols = jnp.swapaxes(right_cols, 1, 2)
    right_all = lax.all_gather(right_cols, "row", axis=1, tiled=True)
    triangle = jnp.einsum(
        "bikc,bjkc->bijc", left_cols, right_all, preferred_element_type=jnp.float32
    )
    triangle = lax.all_to_all(
        triangle.astype(jnp.bfloat16), "head", split_axis=2, concat_axis=3, tiled=True
    )
    tri_unit, tri_scale = normalize(triangle.astype(jnp.float32))
    shaped = (tri_unit * gains[1]).astype(jnp.bfloat16)
    branch = project(shaped, weight_out)
    gate = jax.nn.sigmoid(mixed[..., 4 * hidden :])
    kept = (
        pair_unit,
        pair_scale,
        normed,
        mixed,
        left_cols,
        right_all,
        tri_unit,
        tri_scale,
        shaped,
        branch,
        gate,
    )
    return (state + gate * branch, kept)


def triangle_backward(grad_state, kept, weight_in, weight_out, gains, pair_mask, incoming):
    hidden = weight_out.shape[0]
    (
        pair_unit,
        pair_scale,
        normed,
        mixed,
        left_cols,
        right_all,
        tri_unit,
        tri_scale,
        shaped,
        branch,
        gate,
    ) = kept
    grad_branch = (grad_state * gate).astype(jnp.bfloat16)
    grad_gate = grad_state * branch * gate * (1.0 - gate)
    grad_out = weight_grad(shaped, grad_branch)
    grad_shaped = project_back(grad_branch, weight_out)
    grad_tri, gain_two = norm_back(grad_shaped, tri_unit, tri_scale, gains[1])
    tri_cols = lax.all_to_all(
        grad_tri.astype(jnp.bfloat16), "head", split_axis=3, concat_axis=2, tiled=True
    )
    grad_left = jnp.einsum(
        "bijc,bjkc->bikc", tri_cols, right_all, preferred_element_type=jnp.float32
    )
    grad_left = grad_left.astype(jnp.bfloat16)
    summed = lax.psum_scatter(
        jnp.einsum(
            "bijc,bikc->jbkc", tri_cols, left_cols, preferred_element_type=jnp.float32
        ).astype(jnp.bfloat16),
        "row",
        scatter_dimension=0,
        tiled=True,
    ).astype(jnp.float32)
    grad_right = jnp.transpose(summed, (1, 0, 2, 3)).astype(jnp.bfloat16)
    if incoming:
        grad_left, grad_right = (
            lax.all_to_all(
                jnp.swapaxes(grad_left, 1, 2), "row", split_axis=1, concat_axis=2, tiled=True
            ),
            lax.all_to_all(
                jnp.swapaxes(grad_right, 1, 2), "row", split_axis=1, concat_axis=2, tiled=True
            ),
        )
    back_left, back_right = (
        lax.all_to_all(grad_left, "head", split_axis=2, concat_axis=3, tiled=True),
        lax.all_to_all(grad_right, "head", split_axis=2, concat_axis=3, tiled=True),
    )
    mask = pair_mask[..., None]
    back_left = back_left.astype(jnp.float32) * mask
    back_right = back_right.astype(jnp.float32) * mask
    left_sig = jax.nn.sigmoid(mixed[..., :hidden])
    left_value = mixed[..., hidden : 2 * hidden]
    right_sig = jax.nn.sigmoid(mixed[..., 2 * hidden : 3 * hidden])
    right_value = mixed[..., 3 * hidden : 4 * hidden]
    grad_mixed = jnp.concatenate(
        [
            back_left * left_value * left_sig * (1.0 - left_sig),
            back_left * left_sig,
            back_right * right_value * right_sig * (1.0 - right_sig),
            back_right * right_sig,
            grad_gate,
        ],
        axis=-1,
    ).astype(jnp.bfloat16)
    grad_in = weight_grad(normed, grad_mixed)
    grad_normed = project_back(grad_mixed, weight_in)
    grad_first, gain_one = norm_back(grad_normed, pair_unit, pair_scale, gains[0])
    return (grad_state + grad_first, (grad_in, grad_out, gain_one, gain_two))


def transition_forward(state, weight_up, weight_down, gain):
    expand = weight_down.shape[0]
    unit, scale = normalize(state)
    lifted = (unit * gain).astype(jnp.bfloat16)
    inner = project(lifted, weight_up)
    product = (jax.nn.silu(inner[..., :expand]) * inner[..., expand:]).astype(jnp.bfloat16)
    return (state + project(product, weight_down), (unit, scale, lifted, inner, product))


def transition_backward(grad_state, kept, weight_up, weight_down, gain):
    expand = weight_down.shape[0]
    unit, scale, lifted, inner, product = kept
    grad_low = grad_state.astype(jnp.bfloat16)
    grad_down = weight_grad(product, grad_low)
    grad_product = project_back(grad_low, weight_down)
    gate_part = inner[..., :expand]
    up_part = inner[..., expand:]
    gate_sig = jax.nn.sigmoid(gate_part)
    silu_value = gate_part * gate_sig
    silu_slope = gate_sig * (1.0 + gate_part * (1.0 - gate_sig))
    grad_inner = jnp.concatenate(
        [grad_product * up_part * silu_slope, grad_product * silu_value], axis=-1
    )
    grad_inner = grad_inner.astype(jnp.bfloat16)
    grad_up = weight_grad(lifted, grad_inner)
    grad_lifted = project_back(grad_inner, weight_up)
    grad_middle, gain_grad = norm_back(grad_lifted, unit, scale, gain)
    return (grad_middle + grad_state, (grad_up, grad_down, gain_grad))


def block_forward(state, weight_in, weight_out, weight_up, weight_down, gains, pair_mask):
    first, kept_one = triangle_forward(
        state, weight_in[0], weight_out[0], gains[0:2], pair_mask, False
    )
    second, kept_two = triangle_forward(
        first, weight_in[1], weight_out[1], gains[2:4], pair_mask, True
    )
    output, kept_three = transition_forward(second, weight_up, weight_down, gains[4])
    return (output, (kept_one, kept_two, kept_three))


def block_backward(
    grad_state, state, weight_in, weight_out, weight_up, weight_down, gains, pair_mask
):
    skipped, kept = block_forward(
        state, weight_in, weight_out, weight_up, weight_down, gains, pair_mask
    )
    kept_one, kept_two, kept_three = kept
    grad_state, (grad_up, grad_down, gain_five) = transition_backward(
        grad_state, kept_three, weight_up, weight_down, gains[4]
    )
    grad_state, (in_two, out_two, gain_three, gain_four) = triangle_backward(
        grad_state, kept_two, weight_in[1], weight_out[1], gains[2:4], pair_mask, True
    )
    grad_state, (in_one, out_one, gain_one, gain_two) = triangle_backward(
        grad_state, kept_one, weight_in[0], weight_out[0], gains[0:2], pair_mask, False
    )
    return (
        grad_state,
        (
            jnp.stack([in_one, in_two]),
            jnp.stack([out_one, out_two]),
            grad_up,
            grad_down,
            jnp.stack([gain_one, gain_two, gain_three, gain_four, gain_five]),
        ),
    )


def adamw(weight, grad, first, second, rate, decay):
    first_new = BETA_ONE * first + (1.0 - BETA_ONE) * grad
    second_new = BETA_TWO * second + (1.0 - BETA_TWO) * grad * grad
    moved = (
        first_new
        / (1.0 - BETA_ONE**STEP)
        / (jnp.sqrt(second_new / (1.0 - BETA_TWO**STEP)) + ADAM_EPS)
    )
    return (first_new, second_new, weight - rate * (moved + decay * weight))


def per_device(
    single,
    residue_index,
    chain_index,
    token_mask,
    pair_valid,
    target_bins,
    relative_table,
    single_weight,
    triangle_input,
    triangle_output,
    expand_weight,
    reduce_weight,
    distogram_weight,
    norm_gains,
    first_table,
    second_table,
    first_single,
    second_single,
    first_input,
    second_input,
    first_output,
    second_output,
    first_expand,
    second_expand,
    first_reduce,
    second_reduce,
    first_logits,
    second_logits,
    first_gains,
    second_gains,
):
    crops, rows, cols = pair_valid.shape
    width = relative_table.shape[1]
    layers = triangle_input.shape[0]
    row_start = lax.axis_index("row") * rows
    col_start = lax.axis_index("head") * cols

    def take(array, start, count):
        return lax.dynamic_slice_in_dim(array, start, count, 1)

    offset = (
        take(residue_index, row_start, rows)[:, :, None]
        - take(residue_index, col_start, cols)[:, None, :]
    )
    same = (
        take(chain_index, row_start, rows)[:, :, None]
        == take(chain_index, col_start, cols)[:, None, :]
    )
    reach = (relative_table.shape[0] - 2) // 2
    bins = jnp.where(same, jnp.clip(offset, -reach, reach) + reach, 2 * reach + 1)
    relative_hot = (
        bins[..., None] == jnp.arange(relative_table.shape[0])[None, None, None, :]
    ).astype(jnp.float32)
    token_rows = take(token_mask, row_start, rows).astype(jnp.float32)
    token_cols = take(token_mask, col_start, cols).astype(jnp.float32)
    pair_mask = token_rows[:, :, None] * token_cols[:, None, :]
    loss_weight = pair_mask * pair_valid.astype(jnp.float32)
    low_input = triangle_input.astype(jnp.bfloat16)
    low_output = triangle_output.astype(jnp.bfloat16)
    low_expand = expand_weight.astype(jnp.bfloat16)
    low_reduce = reduce_weight.astype(jnp.bfloat16)
    low_logits = distogram_weight.astype(jnp.bfloat16)
    proj = project(single, single_weight.astype(jnp.bfloat16))
    state = project(relative_hot.astype(jnp.bfloat16), relative_table.astype(jnp.bfloat16))
    state = (
        state
        + take(proj, row_start, rows)[:, :, None, :width]
        + take(proj, col_start, cols)[:, None, :, width:]
    )
    inputs = []
    for layer in range(layers):
        inputs.append(state)
        state, unused = block_forward(
            state,
            low_input[layer],
            low_output[layer],
            low_expand[layer],
            low_reduce[layer],
            norm_gains[5 * layer : 5 * layer + 5],
            pair_mask,
        )
    head_unit, head_scale = normalize(state)
    shown = (head_unit * norm_gains[5 * layers]).astype(jnp.bfloat16)
    logits = project(shown, low_logits)
    largest = jnp.max(logits, axis=-1, keepdims=True)
    log_total = largest + jnp.log(jnp.sum(jnp.exp(logits - largest), axis=-1, keepdims=True))
    target_hot = (
        target_bins[..., None] == jnp.arange(logits.shape[-1])[None, None, None, :]
    ).astype(jnp.float32)
    picked = jnp.sum(logits * target_hot, axis=-1)
    loss_local = jnp.sum(loss_weight * (log_total[..., 0] - picked))
    grad_scores = (loss_weight[..., None] * (jnp.exp(logits - log_total) - target_hot)).astype(
        jnp.bfloat16
    )
    grad_logits = weight_grad(shown, grad_scores)
    grad_shown = project_back(grad_scores, low_logits)
    grad_state, gain_last = norm_back(grad_shown, head_unit, head_scale, norm_gains[5 * layers])
    collected = []
    for layer in reversed(range(layers)):
        grad_state, layer_grads = block_backward(
            grad_state,
            inputs[layer],
            low_input[layer],
            low_output[layer],
            low_expand[layer],
            low_reduce[layer],
            norm_gains[5 * layer : 5 * layer + 5],
            pair_mask,
        )
        collected.insert(0, layer_grads)
    grad_input = jnp.stack([entry[0] for entry in collected])
    grad_output = jnp.stack([entry[1] for entry in collected])
    grad_expand = jnp.stack([entry[2] for entry in collected])
    grad_reduce = jnp.stack([entry[3] for entry in collected])
    grad_gains = jnp.concatenate(
        [jnp.concatenate([entry[4] for entry in collected], axis=0), gain_last[None]], axis=0
    )
    grad_table = jnp.einsum(
        "bijr,bijc->rc", relative_hot, grad_state, precision=lax.Precision.HIGHEST
    )
    single_wide = single.astype(jnp.float32)
    row_part = jnp.einsum(
        "bis,bic->sc",
        take(single_wide, row_start, rows),
        jnp.sum(grad_state, axis=2),
        precision=lax.Precision.HIGHEST,
    )
    col_part = jnp.einsum(
        "bjs,bjc->sc",
        take(single_wide, col_start, cols),
        jnp.sum(grad_state, axis=1),
        precision=lax.Precision.HIGHEST,
    )
    grad_single = jnp.concatenate([row_part, col_part], axis=1)
    local_count = jnp.sum(loss_weight)
    valid_count = lax.psum(local_count, ("row", "head"))
    summed = lax.psum(
        (
            grad_table / valid_count,
            grad_single / valid_count,
            grad_input / valid_count,
            grad_output / valid_count,
            grad_expand / valid_count,
            grad_reduce / valid_count,
            grad_logits / valid_count,
            grad_gains / valid_count,
            loss_local,
        ),
        ("row", "head"),
    )
    grads = list(summed[:8])
    loss_sum = summed[8]
    squares = jnp.zeros((), jnp.float32)
    for g in grads:
        squares = squares + jnp.sum(g * g)
    gradient_norm = jnp.sqrt(squares)
    factor = jnp.minimum(1.0, CLIP_NORM / (gradient_norm + 1e-06))
    weights = (
        relative_table,
        single_weight,
        triangle_input,
        triangle_output,
        expand_weight,
        reduce_weight,
        distogram_weight,
        norm_gains,
    )
    firsts = (
        first_table,
        first_single,
        first_input,
        first_output,
        first_expand,
        first_reduce,
        first_logits,
        first_gains,
    )
    seconds = (
        second_table,
        second_single,
        second_input,
        second_output,
        second_expand,
        second_reduce,
        second_logits,
        second_gains,
    )
    result = []
    for index in range(8):
        rate = GAIN_RATE if index == 7 else WEIGHT_RATE
        decay = 0.0 if index == 7 else WEIGHT_DECAY
        result.extend(
            adamw(weights[index], grads[index] * factor, firsts[index], seconds[index], rate, decay)
        )
    return (
        loss_sum,
        valid_count,
        gradient_norm,
        result[0],
        result[1],
        result[2],
        result[3],
        result[4],
        result[5],
        result[6],
        result[7],
        result[8],
        result[9],
        result[10],
        result[11],
        result[12],
        result[13],
        result[14],
        result[15],
        result[16],
        result[17],
        result[18],
        result[19],
        result[20],
        result[21],
        result[22],
        result[23],
    )


def solution(mesh):
    placed = (
        P(),
        P(),
        P(),
        P(),
        P(None, "row", "head"),
        P(None, "row", "head"),
        P(),
        P(),
        P(),
        P(),
        P(),
        P(),
        P(),
        P(),
        P(),
        P(),
        P(),
        P(),
        P(),
        P(),
        P(),
        P(),
        P(),
        P(),
        P(),
        P(),
        P(),
        P(),
        P(),
        P(),
    )
    return jax.shard_map(
        per_device,
        mesh=mesh,
        in_specs=placed,
        out_specs=(
            P(),
            P(),
            P(),
            P(),
            P(),
            P(),
            P(),
            P(),
            P(),
            P(),
            P(),
            P(),
            P(),
            P(),
            P(),
            P(),
            P(),
            P(),
            P(),
            P(),
            P(),
            P(),
            P(),
            P(),
            P(),
            P(),
            P(),
        ),
        check_vma=False,
    )
```

profile of v0, /device:TPU:0, one launch (start us, length us, event | category | flops | bytes accessed | tf_op | source)
XLA Modules:
  0.0 4826.3 jit_solution(11402604057798744784)
XLA Ops:
  45.6 41.8 all_to_all.548
  104.7 40.2 all_to_all.549
  157.8 131.8 %all-gather.5.cloned.1.call-done = bf16[2,384,384,64]{2,1,3,0:T(8,128)(2,1)} async-done(((bf16[2,24,384,64]{2,1,3,0:T(8,128)(2,1)}), bf16[2,384,384,64]{2,1,3,0:T(8,128)(2,1)}) %all-gather.5.cloned.1.call-update) | async-done | bytes 37748752 | tf_op jit(solution)/shard_map/all_gather | solution.py:72
  415.0 42.7 all_to_all.550
  474.6 58.8 %all_to_all.551 = bf16[16,2,36864]{2,1,0:T(2,128)(2,1)} all-to-all(bf16[16,2,36864]{2,1,0:T(2,128)(2,1)} %reshape.477), channel_id=1, replica_groups=mesh['row'=16,'head'=2] {'row'}, dimensions={0} | all-to-all | bytes 4718592 | tf_op jit(solution)/shard_map/all_to_all | solution.py:68
  557.5 44.0 all_to_all.552
  617.3 85.3 %all_to_all.553 = bf16[16,2,36864]{2,1,0:T(2,128)(2,1)} all-to-all(bf16[16,2,36864]{2,1,0:T(2,128)(2,1)S(1)} %reshape.479), channel_id=1, replica_groups=mesh['row'=16,'head'=2] {'row'}, dimensions={0} | all-to-all | bytes 4718592 | tf_op jit(solution)/shard_map/all_to_all | solution.py:67
  722.4 55.6 %all-gather.7.cloned.1.call-done = bf16[2,384,384,64]{2,1,3,0:T(8,128)(2,1)} async-done(((bf16[2,24,384,64]{2,1,3,0:T(8,128)(2,1)}), bf16[2,384,384,64]{2,1,3,0:T(8,128)(2,1)}) %all-gather.7.cloned.1.call-update) | async-done | bytes 37748752 | tf_op jit(solution)/shard_map/all_gather | solution.py:72
  939.4 39.9 all_to_all.554
  1048.6 143.2 %all-gather.9.cloned.1.call-done = bf16[2,384,384,64]{2,1,3,0:T(8,128)(2,1)} async-done(((bf16[2,24,384,64]{2,1,3,0:T(8,128)(2,1)}), bf16[2,384,384,64]{2,1,3,0:T(8,128)(2,1)}) %all-gather.9.cloned.1.call-update) | async-done | bytes 37748752 | tf_op jit(solution)/shard_map/all_gather | solution.py:72
  1317.2 42.6 all_to_all.556
  1376.8 58.8 %all_to_all.557 = bf16[16,2,36864]{2,1,0:T(2,128)(2,1)} all-to-all(bf16[16,2,36864]{2,1,0:T(2,128)(2,1)} %reshape.485), channel_id=1, replica_groups=mesh['row'=16,'head'=2] {'row'}, dimensions={0} | all-to-all | bytes 4718592 | tf_op jit(solution)/shard_map/all_to_all | solution.py:68
  1459.5 44.0 all_to_all.558
  1519.4 85.4 %all_to_all.559 = bf16[16,2,36864]{2,1,0:T(2,128)(2,1)} all-to-all(bf16[16,2,36864]{2,1,0:T(2,128)(2,1)S(1)} %reshape.487), channel_id=1, replica_groups=mesh['row'=16,'head'=2] {'row'}, dimensions={0} | all-to-all | bytes 4718592 | tf_op jit(solution)/shard_map/all_to_all | solution.py:67
  1624.5 55.7 %all-gather.11.cloned.1.call-done = bf16[2,384,384,64]{2,1,3,0:T(8,128)(2,1)} async-done(((bf16[2,24,384,64]{2,1,3,0:T(8,128)(2,1)}), bf16[2,384,384,64]{2,1,3,0:T(8,128)(2,1)}) %all-gather.11.cloned.1.call-update) | async-done | bytes 37748752 | tf_op jit(solution)/shard_map/all_gather | solution.py:72
  1918.6 39.9 all_to_all.560
  1990.3 47.5 copy.473
  2069.7 115.6 %all_to_all.561 = bf16[16,2,36864]{2,1,0:T(2,128)(2,1)} all-to-all(bf16[16,2,36864]{2,1,0:T(2,128)(2,1)S(1)} %reshape.491), channel_id=1, replica_groups=mesh['row'=16,'head'=2] {'row'}, dimensions={0} | all-to-all | bytes 4718592 | tf_op jit(solution)/shard_map/all_to_all | solution.py:137
  2212.2 237.4 %reduce-scatter.5.cloned.1.call-done = bf16[24,2,384,64]{2,3,1,0:T(8,128)(2,1)} async-done(((bf16[384,2,384,64]{2,3,1,0:T(8,128)(2,1)}), bf16[24,2,384,64]{2,3,1,0:T(8,128)(2,1)}) %reduce-scatter.5.cloned.1.call-update) | async-done | bytes 2359312 | tf_op jit(solution)/shard_map/reduce_scatter | solution.py:126
  2656.9 40.5 all_to_all.562
  2729.1 47.5 copy.487
  2859.2 291.1 %reduce-scatter.7.cloned.1.call-done = bf16[24,2,384,64]{2,3,1,0:T(8,128)(2,1)} async-done(((bf16[384,2,384,64]{2,3,1,0:T(8,128)(2,1)}), bf16[24,2,384,64]{2,3,1,0:T(8,128)(2,1)}) %reduce-scatter.7.cloned.1.call-update) | async-done | bytes 2359312 | tf_op jit(solution)/shard_map/reduce_scatter | solution.py:126
  3310.5 39.5 all_to_all.563
  3381.6 47.5 copy.503
  3467.6 96.4 %all_to_all.564 = bf16[16,2,36864]{2,1,0:T(2,128)(2,1)} all-to-all(bf16[16,2,36864]{2,1,0:T(2,128)(2,1)S(1)} %reshape.503), channel_id=1, replica_groups=mesh['row'=16,'head'=2] {'row'}, dimensions={0} | all-to-all | bytes 4718592 | tf_op jit(solution)/shard_map/all_to_all | solution.py:137
  3590.9 236.3 %reduce-scatter.9.cloned.1.call-done = bf16[24,2,384,64]{2,3,1,0:T(8,128)(2,1)} async-done(((bf16[384,2,384,64]{2,3,1,0:T(8,128)(2,1)}), bf16[24,2,384,64]{2,3,1,0:T(8,128)(2,1)}) %reduce-scatter.9.cloned.1.call-update) | async-done | bytes 2359312 | tf_op jit(solution)/shard_map/reduce_scatter | solution.py:126
  4034.4 40.7 all_to_all.565
  4106.9 47.4 copy.517
  4154.3 46.2 psum.71
  4363.7 163.7 %reduce-scatter.11.cloned.1.call-done = bf16[24,2,384,64]{2,3,1,0:T(8,128)(2,1)} async-done(((bf16[384,2,384,64]{2,3,1,0:T(8,128)(2,1)}), bf16[24,2,384,64]{2,3,1,0:T(8,128)(2,1)}) %reduce-scatter.11.cloned.1.call-update) | async-done | bytes 2359312 | tf_op jit(solution)/shard_map/reduce_scatter | solution.py:126
  4655.4 40.2 all-reduce.6
  4697.5 83.8 %all-reduce.5.cloned.1.call-done = (f32[384,256]{0,1:T(8,128)}, f32[2,2,128,640]{3,2,1,0:T(8,128)}, f32[2,2,128,128]{3,2,1,0:T(8,128)}, f32[2,128,1024]{2,1,0:T(8,128)}, f32[2,512,128]{2,1,0:T(8,128)}) async-done(((f32[384,256]{0,1:T(8,128)}, f32[2,2,128,640]{3,2,1,0:T(8,128)}, f32[2,2,128,128]{3,2,1,0:T(8,128)}, f32[2,128,1024]{2,1,0:T(8,128)}, f32[2,512,128]{2,1,0:T(8,128)}), (f32[384,256]{0,1:T(8,128)}, ...) | async-done | bytes 3538960 | tf_op jit(solution)/shard_map/psum | solution.py:388
  (877 shorter events, 2171.1 us)
Async XLA Ops:
  7.2 282.4 %all-gather.5.cloned.1.call-start = ((), (), s32[]{:S(2)}) async-start(), calls=%async_computation.36 | async-start | bytes 40108032 | tf_op jit(solution)/shard_map/all_gather | solution.py:72
  12.5 378.3 %copy-start.139 = (f32[128]{0:T(128)}, f32[128]{0:T(128)S(1)}, u32[]{:S(2)}) copy-start(f32[128]{0:T(128)S(1)} %get-tuple-element.280) | copy-start | bytes 1540
  22.4 1280.7 %copy-start.30 = (f32[2,24,192]{2,1,0:T(8,128)}, f32[2,24,192]{2,1,0:T(8,128)S(1)}, u32[]{:S(2)}) copy-start(f32[2,24,192]{2,1,0:T(8,128)S(1)} %broadcast_multiply_fusion.33) | copy-start | bytes 110596
  157.8 158.3 %copy-start.22 = (bf16[2,24,384,64]{2,1,3,0:T(8,128)(2,1)}, bf16[2,24,384,64]{2,1,3,0:T(8,128)(2,1)S(1)}, u32[]{:S(2)}) copy-start(bf16[2,24,384,64]{2,1,3,0:T(8,128)(2,1)S(1)} %all_to_all.191) | copy-start | bytes 7077892
  329.4 32.1 all-to-all-start.2
  333.2 444.9 %all-gather.7.cloned.1.call-start = ((), (), s32[]{:S(2)}) async-start(), calls=%async_computation.37 | async-start | bytes 40108032 | tf_op jit(solution)/shard_map/all_gather | solution.py:72
  722.4 82.1 %copy-start.20 = (bf16[2,384,24,64]{1,2,3,0:T(8,128)(2,1)}, bf16[2,384,24,64]{1,2,3,0:T(8,128)(2,1)S(1)}, u32[]{:S(2)}) copy-start(bf16[2,384,24,64]{1,2,3,0:T(8,128)(2,1)S(1)} %copy.431) | copy-start | bytes 7077892
  817.8 32.1 all-to-all-start.7
  821.6 370.3 %all-gather.9.cloned.1.call-start = ((), (), s32[]{:S(2)}) async-start(), calls=%async_computation.38 | async-start | bytes 40108032 | tf_op jit(solution)/shard_map/all_gather | solution.py:72
  1048.6 169.6 %copy-start.24 = (bf16[2,24,384,64]{2,1,3,0:T(8,128)(2,1)}, bf16[2,24,384,64]{2,1,3,0:T(8,128)(2,1)S(1)}, u32[]{:S(2)}) copy-start(bf16[2,24,384,64]{2,1,3,0:T(8,128)(2,1)S(1)} %all_to_all.217) | copy-start | bytes 7077892
  1231.4 32.1 all-to-all-start.10
  1235.2 445.1 %all-gather.11.cloned.1.call-start = ((), (), s32[]{:S(2)}) async-start(), calls=%async_computation.39 | async-start | bytes 40108032 | tf_op jit(solution)/shard_map/all_gather | solution.py:72
  1719.9 33.3 all-to-all-start.15
  1724.8 724.7 %reduce-scatter.5.cloned.1.call-start = ((), (), s32[]{:S(2)}) async-start(), calls=%async_computation.40 | async-start | bytes 40108032 | tf_op jit(solution)/shard_map/reduce_scatter | solution.py:126
  1772.0 134.4 %copy-start.62 = (f32[2,24,192]{2,1,0:T(8,128)}, f32[2,24,192]{2,1,0:T(8,128)S(1)}, u32[]{:S(2)}) copy-start(f32[2,24,192]{2,1,0:T(8,128)S(1)} %broadcast_multiply_fusion.24) | copy-start | bytes 110596
  2208.3 255.4 %all-to-all-start.18 = ((bf16[2,2,294912]{2,1,0:T(2,128)(2,1)}), bf16[2,2,294912]{2,1,0:T(2,128)(2,1)S(1)}, u32[]{:S(2)}, u32[]{:S(2)}) async-start(bf16[2,2,294912]{2,1,0:T(2,128)(2,1)} %reshape.493), calls=%async_computation.18 | async-start | bytes 4718592 | tf_op jit(solution)/shard_map/all_to_all | solution.py:145
  2463.7 50.5 %all-to-all-start.19 = ((bf16[16,2,36864]{2,1,0:T(2,128)(2,1)}), bf16[16,2,36864]{2,1,0:T(2,128)(2,1)}, u32[]{:S(2)}, u32[]{:S(2)}) async-start(bf16[16,2,36864]{2,1,0:T(2,128)(2,1)} %reshape.495), calls=%async_computation.20 | async-start | bytes 4718592 | tf_op jit(solution)/shard_map/all_to_all | solution.py:140
  2537.3 32.7 all-to-all-start.20
  2541.1 609.2 %reduce-scatter.7.cloned.1.call-start = ((), (), s32[]{:S(2)}) async-start(), calls=%async_computation.41 | async-start | bytes 40108032 | tf_op jit(solution)/shard_map/reduce_scatter | solution.py:126
  2810.4 30.5 all-to-all-start.22
  3162.9 31.8 all-to-all-start.23
  3166.7 660.5 %reduce-scatter.9.cloned.1.call-start = ((), (), s32[]{:S(2)}) async-start(), calls=%async_computation.42 | async-start | bytes 40108032 | tf_op jit(solution)/shard_map/reduce_scatter | solution.py:126
  3587.1 254.3 %all-to-all-start.26 = ((bf16[2,2,294912]{2,1,0:T(2,128)(2,1)}), bf16[2,2,294912]{2,1,0:T(2,128)(2,1)S(1)}, u32[]{:S(2)}, u32[]{:S(2)}) async-start(bf16[2,2,294912]{2,1,0:T(2,128)(2,1)} %reshape.505), calls=%async_computation.28 | async-start | bytes 4718592 | tf_op jit(solution)/shard_map/all_to_all | solution.py:145
  3841.4 50.5 %all-to-all-start.27 = ((bf16[16,2,36864]{2,1,0:T(2,128)(2,1)}), bf16[16,2,36864]{2,1,0:T(2,128)(2,1)}, u32[]{:S(2)}, u32[]{:S(2)}) async-start(bf16[16,2,36864]{2,1,0:T(2,128)(2,1)} %reshape.507), calls=%async_computation.30 | async-start | bytes 4718592 | tf_op jit(solution)/shard_map/all_to_all | solution.py:140
  3914.9 32.7 all-to-all-start.28
  3918.7 608.7 %reduce-scatter.11.cloned.1.call-start = ((), (), s32[]{:S(2)}) async-start(), calls=%async_computation.43 | async-start | bytes 40108032 | tf_op jit(solution)/shard_map/reduce_scatter | solution.py:126
  4310.3 33.0 all-to-all-start.30
  4540.2 31.8 all-to-all-start.31
  4544.0 237.4 %all-reduce.5.cloned.1.call-start = ((), (), s32[]{:S(2)}) async-start(), calls=%async_computation.44 | async-start | bytes 7077888 | tf_op jit(solution)/shard_map/psum | solution.py:388
  4655.4 150.3 %copy-start.128 = (f32[128,64]{0,1:T(8,128)S(1)}, f32[128,64]{0,1:T(8,128)}, u32[]{:S(2)}) copy-start(f32[128,64]{0,1:T(8,128)} %param.42) | copy-start | bytes 98308
  4655.4 153.2 %copy-start.103 = (f32[2,2,128,128]{3,2,1,0:T(8,128)S(1)}, f32[2,2,128,128]{3,2,1,0:T(8,128)}, u32[]{:S(2)}) copy-start(f32[2,2,128,128]{3,2,1,0:T(8,128)} %param.39) | copy-start | bytes 786436
  4695.7 100.4 %copy-start.129 = (f32[128,64]{0,1:T(8,128)}, f32[128,64]{0,1:T(8,128)S(1)}, u32[]{:S(2)}) copy-start(f32[128,64]{0,1:T(8,128)S(1)} %get-tuple-element.207) | copy-start | bytes 98308
  (223 other events, 2614.8 us)
Sparse Core Ops, SparseCore 0:
  101.4 188.2 all-gather.4
  554.1 223.9 all-gather.6
  993.3 198.5 all-gather.8
  1456.2 224.0 all-gather.10
  2037.9 411.6 reduce-scatter.4
  2776.8 373.4 reduce-scatter.6
  3429.2 397.9 reduce-scatter.8
  4154.4 372.9 reduce-scatter.10
  4641.5 139.7 all-reduce.4
where the time goes:
time: 4850 us; the launch traced here: 4830 us
  waiting for transfers between devices  1610 us (33%)
  blocking collectives  1080 us (22%)
  local copies, waits for them, and re-layouts  1050 us (22%)
  matrix products  623 us (13%)
  other arithmetic  378 us (8%)
  starting transfers between devices  58.8 us (1%)
    reduce_scatter x4, waiting for transfers between devices, triangle_backward(): lax.psum_scatter(jnp.einsum('bijc,bikc->jbkc', tri_cols, left_cols, prefe...  929 us
    all_gather x4, waiting for transfers between devices, triangle_forward(): right_all = lax.all_gather(right_cols, 'row', axis=1, tiled=True)  386 us
    unnamed x510, local copies, waits for them, and re-layouts  273 us
    all_to_all x2, blocking collectives, triangle_backward(): lax.all_to_all(jnp.swapaxes(grad_left, 1, 2), 'row', split_axis=1, concat...  212 us
    convert_element_type x4, local copies, waits for them, and re-layouts, triangle_backward(): summed = lax.psum_scatter(jnp.einsum('bijc,bikc->jbkc', tri_cols, left_co...  190 us
    all_to_all x2, blocking collectives, triangle_forward(): lax.all_to_all(left_cols, 'row', split_axis=2, concat_axis=1, tiled=True)  171 us
    all_to_all x4, blocking collectives, triangle_forward(): lax.all_to_all(left, 'head', split_axis=3, concat_axis=2, tiled=True)  167 us
    all_to_all x4, blocking collectives, triangle_forward(): lax.all_to_all(right, 'head', split_axis=3, concat_axis=2, tiled=True)  167 us
  transfers between devices with their start and end apart: 23, of which 21 were waited for; matrix products, arithmetic and copies ran while one was open for 12% of the time, Pallas kernels for 0%

commit v1 on v0

--- a/solution.py
+++ b/solution.py
@@ -1,6 +1,10 @@
+import functools
+
 import jax
 import jax.numpy as jnp
 from jax import lax
+from jax.experimental import pallas as pl
+from jax.experimental.pallas import tpu as pltpu
 from jax.sharding import PartitionSpec as P
 
 STEP = 10
@@ -248,7 +252,969 @@
     return (first_new, second_new, weight - rate * (moved + decay * weight))
 
 
+def gradients_by_block(
+    single,
+    residue_index,
+    chain_index,
+    token_mask,
+    pair_valid,
+    target_bins,
+    relative_table,
+    single_weight,
+    triangle_input,
+    triangle_output,
+    expand_weight,
+    reduce_weight,
+    distogram_weight,
+    norm_gains,
+):
+    crops, rows, cols = pair_valid.shape
+    width = relative_table.shape[1]
+    layers = triangle_input.shape[0]
+    row_start = lax.axis_index("row") * rows
+    col_start = lax.axis_index("head") * cols
+
+    def take(array, start, count):
+        return lax.dynamic_slice_in_dim(array, start, count, 1)
+
+    offset = (
+        take(residue_index, row_start, rows)[:, :, None]
+        - take(residue_index, col_start, cols)[:, None, :]
+    )
+    same = (
+        take(chain_index, row_start, rows)[:, :, None]
+        == take(chain_index, col_start, cols)[:, None, :]
+    )
+    reach = (relative_table.shape[0] - 2) // 2
+    bins = jnp.where(same, jnp.clip(offset, -reach, reach) + reach, 2 * reach + 1)
+    relative_hot = (
+        bins[..., None] == jnp.arange(relative_table.shape[0])[None, None, None, :]
+    ).astype(jnp.float32)
+    token_rows = take(token_mask, row_start, rows).astype(jnp.float32)
+    token_cols = take(token_mask, col_start, cols).astype(jnp.float32)
+    pair_mask = token_rows[:, :, None] * token_cols[:, None, :]
+    loss_weight = pair_mask * pair_valid.astype(jnp.float32)
+    low_input = triangle_input.astype(jnp.bfloat16)
+    low_output = triangle_output.astype(jnp.bfloat16)
+    low_expand = expand_weight.astype(jnp.bfloat16)
+    low_reduce = reduce_weight.astype(jnp.bfloat16)
+    low_logits = distogram_weight.astype(jnp.bfloat16)
+    proj = project(single, single_weight.astype(jnp.bfloat16))
+    state = project(relative_hot.astype(jnp.bfloat16), relative_table.astype(jnp.bfloat16))
+    state = (
+        state
+        + take(proj, row_start, rows)[:, :, None, :width]
+        + take(proj, col_start, cols)[:, None, :, width:]
+    )
+    inputs = []
+    for layer in range(layers):
+        inputs.append(state)
+        state, unused = block_forward(
+            state,
+            low_input[layer],
+            low_output[layer],
+            low_expand[layer],
+            low_reduce[layer],
+            norm_gains[5 * layer : 5 * layer + 5],
+            pair_mask,
+        )
+    head_unit, head_scale = normalize(state)
+    shown = (head_unit * norm_gains[5 * layers]).astype(jnp.bfloat16)
+    logits = project(shown, low_logits)
+    largest = jnp.max(logits, axis=-1, keepdims=True)
+    log_total = largest + jnp.log(jnp.sum(jnp.exp(logits - largest), axis=-1, keepdims=True))
+    target_hot = (
+        target_bins[..., None] == jnp.arange(logits.shape[-1])[None, None, None, :]
+    ).astype(jnp.float32)
+    picked = jnp.sum(logits * target_hot, axis=-1)
+    loss_local = jnp.sum(loss_weight * (log_total[..., 0] - picked))
+    grad_scores = (loss_weight[..., None] * (jnp.exp(logits - log_total) - target_hot)).astype(
+        jnp.bfloat16
+    )
+    grad_logits = weight_grad(shown, grad_scores)
+    grad_shown = project_back(grad_scores, low_logits)
+    grad_state, gain_last = norm_back(grad_shown, head_unit, head_scale, norm_gains[5 * layers])
+    collected = []
+    for layer in reversed(range(layers)):
+        grad_state, layer_grads = block_backward(
+            grad_state,
+            inputs[layer],
+            low_input[layer],
+            low_output[layer],
+            low_expand[layer],
+            low_reduce[layer],
+            norm_gains[5 * layer : 5 * layer + 5],
+            pair_mask,
+        )
+        collected.insert(0, layer_grads)
+    grad_input = jnp.stack([entry[0] for entry in collected])
+    grad_output = jnp.stack([entry[1] for entry in collected])
+    grad_expand = jnp.stack([entry[2] for entry in collected])
+    grad_reduce = jnp.stack([entry[3] for entry in collected])
+    grad_gains = jnp.concatenate(
+        [jnp.concatenate([entry[4] for entry in collected], axis=0), gain_last[None]], axis=0
+    )
+    grad_table = jnp.einsum(
+        "bijr,bijc->rc", relative_hot, grad_state, precision=lax.Precision.HIGHEST
+    )
+    single_wide = single.astype(jnp.float32)
+    row_part = jnp.einsum(
+        "bis,bic->sc",
+        take(single_wide, row_start, rows),
+        jnp.sum(grad_state, axis=2),
+        precision=lax.Precision.HIGHEST,
+    )
+    col_part = jnp.einsum(
+        "bjs,bjc->sc",
+        take(single_wide, col_start, cols),
+        jnp.sum(grad_state, axis=1),
+        precision=lax.Precision.HIGHEST,
+    )
+    grad_single = jnp.concatenate([row_part, col_part], axis=1)
+    return (
+        loss_local,
+        jnp.sum(loss_weight),
+        grad_table,
+        grad_single,
+        grad_input,
+        grad_output,
+        grad_expand,
+        grad_reduce,
+        grad_logits,
+        grad_gains,
+    )
+
+
+F32 = jnp.float32
+BF16 = jnp.bfloat16
+LANES = 128
+SUBLANES = 8
+VMEM_BYTES = 58 * 2**20
+ROW_BLOCK = 2
+MESH = pl.DeviceIdType.MESH
+
+
+def dot(left, right):
+    return lax.dot_general(left, right, (((1,), (0,)), ((), ())), preferred_element_type=F32)
+
+
+def dot_pairs(left, right):
+    return lax.dot_general(left, right, (((1,), (1,)), ((), ())), preferred_element_type=F32)
+
+
+def sigmoid(value):
+    return 0.5 * jnp.tanh(0.5 * value) + 0.5
+
+
+def unit_of(value):
+    centred = value - jnp.mean(value, axis=0, keepdims=True)
+    scale = lax.rsqrt(jnp.mean(centred * centred, axis=0, keepdims=True) + EPS)
+    return (centred * scale, scale)
+
+
+def unit_back(grad, unit, scale, gain):
+    scaled = grad * gain
+    first = jnp.mean(scaled, axis=0, keepdims=True)
+    second = jnp.mean(scaled * unit, axis=0, keepdims=True)
+    return scale * (scaled - first - unit * second)
+
+
+def fold(value):
+    total = value[:, :LANES]
+    for start in range(LANES, value.shape[1], LANES):
+        total = total + value[:, start : start + LANES]
+    return total
+
+
+def read_rows(ref):
+    return jnp.concatenate([ref[row] for row in range(ref.shape[0])], axis=1)
+
+
+def write_rows(ref, value):
+    cols = ref.shape[2]
+    for row in range(ref.shape[0]):
+        ref[row] = value[:, row * cols : (row + 1) * cols].astype(ref.dtype)
+
+
+def read_wire(ref):
+    peers, rows, _ = ref.shape
+    pieces = []
+    for peer in range(peers):
+        piece = ref[peer].astype(F32)
+        pieces.append(
+            jnp.concatenate(
+                [piece[start : start + SUBLANES] for start in range(0, rows, SUBLANES)], axis=1
+            )
+        )
+    return jnp.concatenate(pieces, axis=0)
+
+
+def write_wire_piece(ref, peer, value):
+    cols = ref.shape[2]
+    ref[peer] = jnp.concatenate(
+        [value[:, start : start + cols] for start in range(0, value.shape[1], cols)], axis=0
+    ).astype(ref.dtype)
+
+
+def write_wire(ref, value):
+    for peer in range(ref.shape[0]):
+        write_wire_piece(ref, peer, value[peer * SUBLANES : (peer + 1) * SUBLANES])
+
+
+def triangle_start(r, name, state):
+    width = state.shape[0]
+    unit, _ = unit_of(state)
+    normed = (unit * r[name + "gain0"][...]).astype(BF16)
+    mixed = dot(r[name + "mix_t"][...], normed)
+    mask = read_rows(r["mask"])
+    for out, base in ((r[name + "a"], 0), (r[name + "b"], 2 * width)):
+        for peer in range(out.shape[0]):
+            start = base + peer * SUBLANES
+            gate = mixed[start : start + SUBLANES]
+            value = mixed[start + width : start + width + SUBLANES]
+            write_wire_piece(out, peer, mask * sigmoid(gate) * value)
+
+
+def triangle_finish(r, name, state):
+    unit, _ = unit_of(state)
+    normed = (unit * r[name + "gain0"][...]).astype(BF16)
+    gate = sigmoid(dot(r[name + "gate_t"][...], normed))
+    tri_unit, tri_scale = unit_of(read_wire(r[name + "tri"]))
+    shaped = (tri_unit * r[name + "gain1"][...]).astype(BF16)
+    branch = dot(r[name + "out_t"][...], shaped)
+    return (state + gate * branch, (gate, tri_unit, tri_scale, shaped, branch))
+
+
+def triangle_back_start(r, name, grad, kept):
+    gate, tri_unit, tri_scale, shaped, branch = kept
+    grad_branch = (grad * gate).astype(BF16)
+    write_rows(r[name + "dgate"], grad * branch * gate * (1.0 - gate))
+    r[name + "d_out"][...] += dot_pairs(shaped, grad_branch)
+    grad_shaped = dot(r[name + "out"][...], grad_branch)
+    r[name + "d_gain1"][...] += fold(grad_shaped * tri_unit)
+    write_wire(r[name + "dtri"], unit_back(grad_shaped, tri_unit, tri_scale, r[name + "gain1"][...]))
+
+
+def triangle_back_finish(r, name, grad, state):
+    width = state.shape[0]
+    unit, scale = unit_of(state)
+    gain = r[name + "gain0"][...]
+    normed = (unit * gain).astype(BF16)
+    mixed = dot(r[name + "mix_t"][...], normed)
+    mask = read_rows(r["mask"])
+    parts = []
+    for source, base in ((r[name + "da"], 0), (r[name + "db"], 2 * width)):
+        back = read_wire(source) * mask
+        gate = sigmoid(mixed[base : base + width])
+        back_gate = back * gate
+        parts.append((back_gate * mixed[base + width : base + 2 * width] * (1.0 - gate)).astype(BF16))
+        parts.append(back_gate.astype(BF16))
+    parts.append(read_rows(r[name + "dgate_in"]))
+    grad_mixed = jnp.concatenate(parts, axis=0)
+    r[name + "d_in"][...] += dot_pairs(normed, grad_mixed)
+    grad_normed = dot(r[name + "in"][...], grad_mixed)
+    r[name + "d_gain0"][...] += fold(grad_normed * unit)
+    return grad + unit_back(grad_normed, unit, scale, gain)
+
+
+def transition(r, name, state):
+    unit, scale = unit_of(state)
+    lifted = (unit * r[name + "gain"][...]).astype(BF16)
+    inner = dot(r[name + "up_t"][...], lifted)
+    half = inner.shape[0] // 2
+    gate = inner[:half]
+    slope = sigmoid(gate)
+    product = (gate * slope * inner[half:]).astype(BF16)
+    return (unit, scale, lifted, inner, slope, product)
+
+
+def transition_finish(r, name, state, kept):
+    return state + dot(r[name + "down_t"][...], kept[5])
+
+
+def transition_back(r, name, grad, kept):
+    unit, scale, lifted, inner, slope, product = kept
+    half = inner.shape[0] // 2
+    gate, up = inner[:half], inner[half:]
+    grad_low = grad.astype(BF16)
+    r[name + "d_down"][...] += dot_pairs(product, grad_low)
+    grad_product = dot(r[name + "down"][...], grad_low)
+    scaled = grad_product * slope
+    grad_inner = jnp.concatenate(
+        [
+            (scaled * up * (1.0 + gate * (1.0 - slope))).astype(BF16),
+            (scaled * gate).astype(BF16),
+        ],
+        axis=0,
+    )
+    r[name + "d_up"][...] += dot_pairs(lifted, grad_inner)
+    grad_lifted = dot(r[name + "up"][...], grad_inner)
+    r[name + "d_gain"][...] += fold(grad_lifted * unit)
+    return grad + unit_back(grad_lifted, unit, scale, r[name + "gain"][...])
+
+
+def head_back(r, state):
+    unit, scale = unit_of(state)
+    gain = r["head_gain"][...]
+    shown = (unit * gain).astype(BF16)
+    logits = dot(r["logits_t"][...], shown)
+    largest = jnp.max(logits, axis=0, keepdims=True)
+    raised = jnp.exp(logits - largest)
+    total = jnp.sum(raised, axis=0, keepdims=True)
+    log_total = largest + jnp.log(total)
+    target = read_rows(r["target"])
+    weight = read_rows(r["weight"])
+    hot = lax.broadcasted_iota(jnp.int32, logits.shape, 0) == target
+    picked = jnp.sum(jnp.where(hot, logits, 0.0), axis=0, keepdims=True)
+    r["loss"][...] += fold(weight * (log_total - picked))
+    share = raised * (1.0 / total)
+    grad_scores = (weight * (share - jnp.where(hot, 1.0, 0.0))).astype(BF16)
+    r["d_logits"][...] += dot_pairs(shown, grad_scores)
+    grad_shown = dot(r["logits"][...], grad_scores)
+    r["d_head_gain"][...] += fold(grad_shown * unit)
+    return unit_back(grad_shown, unit, scale, gain)
+
+
+def bins_hot(r):
+    bins = read_rows(r["bins"])
+    shape = (r["table_rows"], bins.shape[1])
+    return jnp.where(lax.broadcasted_iota(jnp.int32, shape, 0) == bins, 1.0, 0.0).astype(BF16)
+
+
+def block_spec(shape, kind):
+    if kind == "rows":
+        return pl.BlockSpec((ROW_BLOCK,) + shape[1:], lambda step: (step,) + (0,) * (len(shape) - 1))
+    if kind == "wire":
+        return pl.BlockSpec((shape[0], SUBLANES * ROW_BLOCK, shape[2]), lambda step: (0, step, 0))
+    return pl.BlockSpec(shape, lambda step: (0,) * len(shape))
+
+
+def run_stage(body, name, rows, inputs, outputs, extra=None):
+    in_names, out_names = list(inputs), list(outputs)
+
+    def kernel(*refs):
+        named = dict(zip(in_names + out_names, refs))
+        named.update(extra or {})
+
+        @pl.when(pl.program_id(0) == 0)
+        def _():
+            for out in out_names:
+                if outputs[out][2] == "sum":
+                    named[out][...] = jnp.zeros(outputs[out][0], outputs[out][1])
+
+        body(named)
+
+    results = pl.pallas_call(
+        kernel,
+        grid=(rows // ROW_BLOCK,),
+        in_specs=[block_spec(inputs[key][0].shape, inputs[key][1]) for key in in_names],
+        out_specs=[block_spec(outputs[key][0], outputs[key][2]) for key in out_names],
+        out_shape=[jax.ShapeDtypeStruct(outputs[key][0], outputs[key][1]) for key in out_names],
+        compiler_params=pltpu.CompilerParams(
+            dimension_semantics=("arbitrary",), vmem_limit_bytes=VMEM_BYTES
+        ),
+        name=name,
+    )(*[inputs[key][0] for key in in_names])
+    return dict(zip(out_names, results))
+
+
+def flip(value, step, count):
+    result, bit = 0, 1
+    while bit < count:
+        result = result + lax.rem(lax.div(value, bit) + (step // bit) % 2, 2) * bit
+        bit *= 2
+    return result
+
+
+class Exchange:
+    def __init__(self, count, half):
+        row, head = lax.axis_index("row"), lax.axis_index("head")
+        place = lax.rem(row, half)
+        self.count = count
+        self.base = row - place
+        self.me = place * 2 + head
+
+    def peer(self, step):
+        return flip(self.me, step, self.count)
+
+    def device(self, peer):
+        return (self.base + lax.div(peer, 2), lax.rem(peer, 2))
+
+    def greet(self):
+        barrier = pltpu.get_barrier_semaphore()
+        for step in range(1, self.count):
+            pl.semaphore_signal(
+                barrier, inc=1, device_id=self.device(self.peer(step)), device_id_type=MESH
+            )
+        pl.semaphore_wait(barrier, self.count - 1)
+
+    def send(self, moves):
+        copies = []
+        for step in range(1, self.count):
+            peer = self.peer(step)
+            for source, target, send_sems, recv_sems in moves:
+                copy = pltpu.make_async_remote_copy(
+                    src_ref=source.at[peer],
+                    dst_ref=target.at[self.me],
+                    send_sem=send_sems.at[step],
+                    recv_sem=recv_sems.at[step],
+                    device_id=self.device(peer),
+                    device_id_type=MESH,
+                )
+                copy.start()
+                copies.append(copy)
+        for source, target, send_sems, _ in moves:
+            copy = pltpu.make_async_copy(source.at[self.me], target.at[self.me], send_sems.at[0])
+            copy.start()
+            copies.append(copy)
+        return copies
+
+
+def wait_all(copies):
+    for copy in copies:
+        copy.wait()
+
+
+def widen(wide, low):
+    peers, rows, cols = low.shape
+
+    def step(peer, carry):
+        value = low[peer].astype(F32)
+        start = pl.multiple_of(peer * rows, SUBLANES)
+        for lane in range(cols // LANES):
+            wide[lane, pl.ds(start, rows), :] = value[:, lane * LANES : (lane + 1) * LANES]
+        return carry
+
+    lax.fori_loop(0, peers, step, 0)
+
+
+def narrow(low, wide):
+    peers, rows, cols = low.shape
+
+    def step(peer, carry):
+        start = pl.multiple_of(peer * rows, SUBLANES)
+        low[peer] = jnp.concatenate(
+            [wide[lane, pl.ds(start, rows), :] for lane in range(cols // LANES)], axis=1
+        ).astype(low.dtype)
+        return carry
+
+    lax.fori_loop(0, peers, step, 0)
+
+
+def take_channel(wide, channel):
+    lanes, rows, _ = wide.shape
+    count = rows // SUBLANES
+    return jnp.concatenate(
+        [wide[lane, pl.ds(channel, count, stride=SUBLANES), :] for lane in range(lanes)], axis=1
+    )
+
+
+def put_channel(wide, channel, value):
+    lanes, rows, _ = wide.shape
+    count = rows // SUBLANES
+    for lane in range(lanes):
+        wide[lane, pl.ds(channel, count, stride=SUBLANES), :] = value[
+            :, lane * LANES : (lane + 1) * LANES
+        ]
+
+
+def product_of(left, right, left_axis, right_axis):
+    return lax.dot_general(
+        left, right, (((left_axis,), (right_axis,)), ((), ())), preferred_element_type=F32
+    )
+
+
+def forward_exchange(half, incoming, a, b):
+    peers, rows, cols = a.shape
+    tokens = peers * rows // SUBLANES
+
+    def kernel(a_ref, b_ref, a_out, b_out, tri_out, a_got, b_got, wide_a, wide_b, low, *sems):
+        ring = Exchange(peers, half)
+        ring.greet()
+        copies = ring.send(
+            [(a_ref, a_got, sems[0], sems[1]), (b_ref, b_got, sems[2], sems[3])]
+        )
+        wait_all(copies)
+        widen(wide_a, a_got)
+        widen(wide_b, b_got)
+
+        def step(channel, carry):
+            left = take_channel(wide_a, channel).astype(BF16)
+            right = take_channel(wide_b, channel).astype(BF16)
+            a_out[channel] = left
+            b_out[channel] = right
+            axis = 0 if incoming else 1
+            put_channel(wide_a, channel, product_of(left, right, axis, axis))
+            return carry
+
+        lax.fori_loop(0, SUBLANES, step, 0)
+        narrow(low, wide_a)
+        wait_all(ring.send([(low, tri_out, sems[4], sems[5])]))
+
+    wire = jax.ShapeDtypeStruct(a.shape, BF16)
+    block = jax.ShapeDtypeStruct((SUBLANES, tokens, cols), BF16)
+    wide = pltpu.VMEM((cols // LANES, peers * rows, LANES), F32)
+    anywhere = pl.BlockSpec(memory_space=pl.ANY)
+    inside = pl.BlockSpec(memory_space=pltpu.VMEM)
+    return pl.pallas_call(
+        kernel,
+        in_specs=[anywhere, anywhere],
+        out_specs=[inside, inside, anywhere],
+        out_shape=[block, block, wire],
+        scratch_shapes=[pltpu.VMEM(a.shape, BF16)] * 2
+        + [wide] * 2
+        + [pltpu.VMEM(a.shape, BF16)]
+        + [pltpu.SemaphoreType.DMA((peers,))] * 6,
+        compiler_params=pltpu.CompilerParams(
+            collective_id=1 if incoming else 0, has_side_effects=True, vmem_limit_bytes=VMEM_BYTES
+        ),
+        name="incoming_forward" if incoming else "outgoing_forward",
+    )(a, b)
+
+
+def backward_exchange(half, incoming, dtri, a, b):
+    peers, rows, cols = dtri.shape
+
+    def kernel(dtri_ref, a_ref, b_ref, da_out, db_out, got, wide_a, wide_b, low_a, low_b, *sems):
+        ring = Exchange(peers, half)
+        ring.greet()
+        wait_all(ring.send([(dtri_ref, got, sems[0], sems[1])]))
+        widen(wide_a, got)
+
+        def step(channel, carry):
+            grad = take_channel(wide_a, channel).astype(BF16)
+            left, right = a_ref[channel], b_ref[channel]
+            if incoming:
+                grad_left = product_of(right, grad, 1, 1)
+                grad_right = product_of(left, grad, 1, 0)
+            else:
+                grad_left = product_of(grad, right, 1, 0)
+                grad_right = product_of(grad, left, 0, 0)
+            put_channel(wide_a, channel, grad_left)
+            put_channel(wide_b, channel, grad_right)
+            return carry
+
+        lax.fori_loop(0, SUBLANES, step, 0)
+        narrow(low_a, wide_a)
+        narrow(low_b, wide_b)
+        wait_all(
+            ring.send([(low_a, da_out, sems[2], sems[3]), (low_b, db_out, sems[4], sems[5])])
+        )
+
+    wire = jax.ShapeDtypeStruct(dtri.shape, BF16)
+    wide = pltpu.VMEM((cols // LANES, peers * rows, LANES), F32)
+    anywhere = pl.BlockSpec(memory_space=pl.ANY)
+    inside = pl.BlockSpec(memory_space=pltpu.VMEM)
+    return pl.pallas_call(
+        kernel,
+        in_specs=[anywhere, inside, inside],
+        out_specs=[anywhere, anywhere],
+        out_shape=[wire, wire],
+        scratch_shapes=[pltpu.VMEM(dtri.shape, BF16)]
+        + [wide] * 2
+        + [pltpu.VMEM(dtri.shape, BF16)] * 2
+        + [pltpu.SemaphoreType.DMA((peers,))] * 6,
+        compiler_params=pltpu.CompilerParams(
+            collective_id=3 if incoming else 2, has_side_effects=True, vmem_limit_bytes=VMEM_BYTES
+        ),
+        name="incoming_backward" if incoming else "outgoing_backward",
+    )(dtri, a, b)
+
+
+def by_crop(value, rows_axis, head_axis):
+    count, heads = rows_axis, head_axis
+    half = count // 2
+    same, other = [], []
+    for row in range(count):
+        for head in range(heads):
+            source = row * heads + head
+            for crop, pairs in ((head, same), (1 - head, other)):
+                pairs.append((source, (crop * half + row // 2) * heads + row % 2))
+    head = lax.axis_index("head")
+    crop = lax.axis_index("row") // half
+    mine = lax.dynamic_index_in_dim(value, head, 0, keepdims=False)
+    rest = lax.dynamic_index_in_dim(value, 1 - head, 0, keepdims=False)
+    mine = lax.ppermute(mine, ("row", "head"), same)
+    rest = lax.ppermute(rest, ("row", "head"), other)
+    low = jnp.where(crop == 0, mine, rest)
+    high = jnp.where(crop == 0, rest, mine)
+    return jnp.concatenate([low, high], axis=-1)
+
+
+def gradients_by_crop(
+    row_count,
+    head_count,
+    single,
+    residue_index,
+    chain_index,
+    token_mask,
+    pair_valid,
+    target_bins,
+    relative_table,
+    single_weight,
+    triangle_input,
+    triangle_output,
+    expand_weight,
+    reduce_weight,
+    distogram_weight,
+    norm_gains,
+):
+    crops, tokens = token_mask.shape
+    width = relative_table.shape[1]
+    layers = triangle_input.shape[0]
+    half = row_count // crops
+    peers = half * head_count
+    rows = tokens // peers
+    row_index = lax.axis_index("row")
+    crop = row_index // half
+    start = ((row_index % half) * head_count + lax.axis_index("head")) * rows
+
+    placed = by_crop(jnp.stack([pair_valid, target_bins], axis=1), row_count, head_count)
+    valid, target = placed[0], placed[1]
+
+    def of_crop(array):
+        return lax.dynamic_index_in_dim(array, crop, 0, keepdims=False)
+
+    def of_rows(array):
+        return lax.dynamic_slice_in_dim(array, start, rows, 0)
+
+    residues, chains = of_crop(residue_index), of_crop(chain_index)
+    reach = (relative_table.shape[0] - 2) // 2
+    bins = jnp.where(
+        of_rows(chains)[:, None] == chains[None, :],
+        jnp.clip(of_rows(residues)[:, None] - residues[None, :], -reach, reach) + reach,
+        2 * reach + 1,
+    )
+    present = of_crop(token_mask).astype(F32)
+    pair_mask = of_rows(present)[:, None] * present[None, :]
+    loss_weight = pair_mask * valid.astype(F32)
+    table_rows = -(-relative_table.shape[0] // 16) * 16
+    table_t = jnp.pad(relative_table, ((0, table_rows - relative_table.shape[0]), (0, 0))).T
+    tokens_single = of_crop(single)
+    proj = project(tokens_single, single_weight.astype(BF16))
+    proj_rows = of_rows(proj[:, :width])[:, :, None]
+    proj_cols = proj[:, width:].T
+    bins, pair_mask = bins[:, None, :], pair_mask[:, None, :]
+
+    low_input = triangle_input.astype(BF16)
+    low_output = triangle_output.astype(BF16)
+    low_expand = expand_weight.astype(BF16)
+    low_reduce = reduce_weight.astype(BF16)
+    low_logits = distogram_weight.astype(BF16)
+
+    def gain(index):
+        return (norm_gains[index][:, None], "whole")
+
+    def triangle_weights(layer, kind, names):
+        weight_in, weight_out = low_input[layer, kind], low_output[layer, kind]
+        found = {
+            "gain0": gain(5 * layer + 2 * kind),
+            "gain1": gain(5 * layer + 2 * kind + 1),
+            "mix_t": (weight_in[:, : 4 * width].T, "whole"),
+            "gate_t": (weight_in[:, 4 * width :].T, "whole"),
+            "in": (weight_in, "whole"),
+            "out": (weight_out, "whole"),
+            "out_t": (weight_out.T, "whole"),
+        }
+        return {f"t{layer}{kind}{name}": found[name] for name in names.split()}
+
+    def transition_weights(layer, names):
+        found = {
+            "gain": gain(5 * layer + 4),
+            "up": (low_expand[layer], "whole"),
+            "up_t": (low_expand[layer].T, "whole"),
+            "down": (low_reduce[layer], "whole"),
+            "down_t": (low_reduce[layer].T, "whole"),
+        }
+        return {f"f{layer}{name}": found[name] for name in names.split()}
+
+    state_shape = (rows, width, tokens)
+    wire_shape = (peers, rows * SUBLANES, tokens)
+    hidden = low_expand.shape[2]
+    state_out = (state_shape, F32, "rows")
+    wire_out = (wire_shape, BF16, "wire")
+    gate_out = (state_shape, BF16, "rows")
+    gain_out = ((width, LANES), F32, "sum")
+    mask_in = {"mask": (pair_mask, "rows")}
+
+    def start_outs(name):
+        return {name + "a": wire_out, name + "b": wire_out}
+
+    def back_start_outs(name):
+        return {
+            name + "dgate": gate_out,
+            name + "dtri": wire_out,
+            name + "d_out": ((width, width), F32, "sum"),
+            name + "d_gain1": gain_out,
+        }
+
+    def back_finish_outs(name):
+        return {name + "d_in": ((width, 5 * width), F32, "sum"), name + "d_gain0": gain_out}
+
+    def transition_outs(name):
+        return {
+            name + "d_up": ((width, hidden), F32, "sum"),
+            name + "d_down": ((hidden // 2, width), F32, "sum"),
+            name + "d_gain": gain_out,
+        }
+
+    states, tris, lefts, rights, middles = {}, {}, {}, {}, {}
+    sums = {}
+
+    def body(r):
+        hot = bins_hot(r)
+        state = dot(r["table_t"][...], hot)
+        cols = r["proj_cols"][...]
+        state = state + jnp.concatenate(
+            [cols + r["proj_rows"][row] for row in range(ROW_BLOCK)], axis=1
+        )
+        write_rows(r["state"], state)
+        triangle_start(r, "t00", state)
+
+    got = run_stage(
+        body,
+        "first_state",
+        rows,
+        {
+            "bins": (bins, "rows"),
+            "proj_rows": (proj_rows, "rows"),
+            "proj_cols": (proj_cols, "whole"),
+            "table_t": (table_t.astype(BF16), "whole"),
+            **mask_in,
+            **triangle_weights(0, 0, "gain0 mix_t"),
+        },
+        {"state": state_out, **start_outs("t00")},
+        {"table_rows": table_rows},
+    )
+    states["t00"] = got["state"]
+
+    for layer in range(layers):
+        for kind in range(2):
+            name = f"t{layer}{kind}"
+            lefts[name], rights[name], tris[name] = forward_exchange(
+                half, kind == 1, got[name + "a"], got[name + "b"]
+            )
+            inputs = {
+                "state": (states[name], "rows"),
+                name + "tri": (tris[name], "wire"),
+                **triangle_weights(layer, kind, "gain0 gain1 gate_t out_t"),
+            }
+            if kind == 0:
+                following = f"t{layer}1"
+
+                def body(r, name=name, following=following):
+                    state, _ = triangle_finish(r, name, read_rows(r["state"]))
+                    write_rows(r["next"], state)
+                    triangle_start(r, following, state)
+
+                got = run_stage(
+                    body,
+                    "between_updates",
+                    rows,
+                    {**inputs, **mask_in, **triangle_weights(layer, 1, "gain0 mix_t")},
+                    {"next": state_out, **start_outs(following)},
+                )
+                states[following] = got["next"]
+            elif layer + 1 < layers:
+                following = f"t{layer + 1}0"
+                lift = f"f{layer}"
+
+                def body(r, name=name, following=following, lift=lift):
+                    state, _ = triangle_finish(r, name, read_rows(r["state"]))
+                    write_rows(r["middle"], state)
+                    state = transition_finish(r, lift, state, transition(r, lift, state))
+                    write_rows(r["next"], state)
+                    triangle_start(r, following, state)
+
+                got = run_stage(
+                    body,
+                    "layer_end",
+                    rows,
+                    {
+                        **inputs,
+                        **mask_in,
+                        **transition_weights(layer, "gain up_t down_t"),
+                        **triangle_weights(layer + 1, 0, "gain0 mix_t"),
+                    },
+                    {"middle": state_out, "next": state_out, **start_outs(following)},
+                )
+                middles[layer] = got["middle"]
+                states[following] = got["next"]
+
+    lift = f"f{layers - 1}"
+
+    def body(r, name=name):
+        state, kept = triangle_finish(r, name, read_rows(r["state"]))
+        lifted = transition(r, lift, state)
+        grad = head_back(r, transition_finish(r, lift, state, lifted))
+        grad = transition_back(r, lift, grad, lifted)
+        write_rows(r["grad"], grad)
+        triangle_back_start(r, name, grad, kept)
+
+    got = run_stage(
+        body,
+        "loss",
+        rows,
+        {
+            **inputs,
+            **triangle_weights(layers - 1, 1, "out"),
+            **transition_weights(layers - 1, "gain up_t down_t up down"),
+            "head_gain": gain(5 * layers),
+            "logits": (low_logits, "whole"),
+            "logits_t": (low_logits.T, "whole"),
+            "target": (target[:, None, :], "rows"),
+            "weight": (loss_weight[:, None, :], "rows"),
+        },
+        {
+            "grad": state_out,
+            "loss": ((1, LANES), F32, "sum"),
+            "d_logits": (distogram_weight.shape, F32, "sum"),
+            "d_head_gain": gain_out,
+            **transition_outs(lift),
+            **back_start_outs(name),
+        },
+    )
+    sums.update(got)
+
+    for layer in reversed(range(layers)):
+        for kind in (1, 0):
+            name = f"t{layer}{kind}"
+            grad_left, grad_right = backward_exchange(
+                half, kind == 1, got[name + "dtri"], lefts[name], rights[name]
+            )
+            inputs = {
+                "grad_in": (got["grad"], "rows"),
+                "state": (states[name], "rows"),
+                name + "da": (grad_left, "wire"),
+                name + "db": (grad_right, "wire"),
+                name + "dgate_in": (got[name + "dgate"], "rows"),
+                **mask_in,
+                **triangle_weights(layer, kind, "gain0 mix_t in"),
+            }
+            if kind == 1:
+                before = f"t{layer}0"
+
+                def body(r, name=name, before=before):
+                    grad = triangle_back_finish(
+                        r, name, read_rows(r["grad_in"]), read_rows(r["state"])
+                    )
+                    write_rows(r["grad"], grad)
+                    _, kept = triangle_finish(r, before, read_rows(r["before"]))
+                    triangle_back_start(r, before, grad, kept)
+
+                got = run_stage(
+                    body,
+                    "between_updates_back",
+                    rows,
+                    {
+                        **inputs,
+                        "before": (states[before], "rows"),
+                        before + "tri": (tris[before], "wire"),
+                        **triangle_weights(layer, 0, "gain0 gain1 gate_t out out_t"),
+                    },
+                    {"grad": state_out, **back_finish_outs(name), **back_start_outs(before)},
+                )
+            elif layer > 0:
+                before = f"t{layer - 1}1"
+                lift = f"f{layer - 1}"
+
+                def body(r, name=name, before=before, lift=lift):
+                    grad = triangle_back_finish(
+                        r, name, read_rows(r["grad_in"]), read_rows(r["state"])
+                    )
+                    grad = transition_back(r, lift, grad, transition(r, lift, read_rows(r["middle"])))
+                    write_rows(r["grad"], grad)
+                    _, kept = triangle_finish(r, before, read_rows(r["before"]))
+                    triangle_back_start(r, before, grad, kept)
+
+                got = run_stage(
+                    body,
+                    "layer_end_back",
+                    rows,
+                    {
+                        **inputs,
+                        "middle": (middles[layer - 1], "rows"),
+                        "before": (states[before], "rows"),
+                        before + "tri": (tris[before], "wire"),
+                        **transition_weights(layer - 1, "gain up_t up down"),
+                        **triangle_weights(layer - 1, 1, "gain0 gain1 gate_t out out_t"),
+                    },
+                    {
+                        "grad": state_out,
+                        **back_finish_outs(name),
+                        **transition_outs(lift),
+                        **back_start_outs(before),
+                    },
+                )
+            else:
+
+                def body(r, name=name):
+                    grad = triangle_back_finish(
+                        r, name, read_rows(r["grad_in"]), read_rows(r["state"])
+                    )
+                    hot = bins_hot(r)
+                    high = grad.astype(BF16)
+                    low = (grad - high.astype(F32)).astype(BF16)
+                    r["d_table"][...] += dot_pairs(high, hot) + dot_pairs(low, hot)
+                    cols = r["d_cols"].shape[1]
+                    for row in range(ROW_BLOCK):
+                        part = grad[:, row * cols : (row + 1) * cols]
+                        r["d_rows"][row] = fold(part)
+                        r["d_cols"][...] += part
+
+                got = run_stage(
+                    body,
+                    "first_state_back",
+                    rows,
+                    {**inputs, "bins": (bins, "rows")},
+                    {
+                        **back_finish_outs(name),
+                        "d_table": ((width, table_rows), F32, "sum"),
+                        "d_rows": ((rows, width, LANES), F32, "rows"),
+                        "d_cols": ((width, tokens), F32, "sum"),
+                    },
+                    {"table_rows": table_rows},
+                )
+            sums.update(got)
+
+    wide_single = tokens_single.astype(F32)
+    row_part = jnp.einsum(
+        "is,ic->sc",
+        of_rows(wide_single),
+        jnp.sum(sums["d_rows"], axis=2),
+        precision=lax.Precision.HIGHEST,
+    )
+    col_part = jnp.einsum(
+        "js,cj->sc", wide_single, sums["d_cols"], precision=lax.Precision.HIGHEST
+    )
+    gains = []
+    for layer in range(layers):
+        for part in (f"t{layer}0d_gain0", f"t{layer}0d_gain1", f"t{layer}1d_gain0", f"t{layer}1d_gain1", f"f{layer}d_gain"):
+            gains.append(jnp.sum(sums[part], axis=1))
+    gains.append(jnp.sum(sums["d_head_gain"], axis=1))
+
+    def stacked(part):
+        return jnp.stack(
+            [jnp.stack([sums[f"t{layer}{kind}{part}"] for kind in range(2)]) for layer in range(layers)]
+        )
+
+    return (
+        jnp.sum(sums["loss"]),
+        jnp.sum(loss_weight),
+        sums["d_table"][:, : relative_table.shape[0]].T,
+        jnp.concatenate([row_part, col_part], axis=1),
+        stacked("d_in"),
+        stacked("d_out"),
+        jnp.stack([sums[f"f{layer}d_up"] for layer in range(layers)]),
+        jnp.stack([sums[f"f{layer}d_down"] for layer in range(layers)]),
+        sums["d_logits"],
+        jnp.stack(gains),
+    )
+
+
 def per_device(
+    row_count,
+    head_count,
     single,
     residue_index,
     chain_index,
@@ -280,127 +1246,38 @@
     first_gains,
     second_gains,
 ):
-    crops, rows, cols = pair_valid.shape
+    crops, tokens = token_mask.shape
     width = relative_table.shape[1]
-    layers = triangle_input.shape[0]
-    row_start = lax.axis_index("row") * rows
-    col_start = lax.axis_index("head") * cols
-
-    def take(array, start, count):
-        return lax.dynamic_slice_in_dim(array, start, count, 1)
-
-    offset = (
-        take(residue_index, row_start, rows)[:, :, None]
-        - take(residue_index, col_start, cols)[:, None, :]
-    )
-    same = (
-        take(chain_index, row_start, rows)[:, :, None]
-        == take(chain_index, col_start, cols)[:, None, :]
-    )
-    reach = (relative_table.shape[0] - 2) // 2
-    bins = jnp.where(same, jnp.clip(offset, -reach, reach) + reach, 2 * reach + 1)
-    relative_hot = (
-        bins[..., None] == jnp.arange(relative_table.shape[0])[None, None, None, :]
-    ).astype(jnp.float32)
-    token_rows = take(token_mask, row_start, rows).astype(jnp.float32)
-    token_cols = take(token_mask, col_start, cols).astype(jnp.float32)
-    pair_mask = token_rows[:, :, None] * token_cols[:, None, :]
-    loss_weight = pair_mask * pair_valid.astype(jnp.float32)
-    low_input = triangle_input.astype(jnp.bfloat16)
-    low_output = triangle_output.astype(jnp.bfloat16)
-    low_expand = expand_weight.astype(jnp.bfloat16)
-    low_reduce = reduce_weight.astype(jnp.bfloat16)
-    low_logits = distogram_weight.astype(jnp.bfloat16)
-    proj = project(single, single_weight.astype(jnp.bfloat16))
-    state = project(relative_hot.astype(jnp.bfloat16), relative_table.astype(jnp.bfloat16))
-    state = (
-        state
-        + take(proj, row_start, rows)[:, :, None, :width]
-        + take(proj, col_start, cols)[:, None, :, width:]
-    )
-    inputs = []
-    for layer in range(layers):
-        inputs.append(state)
-        state, unused = block_forward(
-            state,
-            low_input[layer],
-            low_output[layer],
-            low_expand[layer],
-            low_reduce[layer],
-            norm_gains[5 * layer : 5 * layer + 5],
-            pair_mask,
-        )
-    head_unit, head_scale = normalize(state)
-    shown = (head_unit * norm_gains[5 * layers]).astype(jnp.bfloat16)
-    logits = project(shown, low_logits)
-    largest = jnp.max(logits, axis=-1, keepdims=True)
-    log_total = largest + jnp.log(jnp.sum(jnp.exp(logits - largest), axis=-1, keepdims=True))
-    target_hot = (
-        target_bins[..., None] == jnp.arange(logits.shape[-1])[None, None, None, :]
-    ).astype(jnp.float32)
-    picked = jnp.sum(logits * target_hot, axis=-1)
-    loss_local = jnp.sum(loss_weight * (log_total[..., 0] - picked))
-    grad_scores = (loss_weight[..., None] * (jnp.exp(logits - log_total) - target_hot)).astype(
-        jnp.bfloat16
-    )
-    grad_logits = weight_grad(shown, grad_scores)
-    grad_shown = project_back(grad_scores, low_logits)
-    grad_state, gain_last = norm_back(grad_shown, head_unit, head_scale, norm_gains[5 * layers])
-    collected = []
-    for layer in reversed(range(layers)):
-        grad_state, layer_grads = block_backward(
-            grad_state,
-            inputs[layer],
-            low_input[layer],
-            low_output[layer],
-            low_expand[layer],
-            low_reduce[layer],
-            norm_gains[5 * layer : 5 * layer + 5],
-            pair_mask,
-        )
-        collected.insert(0, layer_grads)
-    grad_input = jnp.stack([entry[0] for entry in collected])
-    grad_output = jnp.stack([entry[1] for entry in collected])
-    grad_expand = jnp.stack([entry[2] for entry in collected])
-    grad_reduce = jnp.stack([entry[3] for entry in collected])
-    grad_gains = jnp.concatenate(
-        [jnp.concatenate([entry[4] for entry in collected], axis=0), gain_last[None]], axis=0
-    )
-    grad_table = jnp.einsum(
-        "bijr,bijc->rc", relative_hot, grad_state, precision=lax.Precision.HIGHEST
-    )
-    single_wide = single.astype(jnp.float32)
-    row_part = jnp.einsum(
-        "bis,bic->sc",
-        take(single_wide, row_start, rows),
-        jnp.sum(grad_state, axis=2),
-        precision=lax.Precision.HIGHEST,
-    )
-    col_part = jnp.einsum(
-        "bjs,bjc->sc",
-        take(single_wide, col_start, cols),
-        jnp.sum(grad_state, axis=1),
-        precision=lax.Precision.HIGHEST,
-    )
-    grad_single = jnp.concatenate([row_part, col_part], axis=1)
-    local_count = jnp.sum(loss_weight)
-    valid_count = lax.psum(local_count, ("row", "head"))
-    summed = lax.psum(
-        (
-            grad_table / valid_count,
-            grad_single / valid_count,
-            grad_input / valid_count,
-            grad_output / valid_count,
-            grad_expand / valid_count,
-            grad_reduce / valid_count,
-            grad_logits / valid_count,
-            grad_gains / valid_count,
-            loss_local,
-        ),
-        ("row", "head"),
-    )
-    grads = list(summed[:8])
-    loss_sum = summed[8]
+    peers = row_count * head_count // crops
+    given = (
+        single,
+        residue_index,
+        chain_index,
+        token_mask,
+        pair_valid,
+        target_bins,
+        relative_table,
+        single_weight,
+        triangle_input,
+        triangle_output,
+        expand_weight,
+        reduce_weight,
+        distogram_weight,
+        norm_gains,
+    )
+    if (
+        crops == 2
+        and head_count == 2
+        and width == SUBLANES * peers
+        and tokens % (peers * ROW_BLOCK) == 0
+        and tokens % LANES == 0
+    ):
+        local = gradients_by_crop(row_count, head_count, *given)
+    else:
+        local = gradients_by_block(*given)
+    summed = lax.psum(local, ("row", "head"))
+    loss_sum, valid_count = summed[0], summed[1]
+    grads = [grad / valid_count for grad in summed[2:]]
     squares = jnp.zeros((), jnp.float32)
     for g in grads:
         squares = squares + jnp.sum(g * g)
@@ -508,7 +1385,7 @@
         P(),
     )
     return jax.shard_map(
-        per_device,
+        functools.partial(per_device, mesh.shape["row"], mesh.shape["head"]),
         mesh=mesh,
         in_specs=placed,
         out_specs=(

time: 4850 us -> 1320 us (0.27)
  waiting for transfers between devices: 1610 us -> 81 us
  Pallas kernels: 0 us -> 1050 us
  blocking collectives: 1080 us -> 43 us
  local copies, waits for them, and re-layouts: 1050 us -> 49.4 us
  matrix products: 623 us -> 1.87 us
  other arithmetic: 378 us -> 53.9 us
  starting transfers between devices: 58.8 us -> 6.43 us
    pallas_call x0 -> x17, Pallas kernels: none -> 1050 us  [the longest x4 420 us: forward_exchange(): pl.pallas_call(kernel, in_specs=[anywhere, anywhere], out_specs=[inside,...]
    all_to_all x18 -> x0, blocking collectives: 995 us -> none  [the longest x2 212 us: triangle_backward(): lax.all_to_all(jnp.swapaxes(grad_left, 1, 2), 'row', split_axis=1, concat...]
    reduce_scatter x4 -> x0, waiting for transfers between devices: 929 us -> none  [triangle_backward(): lax.psum_scatter(jnp.einsum('bijc,bikc->jbkc', tri_cols, left_cols, prefe...]
    convert_element_type x56 -> x2, local copies, waits for them, and re-layouts: 519 us -> 1.35 us  [the longest x1 0.72 us: gradients_by_crop(): low_logits = distogram_weight.astype(BF16)]
    dot_general x41 -> x2, matrix products: 513 us -> 1.62 us  [the longest x1 1.33 us: gradients_by_crop(): jnp.einsum('js,cj->sc', wide_single, sums['d_cols'], precision=lax.Precis...]
    all_gather x4 -> x0, waiting for transfers between devices: 386 us -> none  [triangle_forward(): right_all = lax.all_gather(right_cols, 'row', axis=1, tiled=True)]
    unnamed x510 -> x150, local copies, waits for them, and re-layouts: 273 us -> 17.3 us
    all_to_all x40 -> x0, local copies, waits for them, and re-layouts: 252 us -> none  [the longest x8 55.7 us: triangle_backward(): lax.all_to_all(grad_tri.astype(jnp.bfloat16), 'head', split_axis=3, conca...]
  transfers between devices with their start and end apart: 23 -> 3, of which waited for: 21 -> 1; matrix products, arithmetic and copies ran while one was open for 12% -> 4% of each run, Pallas kernels for 0% -> 0%
where the time goes in v1:
time: 1320 us; the launch traced here: 1310 us
  Pallas kernels  1050 us (80%)
  waiting for transfers between devices  81 us (6%)
  other arithmetic  53.9 us (4%)
  local copies, waits for them, and re-layouts  49.4 us (4%)
  blocking collectives  43 us (3%)
  between operations  21.6 us (2%)
    pallas_call x4, Pallas kernels, forward_exchange(): pl.pallas_call(kernel, in_specs=[anywhere, anywhere], out_specs=[inside,...  420 us
    pallas_call x4, Pallas kernels, backward_exchange(): pl.pallas_call(kernel, in_specs=[anywhere, inside, inside], out_specs=[an...  419 us
    pallas_call x9, Pallas kernels, run_stage(): pl.pallas_call(kernel, grid=(rows // ROW_BLOCK,), in_specs=[block_spec(in...  213 us
    psum x1, waiting for transfers between devices, per_device(): summed = lax.psum(local, ('row', 'head'))  81 us
    psum x1, blocking collectives, per_device(): summed = lax.psum(local, ('row', 'head'))  43 us
  transfers between devices with their start and end apart: 3, of which 1 were waited for; matrix products, arithmetic and copies ran while one was open for 4% of the time, Pallas kernels for 0%

profile of v1, /device:TPU:0, one launch (start us, length us, event | category | flops | bytes accessed | tf_op | source)
XLA Modules:
  0.0 1309.8 jit_solution(15646458108635515015)
XLA Ops:
  8.8 2.1 collective-permute-start
  11.5 4.3 collective-permute-start.1
  52.4 12.3 first_state.1
  64.7 105.5 %outgoing_forward.2 = (bf16[8,384,384]{2,1,0:T(8,128)(2,1)}, bf16[8,384,384]{2,1,0:T(8,128)(2,1)}, bf16[16,192,384]{2,1,0:T(8,128)(2,1)}) custom-call(bf16[16,192,384]{2,1,0:T(8,128)(2,1)} %get-tuple-element.101.a_ref, bf16[16,192,384]{2,1,0:T(8,128)(2,1)} %get-tuple-element.102.b_ref), custom_call_target="tpu_custom_call" | custom-call | tf_op jit(solution)/shard_map/outgoing_forward/pallas_call | solution.py:759
  170.2 14.1 %between_updates.2 = (f32[24,128,384]{2,1,0:T(8,128)}, bf16[16,192,384]{2,1,0:T(8,128)(2,1)}, bf16[16,192,384]{2,1,0:T(8,128)(2,1)}) custom-call(f32[24,128,384]{2,1,0:T(8,128)} %get-tuple-element.100.refs_0_.refs_9_.refs_1_, bf16[16,192,384]{2,1,0:T(8,128)(2,1)} %get-tuple-element.103.refs_1_.refs_10_, f32[128,1]{1,0:T(8,128)} %copy.215.refs_5_.refs_2_.refs_11_.refs_6_, ...), custom_call_target="tpu_custom_call" | custom-call | tf_op jit(solution)/shard_map/between_updates/pallas_call | solution.py:607
  184.3 106.6 %incoming_forward.2 = (bf16[8,384,384]{2,1,0:T(8,128)(2,1)}, bf16[8,384,384]{2,1,0:T(8,128)(2,1)}, bf16[16,192,384]{2,1,0:T(8,128)(2,1)}) custom-call(bf16[16,192,384]{2,1,0:T(8,128)(2,1)} %get-tuple-element.105.a_ref, bf16[16,192,384]{2,1,0:T(8,128)(2,1)} %get-tuple-element.106.b_ref), custom_call_target="tpu_custom_call" | custom-call | tf_op jit(solution)/shard_map/incoming_forward/pallas_call | solution.py:759
  290.9 21.9 %layer_end.1 = (f32[24,128,384]{2,1,0:T(8,128)}, f32[24,128,384]{2,1,0:T(8,128)}, bf16[16,192,384]{2,1,0:T(8,128)(2,1)}, bf16[16,192,384]{2,1,0:T(8,128)(2,1)}) custom-call(f32[24,128,384]{2,1,0:T(8,128)} %get-tuple-element.104.refs_0_.refs_10_.refs_1_, bf16[16,192,384]{2,1,0:T(8,128)(2,1)} %get-tuple-element.107.refs_1_.refs_11_, ...), custom_call_target="tpu_custom_call" | custom-call | tf_op jit(solution)/shard_map/layer_end/pallas_call | solution.py:607
  312.9 101.9 %outgoing_forward.3 = (bf16[8,384,384]{2,1,0:T(8,128)(2,1)}, bf16[8,384,384]{2,1,0:T(8,128)(2,1)}, bf16[16,192,384]{2,1,0:T(8,128)(2,1)}) custom-call(bf16[16,192,384]{2,1,0:T(8,128)(2,1)} %get-tuple-element.109.a_ref, bf16[16,192,384]{2,1,0:T(8,128)(2,1)} %get-tuple-element.110.b_ref), custom_call_target="tpu_custom_call" | custom-call | tf_op jit(solution)/shard_map/outgoing_forward/pallas_call | solution.py:759
  414.7 14.2 %between_updates.3 = (f32[24,128,384]{2,1,0:T(8,128)}, bf16[16,192,384]{2,1,0:T(8,128)(2,1)}, bf16[16,192,384]{2,1,0:T(8,128)(2,1)}) custom-call(f32[24,128,384]{2,1,0:T(8,128)} %get-tuple-element.108.refs_0_.refs_9_.refs_1_, bf16[16,192,384]{2,1,0:T(8,128)(2,1)} %get-tuple-element.111.refs_1_.refs_10_, f32[128,1]{1,0:T(8,128)} %copy.229.refs_10_.refs_2_.refs_11_.refs_6_, ...), custom_call_target="tpu_custom_call" | custom-call | tf_op jit(solution)/shard_map/between_updates/pallas_call | solution.py:607
  428.9 106.1 %incoming_forward.3 = (bf16[8,384,384]{2,1,0:T(8,128)(2,1)}, bf16[8,384,384]{2,1,0:T(8,128)(2,1)}, bf16[16,192,384]{2,1,0:T(8,128)(2,1)}) custom-call(bf16[16,192,384]{2,1,0:T(8,128)(2,1)} %get-tuple-element.113.a_ref, bf16[16,192,384]{2,1,0:T(8,128)(2,1)} %get-tuple-element.114.b_ref), custom_call_target="tpu_custom_call" | custom-call | tf_op jit(solution)/shard_map/incoming_forward/pallas_call | solution.py:759
  535.0 47.9 %loss.1 = (f32[24,128,384]{2,1,0:T(8,128)}, f32[1,128]{1,0:T(1,128)}, f32[128,64]{1,0:T(8,128)}, f32[128,128]{1,0:T(8,128)}, f32[128,1024]{1,0:T(8,128)}, /*inde...) custom-call(f32[24,128,384]{2,1,0:T(8,128)} %get-tuple-element.112.r, ...), custom_call_target="tpu_custom_call" | custom-call | tf_op jit(solution)/shard_map/loss/pallas_call | solution.py:607
  582.9 103.5 %incoming_backward.2 = (bf16[16,192,384]{2,1,0:T(8,128)(2,1)}, bf16[16,192,384]{2,1,0:T(8,128)(2,1)}) custom-call(bf16[16,192,384]{2,1,0:T(8,128)(2,1)} %get-tuple-element.118.dtri_ref, bf16[8,384,384]{2,1,0:T(8,128)(2,1)} %get-tuple-element.119.a_ref, bf16[8,384,384]{2,1,0:T(8,128)(2,1)} %get-tuple-element.120.b_ref), custom_call_target="tpu_custom_call" | custom-call | tf_op jit(solution)/shard_map/incoming_backward/pallas_call | solution.py:808
  686.4 21.3 %between_updates_back.2 = (f32[24,128,384]{2,1,0:T(8,128)}, f32[128,640]{1,0:T(8,128)}, f32[128,128]{1,0:T(8,128)}, bf16[24,128,384]{2,1,0:T(8,128)(2,1)}, bf16[...) custom-call(f32[24,128,384]{2,1,0:T(8,128)} %get-tuple-element.117.refs_0_, ...), custom_call_target="tpu_custom_call" | custom-call | tf_op jit(solution)/shard_map/between_updates_back/pallas_call | solution.py:607
  707.7 106.2 %outgoing_backward.2 = (bf16[16,192,384]{2,1,0:T(8,128)(2,1)}, bf16[16,192,384]{2,1,0:T(8,128)(2,1)}) custom-call(bf16[16,192,384]{2,1,0:T(8,128)(2,1)} %get-tuple-element.125.dtri_ref, bf16[8,384,384]{2,1,0:T(8,128)(2,1)} %get-tuple-element.126.a_ref, bf16[8,384,384]{2,1,0:T(8,128)(2,1)} %get-tuple-element.127.b_ref), custom_call_target="tpu_custom_call" | custom-call | tf_op jit(solution)/shard_map/outgoing_backward/pallas_call | solution.py:808
  813.9 41.9 %layer_end_back.1 = (f32[24,128,384]{2,1,0:T(8,128)}, f32[128,640]{1,0:T(8,128)}, f32[128,128]{1,0:T(8,128)}, f32[128,1024]{1,0:T(8,128)}, f32[512,128]{1,0:T(8,...) custom-call(f32[24,128,384]{2,1,0:T(8,128)} %get-tuple-element.124.r, ...), custom_call_target="tpu_custom_call" | custom-call | tf_op jit(solution)/shard_map/layer_end_back/pallas_call | solution.py:607
  855.8 103.3 %incoming_backward.3 = (bf16[16,192,384]{2,1,0:T(8,128)(2,1)}, bf16[16,192,384]{2,1,0:T(8,128)(2,1)}) custom-call(bf16[16,192,384]{2,1,0:T(8,128)(2,1)} %get-tuple-element.133.dtri_ref, bf16[8,384,384]{2,1,0:T(8,128)(2,1)} %get-tuple-element.134.a_ref, bf16[8,384,384]{2,1,0:T(8,128)(2,1)} %get-tuple-element.135.b_ref), custom_call_target="tpu_custom_call" | custom-call | tf_op jit(solution)/shard_map/incoming_backward/pallas_call | solution.py:808
  959.1 21.3 %between_updates_back.3 = (f32[24,128,384]{2,1,0:T(8,128)}, f32[128,640]{1,0:T(8,128)}, f32[128,128]{1,0:T(8,128)}, bf16[24,128,384]{2,1,0:T(8,128)(2,1)}, bf16[...) custom-call(f32[24,128,384]{2,1,0:T(8,128)} %get-tuple-element.132.refs_0_, ...), custom_call_target="tpu_custom_call" | custom-call | tf_op jit(solution)/shard_map/between_updates_back/pallas_call | solution.py:607
  980.4 106.5 %outgoing_backward.3 = (bf16[16,192,384]{2,1,0:T(8,128)(2,1)}, bf16[16,192,384]{2,1,0:T(8,128)(2,1)}) custom-call(bf16[16,192,384]{2,1,0:T(8,128)(2,1)} %get-tuple-element.140.dtri_ref, bf16[8,384,384]{2,1,0:T(8,128)(2,1)} %get-tuple-element.141.a_ref, bf16[8,384,384]{2,1,0:T(8,128)(2,1)} %get-tuple-element.142.b_ref), custom_call_target="tpu_custom_call" | custom-call | tf_op jit(solution)/shard_map/outgoing_backward/pallas_call | solution.py:808
  1086.9 18.2 %first_state_back.1 = (f32[128,640]{1,0:T(8,128)}, f32[128,128]{1,0:T(8,128)}, f32[128,80]{1,0:T(8,128)}, f32[24,128,128]{2,1,0:T(8,128)}, f32[128,384]{1,0:T(8,128)}) custom-call(f32[24,128,384]{2,1,0:T(8,128)} %get-tuple-element.139.refs_0_, f32[24,128,384]{2,1,0:T(8,128)} %get-tuple-element.100.refs_0_.refs_9_.refs_1_, ...), custom_call_target="tpu_custom_call" | custom-call | tf_op jit(solution)/shard_map/first_state_back/pallas_call | solution.py:607
  1106.5 1.9 reduce_sum.201
  1126.5 43.0 %all-reduce.7 = (f32[]{:T(128)}, f32[]{:T(128)}, f32[66,128]{0,1:T(8,128)S(1)}, f32[128,64]{1,0:T(8,128)S(1)}, f32[11,128]{1,0:T(8,128)S(1)}) all-reduce(f32[]{:T(128)} %reduce_sum.198, f32[]{:T(128)} %fusion.18, f32[66,128]{0,1:T(8,128)S(1)} %slice_bitcast_fusion.16, ...), channel_id=1, replica_groups=mesh['row'=16,'head'=2] {'row','head'}, use_global_device_ids=true, to_apply=%region_1.2 | all-reduce | flops 18050 | bytes 144400 | tf_op jit(solution)/shard_map/psum | solution.py:1278
  1173.4 81.0 %all-reduce.6.cloned.1.call-done = (f32[384,256]{0,1:T(8,128)}, f32[2,2,128,640]{3,2,1,0:T(8,128)}, f32[2,2,128,128]{3,2,1,0:T(8,128)}, f32[2,128,1024]{2,1,0:T(8,128)}, f32[2,512,128]{2,1,0:T(8,128)}) async-done(((f32[384,256]{0,1:T(8,128)}, f32[2,2,128,640]{3,2,1,0:T(8,128)}, f32[2,2,128,128]{3,2,1,0:T(8,128)}, f32[2,128,1024]{2,1,0:T(8,128)}, f32[2,512,128]{2,1,0:T(8,128)}), (f32[384,256]{0,1:T(8,128)}, ...) | async-done | bytes 3538960 | tf_op jit(solution)/shard_map/psum | solution.py:1278
  1254.4 2.5 multiply_reduce_fusion.3
  1256.8 2.9 multiply_reduce_fusion
  1259.7 2.3 multiply_reduce_fusion.4
  1275.0 2.1 copy.286
  1277.0 1.9 copy.287
  1278.9 1.9 copy.288
  1280.8 2.2 multiply_subtract_fusion.5
  1287.8 5.4 multiply_subtract_fusion
  1295.0 3.1 multiply_subtract_fusion.1
  1298.2 2.1 multiply_subtract_fusion.2
  (247 shorter events, 76.8 us)
Async XLA Ops:
  7.2 12.8 copy-start
  7.2 1247.1 %all-reduce.6.cloned.1.call-start = ((), (), s32[]{:S(2)}) async-start(), calls=%async_computation | async-start | bytes 7077888 | tf_op jit(solution)/shard_map/psum | solution.py:1278
  8.8 41.3 %collective-permute-start = (s32[2,24,192]{2,0,1:T(2,128)}, s32[2,24,192]{2,0,1:T(2,128)}, u32[]{:S(2)}, u32[]{:S(2)}) collective-permute-start(s32[2,24,192]{2,0,1:T(2,128)} %bitcast.157), channel_id=1, source_target_pairs={{0,0},{1,16},{2,1},{3,17},{4,2},{5,18},{6,3},{7,19},{8,4},{9,20},{... | collective-permute-start | bytes 110600 | tf_op jit(solution)/shard_map/ppermute | solution.py:837
  11.5 38.6 %collective-permute-start.1 = (s32[2,24,192]{2,0,1:T(2,128)}, s32[2,24,192]{2,0,1:T(2,128)}, u32[]{:S(2)}, u32[]{:S(2)}) collective-permute-start(s32[2,24,192]{2,0,1:T(2,128)} %bitcast.156), channel_id=1, source_target_pairs={{0,16},{1,0},{2,17},{3,1},{4,18},{5,2},{6,19},{7,3},{8,20},{9,4},{... | collective-permute-start | bytes 110600 | tf_op jit(solution)/shard_map/ppermute | solution.py:838
  17.9 4.5 copy-start.63
  17.9 4.5 copy-start.56
  17.9 4.6 copy-start.17
  24.4 5.6 copy-start.23
  24.4 7.1 copy-start.41
  24.4 8.5 copy-start.22
  25.2 9.3 copy-start.43
  26.7 24.9 %copy-start.59 = (f32[24]{0:T(128)}, f32[24]{0:T(128)S(1)}, u32[]{:S(2)}) copy-start(f32[24]{0:T(128)S(1)} %fusion.30) | copy-start | bytes 292
  26.7 11.5 copy-start.21
  28.4 11.3 copy-start.42
  1113.9 10.6 copy-start.48
  1113.9 10.7 copy-start.47
  1113.9 10.8 copy-start.46
  1113.9 10.9 copy-start.45
  1114.0 11.0 copy-start.60
  1114.0 12.6 copy-start.44
  1169.5 94.1 %copy-start.37 = (f32[128,64]{1,0:T(8,128)}, f32[128,64]{1,0:T(8,128)S(1)}, u32[]{:S(2)}) copy-start(f32[128,64]{1,0:T(8,128)S(1)} %get-tuple-element.257) | copy-start | bytes 98308
  1254.4 7.7 copy-start.5
  1254.4 9.2 copy-start.9
  1259.7 13.4 %copy-start.11 = (f32[384,256]{0,1:T(8,128)S(1)}, f32[384,256]{0,1:T(8,128)}, u32[]{:S(2)}) copy-start(f32[384,256]{0,1:T(8,128)} %get-tuple-element.259) | copy-start | bytes 1179652
  1274.9 12.7 copy-start.1
  1275.0 12.7 copy-start.2
  1287.7 5.5 copy-start.18
  1287.7 5.5 copy-start.35
  1287.7 5.5 copy-start.36
  1287.7 7.2 copy-start.6
  1287.7 7.2 copy-start.19
  1287.7 7.2 copy-start.20
  (36 other events, 87.1 us)
Sparse Core Ops, SparseCore 0:
  1113.7 140.5 all-reduce.5

commit v2 on v1

--- a/solution.py
+++ b/solution.py
@@ -391,6 +391,7 @@
 SUBLANES = 8
 VMEM_BYTES = 58 * 2**20
 ROW_BLOCK = 2
+CHUNK_STEPS = 3
 MESH = pl.DeviceIdType.MESH
 
 
@@ -584,34 +585,66 @@
 def block_spec(shape, kind):
     if kind == "rows":
         return pl.BlockSpec((ROW_BLOCK,) + shape[1:], lambda step: (step,) + (0,) * (len(shape) - 1))
+    if kind == "anywhere":
+        return pl.BlockSpec(memory_space=pl.ANY)
     if kind == "wire":
         return pl.BlockSpec((shape[0], SUBLANES * ROW_BLOCK, shape[2]), lambda step: (0, step, 0))
     return pl.BlockSpec(shape, lambda step: (0,) * len(shape))
 
 
-def run_stage(body, name, rows, inputs, outputs, extra=None):
+def run_stage(body, name, rows, inputs, outputs, extra=None, exchange=None):
     in_names, out_names = list(inputs), list(outputs)
+    steps = rows // ROW_BLOCK
+    scratch = exchange.scratch() if exchange else []
 
     def kernel(*refs):
+        step = pl.program_id(0)
         named = dict(zip(in_names + out_names, refs))
         named.update(extra or {})
-
-        @pl.when(pl.program_id(0) == 0)
+        held = refs[len(in_names) + len(out_names) :]
+        ring = Exchange(exchange.peers, exchange.half) if exchange else None
+
+        @pl.when(step == 0)
         def _():
+            if exchange:
+                ring.greet()
             for out in out_names:
                 if outputs[out][2] == "sum":
                     named[out][...] = jnp.zeros(outputs[out][0], outputs[out][1])
 
+        if exchange:
+            here = pl.ds(pl.multiple_of(step * SUBLANES * ROW_BLOCK, 16), SUBLANES * ROW_BLOCK)
+            for index, wire in enumerate(exchange.wires):
+                named[wire] = held[index].at[:, here, :]
         body(named)
+        if exchange:
+            moves = exchange.moves(held)
+
+            @pl.when(step % CHUNK_STEPS == CHUNK_STEPS - 1)
+            def _():
+                @pl.when(step == CHUNK_STEPS - 1)
+                def _():
+                    ring.meet()
+
+                ring.start(moves, step // CHUNK_STEPS)
+
+            @pl.when(step == steps - 1)
+            def _():
+                lax.fori_loop(0, steps // CHUNK_STEPS, lambda chunk, _: ring.wait(moves, chunk), None)
+                exchange.finish(ring, named, held)
 
     results = pl.pallas_call(
         kernel,
-        grid=(rows // ROW_BLOCK,),
+        grid=(steps,),
         in_specs=[block_spec(inputs[key][0].shape, inputs[key][1]) for key in in_names],
         out_specs=[block_spec(outputs[key][0], outputs[key][2]) for key in out_names],
         out_shape=[jax.ShapeDtypeStruct(outputs[key][0], outputs[key][1]) for key in out_names],
+        scratch_shapes=scratch,
         compiler_params=pltpu.CompilerParams(
-            dimension_semantics=("arbitrary",), vmem_limit_bytes=VMEM_BYTES
+            dimension_semantics=("arbitrary",),
+            vmem_limit_bytes=VMEM_BYTES,
+            has_side_effects=exchange is not None,
+            collective_id=exchange.collective_id if exchange else None,
         ),
         name=name,
     )(*[inputs[key][0] for key in in_names])
@@ -626,53 +659,81 @@
     return result
 
 
+def position(row, head, half, heads):
+    inner = half // 2 * heads
+    return (row % 2) * inner + (row // 2) * heads + head
+
+
+def place_of(position, half, heads):
+    inner = half // 2 * heads
+    rest = lax.rem(position, inner)
+    return (lax.div(rest, heads) * 2 + lax.div(position, inner), lax.rem(rest, heads))
+
+
 class Exchange:
     def __init__(self, count, half):
         row, head = lax.axis_index("row"), lax.axis_index("head")
         place = lax.rem(row, half)
+        inner = count // 2
         self.count = count
+        self.half = half
         self.base = row - place
-        self.me = place * 2 + head
+        self.me = lax.rem(place, 2) * inner + lax.div(place, 2) * (count // half) + head
+        self.order = []
+        for step in range(1, count):
+            for other in (step, step ^ (inner - 1)):
+                if other and other not in self.order:
+                    self.order.append(other)
 
     def peer(self, step):
         return flip(self.me, step, self.count)
 
     def device(self, peer):
-        return (self.base + lax.div(peer, 2), lax.rem(peer, 2))
+        place, head = place_of(peer, self.half, self.count // self.half)
+        return (self.base + place, head)
 
     def greet(self):
         barrier = pltpu.get_barrier_semaphore()
-        for step in range(1, self.count):
+        for step in self.order:
             pl.semaphore_signal(
                 barrier, inc=1, device_id=self.device(self.peer(step)), device_id_type=MESH
             )
-        pl.semaphore_wait(barrier, self.count - 1)
-
-    def send(self, moves):
-        copies = []
-        for step in range(1, self.count):
+
+    def meet(self):
+        pl.semaphore_wait(pltpu.get_barrier_semaphore(), self.count - 1)
+
+    def copies(self, moves, chunk, steps):
+        found = []
+        for step in steps:
             peer = self.peer(step)
             for source, target, send_sems, recv_sems in moves:
-                copy = pltpu.make_async_remote_copy(
-                    src_ref=source.at[peer],
-                    dst_ref=target.at[self.me],
-                    send_sem=send_sems.at[step],
-                    recv_sem=recv_sems.at[step],
-                    device_id=self.device(peer),
-                    device_id_type=MESH,
-                )
-                copy.start()
-                copies.append(copy)
-        for source, target, send_sems, _ in moves:
-            copy = pltpu.make_async_copy(source.at[self.me], target.at[self.me], send_sems.at[0])
+                size = source.shape[1] // send_sems.shape[0]
+                rows = pl.ds(pl.multiple_of(chunk * size, 16), size)
+                if step == 0:
+                    copy = pltpu.make_async_copy(
+                        source.at[self.me, rows, :],
+                        target.at[self.me, rows, :],
+                        send_sems.at[chunk, 0],
+                    )
+                else:
+                    copy = pltpu.make_async_remote_copy(
+                        src_ref=source.at[peer, rows, :],
+                        dst_ref=target.at[self.me, rows, :],
+                        send_sem=send_sems.at[chunk, step],
+                        recv_sem=recv_sems.at[chunk, step],
+                        device_id=self.device(peer),
+                        device_id_type=MESH,
+                    )
+                found.append(copy)
+        return found
+
+    def start(self, moves, chunk):
+        for copy in self.copies(moves, chunk, self.order + [0]):
             copy.start()
-            copies.append(copy)
-        return copies
-
-
-def wait_all(copies):
-    for copy in copies:
-        copy.wait()
+
+    def wait(self, moves, chunk):
+        for copy in self.copies(moves, chunk, self.order + [0]):
+            copy.wait()
 
 
 def widen(wide, low):
@@ -688,8 +749,8 @@
     lax.fori_loop(0, peers, step, 0)
 
 
-def narrow(low, wide):
-    peers, rows, cols = low.shape
+def narrow(low, wide, first, last):
+    _, rows, cols = low.shape
 
     def step(peer, carry):
         start = pl.multiple_of(peer * rows, SUBLANES)
@@ -698,7 +759,7 @@
         ).astype(low.dtype)
         return carry
 
-    lax.fori_loop(0, peers, step, 0)
+    lax.fori_loop(first, last, step, 0)
 
 
 def take_channel(wide, channel):
@@ -706,14 +767,12 @@
     count = rows // SUBLANES
     return jnp.concatenate(
         [wide[lane, pl.ds(channel, count, stride=SUBLANES), :] for lane in range(lanes)], axis=1
-    )
-
-
-def put_channel(wide, channel, value):
-    lanes, rows, _ = wide.shape
-    count = rows // SUBLANES
-    for lane in range(lanes):
-        wide[lane, pl.ds(channel, count, stride=SUBLANES), :] = value[
+    ).astype(BF16)
+
+
+def put_channel(wide, channel, value, first=0):
+    for lane in range(wide.shape[0]):
+        wide[lane, pl.ds(first * SUBLANES + channel, value.shape[0], stride=SUBLANES), :] = value[
             :, lane * LANES : (lane + 1) * LANES
         ]
 
@@ -724,101 +783,131 @@
     )
 
 
-def forward_exchange(half, incoming, a, b):
-    peers, rows, cols = a.shape
-    tokens = peers * rows // SUBLANES
-
-    def kernel(a_ref, b_ref, a_out, b_out, tri_out, a_got, b_got, wide_a, wide_b, low, *sems):
-        ring = Exchange(peers, half)
-        ring.greet()
-        copies = ring.send(
-            [(a_ref, a_got, sems[0], sems[1]), (b_ref, b_got, sems[2], sems[3])]
-        )
-        wait_all(copies)
+class Forward:
+    def __init__(self, peers, half, rows, tokens, name, incoming, collective_id):
+        self.peers, self.half, self.incoming = peers, half, incoming
+        self.rows, self.tokens, self.name = rows * SUBLANES, tokens, name
+        self.chunks = rows // ROW_BLOCK // CHUNK_STEPS
+        self.wires = [name + "a", name + "b"]
+        self.collective_id = collective_id
+
+    def outs(self):
+        block = ((SUBLANES, self.tokens, self.tokens), BF16, "whole")
+        tri = ((self.peers, self.rows, self.tokens), BF16, "anywhere")
+        return {self.name + "left": block, self.name + "right": block, self.name + "tri": tri}
+
+    def scratch(self):
+        low = pltpu.VMEM((self.peers, self.rows, self.tokens), BF16)
+        wide = pltpu.VMEM((self.tokens // LANES, self.peers * self.rows, LANES), F32)
+        many = pltpu.SemaphoreType.DMA((self.chunks, self.peers))
+        once = pltpu.SemaphoreType.DMA((1, self.peers))
+        return [low] * 5 + [wide] * 3 + [many] * 4 + [once] * 2
+
+    def moves(self, held):
+        return [(held[0], held[2], held[8], held[9]), (held[1], held[3], held[10], held[11])]
+
+    def finish(self, ring, named, held):
+        _, _, a_got, b_got, low, wide_a, wide_b, wide_tri = held[:8]
+        left_out, right_out = named[self.name + "left"], named[self.name + "right"]
         widen(wide_a, a_got)
         widen(wide_b, b_got)
-
-        def step(channel, carry):
-            left = take_channel(wide_a, channel).astype(BF16)
-            right = take_channel(wide_b, channel).astype(BF16)
-            a_out[channel] = left
-            b_out[channel] = right
-            axis = 0 if incoming else 1
-            put_channel(wide_a, channel, product_of(left, right, axis, axis))
+        axis = 0 if self.incoming else 1
+        middle = self.tokens * 2 // 3 // LANES * LANES
+        reach = self.peers // 2
+        tri = [(low, named[self.name + "tri"], held[12], held[13])]
+
+        def first(channel, carry):
+            left, right = take_channel(wide_a, channel), take_channel(wide_b, channel)
+            left_out[channel] = left
+            right_out[channel] = right
+            part = left[:, :middle] if self.incoming else left[:middle]
+            put_channel(wide_tri, channel, product_of(part, right, axis, axis))
             return carry
 
-        lax.fori_loop(0, SUBLANES, step, 0)
-        narrow(low, wide_a)
-        wait_all(ring.send([(low, tri_out, sems[4], sems[5])]))
-
-    wire = jax.ShapeDtypeStruct(a.shape, BF16)
-    block = jax.ShapeDtypeStruct((SUBLANES, tokens, cols), BF16)
-    wide = pltpu.VMEM((cols // LANES, peers * rows, LANES), F32)
-    anywhere = pl.BlockSpec(memory_space=pl.ANY)
-    inside = pl.BlockSpec(memory_space=pltpu.VMEM)
-    return pl.pallas_call(
-        kernel,
-        in_specs=[anywhere, anywhere],
-        out_specs=[inside, inside, anywhere],
-        out_shape=[block, block, wire],
-        scratch_shapes=[pltpu.VMEM(a.shape, BF16)] * 2
-        + [wide] * 2
-        + [pltpu.VMEM(a.shape, BF16)]
-        + [pltpu.SemaphoreType.DMA((peers,))] * 6,
-        compiler_params=pltpu.CompilerParams(
-            collective_id=1 if incoming else 0, has_side_effects=True, vmem_limit_bytes=VMEM_BYTES
-        ),
-        name="incoming_forward" if incoming else "outgoing_forward",
-    )(a, b)
-
-
-def backward_exchange(half, incoming, dtri, a, b):
-    peers, rows, cols = dtri.shape
-
-    def kernel(dtri_ref, a_ref, b_ref, da_out, db_out, got, wide_a, wide_b, low_a, low_b, *sems):
-        ring = Exchange(peers, half)
-        ring.greet()
-        wait_all(ring.send([(dtri_ref, got, sems[0], sems[1])]))
-        widen(wide_a, got)
-
-        def step(channel, carry):
-            grad = take_channel(wide_a, channel).astype(BF16)
-            left, right = a_ref[channel], b_ref[channel]
-            if incoming:
-                grad_left = product_of(right, grad, 1, 1)
-                grad_right = product_of(left, grad, 1, 0)
-            else:
-                grad_left = product_of(grad, right, 1, 0)
-                grad_right = product_of(grad, left, 0, 0)
-            put_channel(wide_a, channel, grad_left)
-            put_channel(wide_b, channel, grad_right)
+        def second(channel, carry):
+            left, right = left_out[channel], right_out[channel]
+            part = left[:, middle:] if self.incoming else left[middle:]
+            put_channel(wide_tri, channel, product_of(part, right, axis, axis), middle)
             return carry
 
-        lax.fori_loop(0, SUBLANES, step, 0)
-        narrow(low_a, wide_a)
-        narrow(low_b, wide_b)
-        wait_all(
-            ring.send([(low_a, da_out, sems[2], sems[3]), (low_b, db_out, sems[4], sems[5])])
-        )
-
-    wire = jax.ShapeDtypeStruct(dtri.shape, BF16)
-    wide = pltpu.VMEM((cols // LANES, peers * rows, LANES), F32)
-    anywhere = pl.BlockSpec(memory_space=pl.ANY)
-    inside = pl.BlockSpec(memory_space=pltpu.VMEM)
-    return pl.pallas_call(
-        kernel,
-        in_specs=[anywhere, inside, inside],
-        out_specs=[anywhere, anywhere],
-        out_shape=[wire, wire],
-        scratch_shapes=[pltpu.VMEM(dtri.shape, BF16)]
-        + [wide] * 2
-        + [pltpu.VMEM(dtri.shape, BF16)] * 2
-        + [pltpu.SemaphoreType.DMA((peers,))] * 6,
-        compiler_params=pltpu.CompilerParams(
-            collective_id=3 if incoming else 2, has_side_effects=True, vmem_limit_bytes=VMEM_BYTES
-        ),
-        name="incoming_backward" if incoming else "outgoing_backward",
-    )(dtri, a, b)
+        lax.fori_loop(0, SUBLANES, first, 0)
+        narrow(low, wide_tri, 0, reach)
+        self.send_to(ring, tri, 0)
+        lax.fori_loop(0, SUBLANES, second, 0)
+        narrow(low, wide_tri, reach, self.peers)
+        self.send_to(ring, tri, 1)
+        ring.wait(tri, 0)
+
+    def send_to(self, ring, tri, part):
+        inner = self.peers // 2
+        mine = lax.div(ring.me, inner)
+
+        @pl.when(mine == part)
+        def _():
+            for copy in ring.copies(tri, 0, [step for step in ring.order if step < inner] + [0]):
+                copy.start()
+
+        @pl.when(mine != part)
+        def _():
+            for copy in ring.copies(tri, 0, [step for step in ring.order if step >= inner]):
+                copy.start()
+
+
+class Backward:
+    def __init__(self, peers, half, rows, tokens, name, incoming, collective_id):
+        self.peers, self.half, self.incoming = peers, half, incoming
+        self.rows, self.tokens, self.name = rows * SUBLANES, tokens, name
+        self.chunks = rows // ROW_BLOCK // CHUNK_STEPS
+        self.wires = [name + "dtri"]
+        self.collective_id = collective_id
+
+    def outs(self):
+        grad = ((self.peers, self.rows, self.tokens), BF16, "anywhere")
+        return {self.name + "da": grad, self.name + "db": grad}
+
+    def scratch(self):
+        low = pltpu.VMEM((self.peers, self.rows, self.tokens), BF16)
+        wide = pltpu.VMEM((self.tokens // LANES, self.peers * self.rows, LANES), F32)
+        many = pltpu.SemaphoreType.DMA((self.chunks, self.peers))
+        once = pltpu.SemaphoreType.DMA((1, self.peers))
+        return [low] * 4 + [wide] * 2 + [many] * 2 + [once] * 4
+
+    def moves(self, held):
+        return [(held[0], held[1], held[6], held[7])]
+
+    def finish(self, ring, named, held):
+        _, got, low_a, low_b, wide, wide_grad = held[:6]
+        left_in, right_in = named[self.name + "left"], named[self.name + "right"]
+        widen(wide, got)
+
+        def left_step(channel, carry):
+            grad, right = take_channel(wide, channel), right_in[channel]
+            put_channel(
+                wide_grad,
+                channel,
+                product_of(right, grad, 1, 1) if self.incoming else product_of(grad, right, 1, 0),
+            )
+            return carry
+
+        def right_step(channel, carry):
+            grad, left = take_channel(wide, channel), left_in[channel]
+            put_channel(
+                wide_grad,
+                channel,
+                product_of(left, grad, 1, 0) if self.incoming else product_of(grad, left, 0, 0),
+            )
+            return carry
+
+        lax.fori_loop(0, SUBLANES, left_step, 0)
+        narrow(low_a, wide_grad, 0, self.peers)
+        left_moves = [(low_a, named[self.name + "da"], held[8], held[9])]
+        right_moves = [(low_b, named[self.name + "db"], held[10], held[11])]
+        ring.start(left_moves, 0)
+        lax.fori_loop(0, SUBLANES, right_step, 0)
+        narrow(low_b, wide_grad, 0, self.peers)
+        ring.start(right_moves, 0)
+        ring.wait(left_moves, 0)
+        ring.wait(right_moves, 0)
 
 
 def by_crop(value, rows_axis, head_axis):
@@ -828,8 +917,10 @@
     for row in range(count):
         for head in range(heads):
             source = row * heads + head
+            inner = half // 2 * heads
+            place = row % inner // heads * 2 + row // inner
             for crop, pairs in ((head, same), (1 - head, other)):
-                pairs.append((source, (crop * half + row // 2) * heads + row % 2))
+                pairs.append((source, (crop * half + place) * heads + row % heads))
     head = lax.axis_index("head")
     crop = lax.axis_index("row") // half
     mine = lax.dynamic_index_in_dim(value, head, 0, keepdims=False)
@@ -867,7 +958,7 @@
     rows = tokens // peers
     row_index = lax.axis_index("row")
     crop = row_index // half
-    start = ((row_index % half) * head_count + lax.axis_index("head")) * rows
+    start = position(row_index % half, lax.axis_index("head"), half, head_count) * rows
 
     placed = by_crop(jnp.stack([pair_valid, target_bins], axis=1), row_count, head_count)
     valid, target = placed[0], placed[1]
@@ -905,7 +996,7 @@
     def gain(index):
         return (norm_gains[index][:, None], "whole")
 
-    def triangle_weights(layer, kind, names):
+    def triangle_weights(layer, kind, *names):
         weight_in, weight_out = low_input[layer, kind], low_output[layer, kind]
         found = {
             "gain0": gain(5 * layer + 2 * kind),
@@ -916,9 +1007,9 @@
             "out": (weight_out, "whole"),
             "out_t": (weight_out.T, "whole"),
         }
-        return {f"t{layer}{kind}{name}": found[name] for name in names.split()}
-
-    def transition_weights(layer, names):
+        return {f"t{layer}{kind}{name}": found[name] for name in " ".join(names).split()}
+
+    def transition_weights(layer, *names):
         found = {
             "gain": gain(5 * layer + 4),
             "up": (low_expand[layer], "whole"),
@@ -926,24 +1017,30 @@
             "down": (low_reduce[layer], "whole"),
             "down_t": (low_reduce[layer].T, "whole"),
         }
-        return {f"f{layer}{name}": found[name] for name in names.split()}
+        return {f"f{layer}{name}": found[name] for name in " ".join(names).split()}
 
     state_shape = (rows, width, tokens)
-    wire_shape = (peers, rows * SUBLANES, tokens)
     hidden = low_expand.shape[2]
     state_out = (state_shape, F32, "rows")
-    wire_out = (wire_shape, BF16, "wire")
     gate_out = (state_shape, BF16, "rows")
     gain_out = ((width, LANES), F32, "sum")
     mask_in = {"mask": (pair_mask, "rows")}
 
-    def start_outs(name):
-        return {name + "a": wire_out, name + "b": wire_out}
+    def forward(name, incoming, collective_id):
+        return Forward(peers, half, rows, tokens, name, incoming, collective_id)
+
+    def backward(name, incoming, collective_id):
+        return Backward(peers, half, rows, tokens, name, incoming, collective_id)
+
+    def owned(name):
+        return {name + "left": (got_of[name]["left"], "whole"), name + "right": (got_of[name]["right"], "whole")}
+
+    def keep(name, got):
+        got_of[name] = {part: got[name + part] for part in ("left", "right", "tri")}
 
     def back_start_outs(name):
         return {
             name + "dgate": gate_out,
-            name + "dtri": wire_out,
             name + "d_out": ((width, width), F32, "sum"),
             name + "d_gain1": gain_out,
         }
@@ -958,7 +1055,7 @@
             name + "d_gain": gain_out,
         }
 
-    states, tris, lefts, rights, middles = {}, {}, {}, {}, {}
+    states, middles, got_of = {}, {}, {}
     sums = {}
 
     def body(r):
@@ -971,6 +1068,7 @@
         write_rows(r["state"], state)
         triangle_start(r, "t00", state)
 
+    exchange = forward("t00", False, 0)
     got = run_stage(
         body,
         "first_state",
@@ -983,20 +1081,19 @@
             **mask_in,
             **triangle_weights(0, 0, "gain0 mix_t"),
         },
-        {"state": state_out, **start_outs("t00")},
+        {"state": state_out, **exchange.outs()},
         {"table_rows": table_rows},
+        exchange,
     )
     states["t00"] = got["state"]
+    keep("t00", got)
 
     for layer in range(layers):
         for kind in range(2):
             name = f"t{layer}{kind}"
-            lefts[name], rights[name], tris[name] = forward_exchange(
-                half, kind == 1, got[name + "a"], got[name + "b"]
-            )
             inputs = {
                 "state": (states[name], "rows"),
-                name + "tri": (tris[name], "wire"),
+                name + "tri": (got_of[name]["tri"], "wire"),
                 **triangle_weights(layer, kind, "gain0 gain1 gate_t out_t"),
             }
             if kind == 0:
@@ -1007,14 +1104,17 @@
                     write_rows(r["next"], state)
                     triangle_start(r, following, state)
 
+                exchange = forward(following, True, 1)
                 got = run_stage(
                     body,
                     "between_updates",
                     rows,
                     {**inputs, **mask_in, **triangle_weights(layer, 1, "gain0 mix_t")},
-                    {"next": state_out, **start_outs(following)},
+                    {"next": state_out, **exchange.outs()},
+                    exchange=exchange,
                 )
                 states[following] = got["next"]
+                keep(following, got)
             elif layer + 1 < layers:
                 following = f"t{layer + 1}0"
                 lift = f"f{layer}"
@@ -1026,6 +1126,7 @@
                     write_rows(r["next"], state)
                     triangle_start(r, following, state)
 
+                exchange = forward(following, False, 2)
                 got = run_stage(
                     body,
                     "layer_end",
@@ -1036,10 +1137,12 @@
                         **transition_weights(layer, "gain up_t down_t"),
                         **triangle_weights(layer + 1, 0, "gain0 mix_t"),
                     },
-                    {"middle": state_out, "next": state_out, **start_outs(following)},
+                    {"middle": state_out, "next": state_out, **exchange.outs()},
+                    exchange=exchange,
                 )
                 middles[layer] = got["middle"]
                 states[following] = got["next"]
+                keep(following, got)
 
     lift = f"f{layers - 1}"
 
@@ -1051,14 +1154,16 @@
         write_rows(r["grad"], grad)
         triangle_back_start(r, name, grad, kept)
 
+    exchange = backward(name, True, 3)
     got = run_stage(
         body,
         "loss",
         rows,
         {
             **inputs,
+            **owned(name),
             **triangle_weights(layers - 1, 1, "out"),
-            **transition_weights(layers - 1, "gain up_t down_t up down"),
+            **transition_weights(layers - 1, "gain up_t down_t", "up down"),
             "head_gain": gain(5 * layers),
             "logits": (low_logits, "whole"),
             "logits_t": (low_logits.T, "whole"),
@@ -1072,21 +1177,20 @@
             "d_head_gain": gain_out,
             **transition_outs(lift),
             **back_start_outs(name),
+            **exchange.outs(),
         },
+        exchange=exchange,
     )
     sums.update(got)
 
     for layer in reversed(range(layers)):
         for kind in (1, 0):
             name = f"t{layer}{kind}"
-            grad_left, grad_right = backward_exchange(
-                half, kind == 1, got[name + "dtri"], lefts[name], rights[name]
-            )
             inputs = {
                 "grad_in": (got["grad"], "rows"),
                 "state": (states[name], "rows"),
-                name + "da": (grad_left, "wire"),
-                name + "db": (grad_right, "wire"),
+                name + "da": (got[name + "da"], "wire"),
+                name + "db": (got[name + "db"], "wire"),
                 name + "dgate_in": (got[name + "dgate"], "rows"),
                 **mask_in,
                 **triangle_weights(layer, kind, "gain0 mix_t in"),
@@ -1102,17 +1206,25 @@
                     _, kept = triangle_finish(r, before, read_rows(r["before"]))
                     triangle_back_start(r, before, grad, kept)
 
+                exchange = backward(before, False, 4)
                 got = run_stage(
                     body,
                     "between_updates_back",
                     rows,
                     {
                         **inputs,
+                        **owned(before),
                         "before": (states[before], "rows"),
-                        before + "tri": (tris[before], "wire"),
-                        **triangle_weights(layer, 0, "gain0 gain1 gate_t out out_t"),
+                        before + "tri": (got_of[before]["tri"], "wire"),
+                        **triangle_weights(layer, 0, "gain0 gain1 gate_t out_t", "out"),
                     },
-                    {"grad": state_out, **back_finish_outs(name), **back_start_outs(before)},
+                    {
+                        "grad": state_out,
+                        **back_finish_outs(name),
+                        **back_start_outs(before),
+                        **exchange.outs(),
+                    },
+                    exchange=exchange,
                 )
             elif layer > 0:
                 before = f"t{layer - 1}1"
@@ -1127,24 +1239,28 @@
                     _, kept = triangle_finish(r, before, read_rows(r["before"]))
                     triangle_back_start(r, before, grad, kept)
 
+                exchange = backward(before, True, 5)
                 got = run_stage(
                     body,
                     "layer_end_back",
                     rows,
                     {
                         **inputs,
+                        **owned(before),
                         "middle": (middles[layer - 1], "rows"),
                         "before": (states[before], "rows"),
-                        before + "tri": (tris[before], "wire"),
+                        before + "tri": (got_of[before]["tri"], "wire"),
                         **transition_weights(layer - 1, "gain up_t up down"),
-                        **triangle_weights(layer - 1, 1, "gain0 gain1 gate_t out out_t"),
+                        **triangle_weights(layer - 1, 1, "gain0 gain1 gate_t out_t", "out"),
                     },
                     {
                         "grad": state_out,
                         **back_finish_outs(name),
                         **transition_outs(lift),
                         **back_start_outs(before),
+                        **exchange.outs(),
                     },
+                    exchange=exchange,
                 )
             else:
 
@@ -1269,7 +1385,7 @@
         crops == 2
         and head_count == 2
         and width == SUBLANES * peers
-        and tokens % (peers * ROW_BLOCK) == 0
+        and tokens % (peers * ROW_BLOCK * CHUNK_STEPS) == 0
         and tokens % LANES == 0
     ):
         local = gradients_by_crop(row_count, head_count, *given)

time: 1320 us -> 1090 us (0.83)
  Pallas kernels: 1050 us -> 834 us
    pallas_call x17 -> x9, Pallas kernels: 1050 us -> 834 us  [run_stage(): pl.pallas_call(kernel, grid=(steps,), in_specs=[block_spec(inputs[key][0]...]
  transfers between devices with their start and end apart: 3 -> 3, of which waited for: 1 -> 1; matrix products, arithmetic and copies ran while one was open for 4% -> 5% of each run, Pallas kernels for 0% -> 0%
where the time goes in v2:
time: 1090 us
  Pallas kernels  834 us (77%)
  waiting for transfers between devices  80.8 us (7%)
  other arithmetic  52.1 us (5%)
  local copies, waits for them, and re-layouts  48.2 us (4%)
  blocking collectives  42.1 us (4%)
  between operations  21.5 us (2%)
    pallas_call x9, Pallas kernels, run_stage(): pl.pallas_call(kernel, grid=(steps,), in_specs=[block_spec(inputs[key][0]...  834 us
    psum x1, waiting for transfers between devices, per_device(): summed = lax.psum(local, ('row', 'head'))  80.7 us
    psum x1, blocking collectives, per_device(): summed = lax.psum(local, ('row', 'head'))  42.1 us
  transfers between devices with their start and end apart: 3, of which 1 were waited for; matrix products, arithmetic and copies ran while one was open for 5% of the time, Pallas kernels for 0%

profile of v2, /device:TPU:0, one launch (start us, length us, event | category | flops | bytes accessed | tf_op | source)
XLA Modules:
  0.0 1086.3 jit_solution(3596546100059200203)
XLA Ops:
  8.8 2.1 collective-permute-start
  11.5 3.9 collective-permute-start.1
  15.4 1.4 convert_element_type.51
  26.2 1.7 copy.218.refs_1_
  51.9 95.3 %first_state.1 = (f32[24,128,384]{2,1,0:T(8,128)}, bf16[8,384,384]{2,1,0:T(8,128)(2,1)}, bf16[8,384,384]{2,1,0:T(8,128)(2,1)}, bf16[16,192,384]{2,1,0:T(8,128)(2,1)}) custom-call(s32[24,1,384]{2,1,0:T(1,128)} %compare_select_fusion.refs_0_.refs_9_, f32[24,128,1]{2,1,0:T(8,128)} %copy.218.refs_1_, f32[128,384]{1,0:T(8,128)} %bitcast.162, ...), custom_call_target="tpu_custom_call" | custom-call | tf_op jit(solution)/shard_map/first_state/pallas_call | solution.py:636
  147.2 95.5 %between_updates.2 = (f32[24,128,384]{2,1,0:T(8,128)}, bf16[8,384,384]{2,1,0:T(8,128)(2,1)}, bf16[8,384,384]{2,1,0:T(8,128)(2,1)}, bf16[16,192,384]{2,1,0:T(8,128)(2,1)}) custom-call(f32[24,128,384]{2,1,0:T(8,128)} %get-tuple-element.88.refs_0_.refs_11_.refs_1_, bf16[16,192,384]{2,1,0:T(8,128)(2,1)} %get-tuple-element.89.refs_1_.refs_12_, ...), custom_call_target="tpu_custom_call" | custom-call | tf_op jit(solution)/shard_map/between_updates/pallas_call | solution.py:636
  242.7 101.0 %layer_end.1 = (f32[24,128,384]{2,1,0:T(8,128)}, f32[24,128,384]{2,1,0:T(8,128)}, bf16[8,384,384]{2,1,0:T(8,128)(2,1)}, bf16[8,384,384]{2,1,0:T(8,128)(2,1)}, bf16[16,192,384]{2,1,0:T(8,128)(2,1)}) custom-call(f32[24,128,384]{2,1,0:T(8,128)} %get-tuple-element.90.refs_0_.refs_12_.refs_1_, bf16[16,192,384]{2,1,0:T(8,128)(2,1)} %get-tuple-element.91.refs_1_.refs_13_, ...), custom_call_target="tpu_custom_call" | custom-call | tf_op jit(solution)/shard_map/layer_end/pallas_call | solution.py:636
  343.7 96.2 %between_updates.3 = (f32[24,128,384]{2,1,0:T(8,128)}, bf16[8,384,384]{2,1,0:T(8,128)(2,1)}, bf16[8,384,384]{2,1,0:T(8,128)(2,1)}, bf16[16,192,384]{2,1,0:T(8,128)(2,1)}) custom-call(f32[24,128,384]{2,1,0:T(8,128)} %get-tuple-element.92.refs_0_.refs_11_.refs_1_, bf16[16,192,384]{2,1,0:T(8,128)(2,1)} %get-tuple-element.93.refs_1_.refs_12_, ...), custom_call_target="tpu_custom_call" | custom-call | tf_op jit(solution)/shard_map/between_updates/pallas_call | solution.py:636
  439.9 120.3 %loss.1 = (f32[24,128,384]{2,1,0:T(8,128)}, f32[1,128]{1,0:T(1,128)}, f32[128,64]{1,0:T(8,128)}, f32[128,128]{1,0:T(8,128)}, f32[128,1024]{1,0:T(8,128)}, /*inde...) custom-call(f32[24,128,384]{2,1,0:T(8,128)} %get-tuple-element.94.re, ...), custom_call_target="tpu_custom_call" | custom-call | tf_op jit(solution)/shard_map/loss/pallas_call | solution.py:636
  560.3 96.1 %between_updates_back.2 = (f32[24,128,384]{2,1,0:T(8,128)}, f32[128,640]{1,0:T(8,128)}, f32[128,128]{1,0:T(8,128)}, bf16[24,128,384]{2,1,0:T(8,128)(2,1)}, f32[1...) custom-call(f32[24,128,384]{2,1,0:T(8,128)} %get-tuple-element.99.refs_0_, ...), custom_call_target="tpu_custom_call" | custom-call | tf_op jit(solution)/shard_map/between_updates_back/pallas_call | solution.py:636
  656.4 115.0 %layer_end_back.1 = (f32[24,128,384]{2,1,0:T(8,128)}, f32[128,640]{1,0:T(8,128)}, f32[128,128]{1,0:T(8,128)}, f32[128,1024]{1,0:T(8,128)}, f32[512,128]{1,0:T(8,...) custom-call(f32[24,128,384]{2,1,0:T(8,128)} %get-tuple-element.105.r, ...), custom_call_target="tpu_custom_call" | custom-call | tf_op jit(solution)/shard_map/layer_end_back/pallas_call | solution.py:636
  771.4 96.1 %between_updates_back.3 = (f32[24,128,384]{2,1,0:T(8,128)}, f32[128,640]{1,0:T(8,128)}, f32[128,128]{1,0:T(8,128)}, bf16[24,128,384]{2,1,0:T(8,128)(2,1)}, f32[1...) custom-call(f32[24,128,384]{2,1,0:T(8,128)} %get-tuple-element.112.refs_0_, ...), custom_call_target="tpu_custom_call" | custom-call | tf_op jit(solution)/shard_map/between_updates_back/pallas_call | solution.py:636
  867.5 18.2 %first_state_back.1 = (f32[128,640]{1,0:T(8,128)}, f32[128,128]{1,0:T(8,128)}, f32[128,80]{1,0:T(8,128)}, f32[24,128,128]{2,1,0:T(8,128)}, f32[128,384]{1,0:T(8,128)}) custom-call(f32[24,128,384]{2,1,0:T(8,128)} %get-tuple-element.118.refs_0_, f32[24,128,384]{2,1,0:T(8,128)} %get-tuple-element.88.refs_0_.refs_11_.refs_1_, ...), custom_call_target="tpu_custom_call" | custom-call | tf_op jit(solution)/shard_map/first_state_back/pallas_call | solution.py:636
  887.1 1.9 reduce_sum.201
  895.5 1.5 copy.286
  897.0 1.5 copy.285
  906.2 42.1 %all-reduce.7 = (f32[]{:T(128)}, f32[]{:T(128)}, f32[66,128]{0,1:T(8,128)S(1)}, f32[128,64]{1,0:T(8,128)S(1)}, f32[11,128]{1,0:T(8,128)S(1)}) all-reduce(f32[]{:T(128)} %reduce_sum.198, f32[]{:T(128)} %fusion.18, f32[66,128]{0,1:T(8,128)S(1)} %slice_bitcast_fusion.16, ...), channel_id=1, replica_groups=mesh['row'=16,'head'=2] {'row','head'}, use_global_device_ids=true, to_apply=%region_1.2 | all-reduce | flops 18050 | bytes 144400 | tf_op jit(solution)/shard_map/psum | solution.py:1394
  952.1 80.7 %all-reduce.6.cloned.1.call-done = (f32[384,256]{0,1:T(8,128)}, f32[2,2,128,640]{3,2,1,0:T(8,128)}, f32[2,2,128,128]{3,2,1,0:T(8,128)}, f32[2,128,1024]{2,1,0:T(8,128)}, f32[2,512,128]{2,1,0:T(8,128)}) async-done(((f32[384,256]{0,1:T(8,128)}, f32[2,2,128,640]{3,2,1,0:T(8,128)}, f32[2,2,128,128]{3,2,1,0:T(8,128)}, f32[2,128,1024]{2,1,0:T(8,128)}, f32[2,512,128]{2,1,0:T(8,128)}), (f32[384,256]{0,1:T(8,128)}, ...) | async-done | bytes 3538960 | tf_op jit(solution)/shard_map/psum | solution.py:1394
  1032.8 2.5 multiply_reduce_fusion.3
  1035.3 3.0 multiply_reduce_fusion
  1039.6 1.5 multiply_reduce_fusion.1
  1050.7 1.8 multiply_subtract_fusion.3
  1053.4 2.0 copy.293
  1055.4 1.9 copy.294
  1057.3 2.2 multiply_subtract_fusion.5
  1059.6 1.5 copy.295
  1061.1 1.5 copy.296
  1062.7 1.5 copy.297
  1064.3 5.4 multiply_subtract_fusion
  1069.7 1.7 multiply_subtract_fusion.4
  1071.5 3.1 multiply_subtract_fusion.1
  1074.7 2.1 multiply_subtract_fusion.2
  (243 shorter events, 62.2 us)
Async XLA Ops:
  7.2 12.3 %copy-start = (bf16[2,384,384]{2,1,0:T(8,128)(2,1)S(1)}, bf16[2,384,384]{2,1,0:T(8,128)(2,1)}, u32[]{:S(2)}) copy-start(bf16[2,384,384]{2,1,0:T(8,128)(2,1)} %param.30) | copy-start | bytes 1769476
  7.2 1025.6 %all-reduce.6.cloned.1.call-start = ((), (), s32[]{:S(2)}) async-start(), calls=%async_computation | async-start | bytes 7077888 | tf_op jit(solution)/shard_map/psum | solution.py:1394
  8.8 40.8 %collective-permute-start = (s32[2,24,192]{2,0,1:T(2,128)}, s32[2,24,192]{2,0,1:T(2,128)}, u32[]{:S(2)}, u32[]{:S(2)}) collective-permute-start(s32[2,24,192]{2,0,1:T(2,128)} %bitcast.157), channel_id=1, source_target_pairs={{0,0},{1,16},{2,1},{3,17},{4,4},{5,20},{6,5},{7,21},{8,8},{9,24},{... | collective-permute-start | bytes 110600 | tf_op jit(solution)/shard_map/ppermute | solution.py:928
  11.5 38.1 %collective-permute-start.1 = (s32[2,24,192]{2,0,1:T(2,128)}, s32[2,24,192]{2,0,1:T(2,128)}, u32[]{:S(2)}, u32[]{:S(2)}) collective-permute-start(s32[2,24,192]{2,0,1:T(2,128)} %bitcast.156), channel_id=1, source_target_pairs={{0,16},{1,0},{2,17},{3,1},{4,20},{5,4},{6,21},{7,5},{8,24},{9,8},{... | collective-permute-start | bytes 110600 | tf_op jit(solution)/shard_map/ppermute | solution.py:929
  23.9 5.6 copy-start.24
  24.6 6.4 copy-start.42
  26.2 25.0 %copy-start.61 = (f32[24]{0:T(128)}, f32[24]{0:T(128)S(1)}, u32[]{:S(2)}) copy-start(f32[24]{0:T(128)S(1)} %fusion.30) | copy-start | bytes 292
  26.2 7.0 copy-start.23
  26.2 8.5 copy-start.44
  27.9 11.3 %copy-start.22 = (bf16[512,128]{0,1:T(8,128)(2,1)S(1)}, bf16[512,128]{0,1:T(8,128)(2,1)}, u32[]{:S(2)}) copy-start(bf16[512,128]{0,1:T(8,128)(2,1)} %get-tuple-element.311) | copy-start | bytes 393220
  27.9 12.8 %copy-start.43 = (bf16[128,128]{0,1:T(8,128)(2,1)S(1)}, bf16[128,128]{0,1:T(8,128)(2,1)}, u32[]{:S(2)}) copy-start(bf16[128,128]{0,1:T(8,128)(2,1)} %get-tuple-element.314) | copy-start | bytes 98308
  894.5 10.4 copy-start.50
  894.5 10.5 copy-start.49
  894.5 10.6 copy-start.48
  894.9 10.3 copy-start.47
  894.9 10.4 copy-start.46
  895.0 10.5 copy-start.62
  895.2 11.0 %copy-start.45 = (f32[128,64]{1,0:T(8,128)S(1)}, f32[128,64]{1,0:T(8,128)}, u32[]{:S(2)}) copy-start(f32[128,64]{1,0:T(8,128)} %get-tuple-element.137) | copy-start | bytes 98308
  895.4 10.8 copy-start.51
  948.3 92.9 %copy-start.38 = (f32[128,64]{1,0:T(8,128)}, f32[128,64]{1,0:T(8,128)S(1)}, u32[]{:S(2)}) copy-start(f32[128,64]{1,0:T(8,128)S(1)} %get-tuple-element.233) | copy-start | bytes 98308
  1032.8 5.4 copy-start.18
  1032.8 6.8 copy-start.5
  1035.3 5.9 copy-start.9
  1038.3 12.4 %copy-start.11 = (f32[384,256]{0,1:T(8,128)S(1)}, f32[384,256]{0,1:T(8,128)}, u32[]{:S(2)}) copy-start(f32[384,256]{0,1:T(8,128)} %get-tuple-element.235) | copy-start | bytes 1179652
  1052.5 11.7 %copy-start.2 = (f32[2,2,128,640]{3,2,1,0:T(8,128)S(1)}, f32[2,2,128,640]{3,2,1,0:T(8,128)}, u32[]{:S(2)}) copy-start(f32[2,2,128,640]{3,2,1,0:T(8,128)} %param.38) | copy-start | bytes 3932164
  1053.4 10.8 copy-start.1
  1064.2 5.5 copy-start.19
  1064.2 5.5 copy-start.36
  1064.2 5.5 copy-start.37
  1064.2 7.2 copy-start.6
  1064.2 7.2 copy-start.20
  1064.2 7.2 copy-start.21
  (38 other events, 88.4 us)
Sparse Core Ops, SparseCore 0:
  894.3 138.4 all-reduce.5

commit v3 on v0

--- a/solution.py
+++ b/solution.py
@@ -1,6 +1,10 @@
+import functools
+
 import jax
 import jax.numpy as jnp
 from jax import lax
+from jax.experimental import pallas as pl
+from jax.experimental.pallas import tpu as pltpu
 from jax.sharding import PartitionSpec as P
 
 STEP = 10
@@ -248,7 +252,1379 @@
     return (first_new, second_new, weight - rate * (moved + decay * weight))
 
 
+def gradients_by_block(
+    single,
+    residue_index,
+    chain_index,
+    token_mask,
+    pair_valid,
+    target_bins,
+    relative_table,
+    single_weight,
+    triangle_input,
+    triangle_output,
+    expand_weight,
+    reduce_weight,
+    distogram_weight,
+    norm_gains,
+):
+    crops, rows, cols = pair_valid.shape
+    width = relative_table.shape[1]
+    layers = triangle_input.shape[0]
+    row_start = lax.axis_index("row") * rows
+    col_start = lax.axis_index("head") * cols
+
+    def take(array, start, count):
+        return lax.dynamic_slice_in_dim(array, start, count, 1)
+
+    offset = (
+        take(residue_index, row_start, rows)[:, :, None]
+        - take(residue_index, col_start, cols)[:, None, :]
+    )
+    same = (
+        take(chain_index, row_start, rows)[:, :, None]
+        == take(chain_index, col_start, cols)[:, None, :]
+    )
+    reach = (relative_table.shape[0] - 2) // 2
+    bins = jnp.where(same, jnp.clip(offset, -reach, reach) + reach, 2 * reach + 1)
+    relative_hot = (
+        bins[..., None] == jnp.arange(relative_table.shape[0])[None, None, None, :]
+    ).astype(jnp.float32)
+    token_rows = take(token_mask, row_start, rows).astype(jnp.float32)
+    token_cols = take(token_mask, col_start, cols).astype(jnp.float32)
+    pair_mask = token_rows[:, :, None] * token_cols[:, None, :]
+    loss_weight = pair_mask * pair_valid.astype(jnp.float32)
+    low_input = triangle_input.astype(jnp.bfloat16)
+    low_output = triangle_output.astype(jnp.bfloat16)
+    low_expand = expand_weight.astype(jnp.bfloat16)
+    low_reduce = reduce_weight.astype(jnp.bfloat16)
+    low_logits = distogram_weight.astype(jnp.bfloat16)
+    proj = project(single, single_weight.astype(jnp.bfloat16))
+    state = project(relative_hot.astype(jnp.bfloat16), relative_table.astype(jnp.bfloat16))
+    state = (
+        state
+        + take(proj, row_start, rows)[:, :, None, :width]
+        + take(proj, col_start, cols)[:, None, :, width:]
+    )
+    inputs = []
+    for layer in range(layers):
+        inputs.append(state)
+        state, unused = block_forward(
+            state,
+            low_input[layer],
+            low_output[layer],
+            low_expand[layer],
+            low_reduce[layer],
+            norm_gains[5 * layer : 5 * layer + 5],
+            pair_mask,
+        )
+    head_unit, head_scale = normalize(state)
+    shown = (head_unit * norm_gains[5 * layers]).astype(jnp.bfloat16)
+    logits = project(shown, low_logits)
+    largest = jnp.max(logits, axis=-1, keepdims=True)
+    log_total = largest + jnp.log(jnp.sum(jnp.exp(logits - largest), axis=-1, keepdims=True))
+    target_hot = (
+        target_bins[..., None] == jnp.arange(logits.shape[-1])[None, None, None, :]
+    ).astype(jnp.float32)
+    picked = jnp.sum(logits * target_hot, axis=-1)
+    loss_local = jnp.sum(loss_weight * (log_total[..., 0] - picked))
+    grad_scores = (loss_weight[..., None] * (jnp.exp(logits - log_total) - target_hot)).astype(
+        jnp.bfloat16
+    )
+    grad_logits = weight_grad(shown, grad_scores)
+    grad_shown = project_back(grad_scores, low_logits)
+    grad_state, gain_last = norm_back(grad_shown, head_unit, head_scale, norm_gains[5 * layers])
+    collected = []
+    for layer in reversed(range(layers)):
+        grad_state, layer_grads = block_backward(
+            grad_state,
+            inputs[layer],
+            low_input[layer],
+            low_output[layer],
+            low_expand[layer],
+            low_reduce[layer],
+            norm_gains[5 * layer : 5 * layer + 5],
+            pair_mask,
+        )
+        collected.insert(0, layer_grads)
+    grad_input = jnp.stack([entry[0] for entry in collected])
+    grad_output = jnp.stack([entry[1] for entry in collected])
+    grad_expand = jnp.stack([entry[2] for entry in collected])
+    grad_reduce = jnp.stack([entry[3] for entry in collected])
+    grad_gains = jnp.concatenate(
+        [jnp.concatenate([entry[4] for entry in collected], axis=0), gain_last[None]], axis=0
+    )
+    grad_table = jnp.einsum(
+        "bijr,bijc->rc", relative_hot, grad_state, precision=lax.Precision.HIGHEST
+    )
+    single_wide = single.astype(jnp.float32)
+    row_part = jnp.einsum(
+        "bis,bic->sc",
+        take(single_wide, row_start, rows),
+        jnp.sum(grad_state, axis=2),
+        precision=lax.Precision.HIGHEST,
+    )
+    col_part = jnp.einsum(
+        "bjs,bjc->sc",
+        take(single_wide, col_start, cols),
+        jnp.sum(grad_state, axis=1),
+        precision=lax.Precision.HIGHEST,
+    )
+    grad_single = jnp.concatenate([row_part, col_part], axis=1)
+    return (
+        loss_local,
+        jnp.sum(loss_weight),
+        grad_table,
+        grad_single,
+        grad_input,
+        grad_output,
+        grad_expand,
+        grad_reduce,
+        grad_logits,
+        grad_gains,
+    )
+
+
+F32 = jnp.float32
+BF16 = jnp.bfloat16
+LANES = 128
+SUBLANES = 8
+PACKED = 16
+ROW_BLOCK = 2
+PHASES = SUBLANES // ROW_BLOCK
+CHUNK_ROWS = SUBLANES * SUBLANES
+VMEM_BYTES = 58 * 2**20
+MESH = pl.DeviceIdType.MESH
+ROWS, WIRE, WHOLE, SUM, ANYWHERE = range(5)
+
+
+class Bag:
+    def __init__(self, **entries):
+        self.__dict__.update(entries)
+
+
+class Arg:
+    def __init__(self, array, kind, index=None, block=None, column=None):
+        self.array, self.kind, self.index, self.block = array, kind, index, block
+        self.column = column
+
+    def spec(self):
+        if self.index is None:
+            return block_spec(self.array.shape, self.kind)
+        index = self.index
+        return pl.BlockSpec(self.block, lambda step: index)
+
+
+class Column:
+    def __init__(self, ref, column):
+        self.ref, self.column = ref, column
+
+    def __getitem__(self, _):
+        return self.ref[:, self.column : self.column + 1]
+
+
+class Out:
+    def __init__(self, shape, dtype, kind):
+        self.shape, self.dtype, self.kind = shape, dtype, kind
+
+    def spec(self):
+        return block_spec(self.shape, self.kind)
+
+
+def block_spec(shape, kind):
+    if kind == ANYWHERE:
+        return pl.BlockSpec(memory_space=pl.ANY)
+    if kind == WIRE:
+        return pl.BlockSpec((shape[0], CHUNK_ROWS, shape[2]), lambda step: (0, step // PHASES, 0))
+    if kind == ROWS:
+        return pl.BlockSpec((ROW_BLOCK,) + shape[1:], lambda step: (step,) + (0,) * (len(shape) - 1))
+    return pl.BlockSpec(shape, lambda step: (0,) * len(shape))
+
+
+def is_leaf(value):
+    return isinstance(value, (Arg, Out))
+
+
+def bag_of(tree, leaves):
+    return Bag(
+        **{
+            key: next(leaves) if is_leaf(value) else bag_of(value, leaves)
+            for key, value in tree.items()
+        }
+    )
+
+
+def leaves_of(tree):
+    found = []
+    for value in tree.values():
+        found.extend([value] if is_leaf(value) else leaves_of(value))
+    return found
+
+
+def dot(left, right):
+    return lax.dot_general(left, right, (((1,), (0,)), ((), ())), preferred_element_type=F32)
+
+
+def dot_pairs(left, right):
+    return lax.dot_general(left, right, (((1,), (1,)), ((), ())), preferred_element_type=F32)
+
+
+def product_of(left, right, left_axis, right_axis):
+    return lax.dot_general(
+        left, right, (((left_axis,), (right_axis,)), ((), ())), preferred_element_type=F32
+    )
+
+
+def sigmoid(value):
+    return 0.5 * jnp.tanh(0.5 * value) + 0.5
+
+
+def unit_of(value):
+    centred = value - jnp.mean(value, axis=0, keepdims=True)
+    scale = lax.rsqrt(jnp.mean(centred * centred, axis=0, keepdims=True) + EPS)
+    return (centred * scale, scale)
+
+
+def unit_back(grad, unit, scale, gain):
+    scaled = grad * gain
+    first = jnp.mean(scaled, axis=0, keepdims=True)
+    second = jnp.mean(scaled * unit, axis=0, keepdims=True)
+    return scale * (scaled - first - unit * second)
+
+
+def fold(value):
+    total = value[:, :LANES]
+    for start in range(LANES, value.shape[1], LANES):
+        total = total + value[:, start : start + LANES]
+    return total
+
+
+def read_rows(ref):
+    return jnp.concatenate([ref[row] for row in range(ref.shape[0])], axis=1)
+
+
+def write_rows(ref, value):
+    cols = ref.shape[2]
+    for row in range(ref.shape[0]):
+        ref[row] = value[:, row * cols : (row + 1) * cols].astype(ref.dtype)
+
+
+class Wire:
+    def __init__(self, wide, phase):
+        self.wide, self.phase = wide, phase
+
+    def tokens(self, row):
+        width = self.wide.shape[1] // SUBLANES
+        return pl.ds(self.phase * ROW_BLOCK + row, width, stride=SUBLANES)
+
+    def read(self):
+        lanes = self.wide.shape[0]
+        return jnp.concatenate(
+            [
+                self.wide[lane, self.tokens(row), :]
+                for row in range(ROW_BLOCK)
+                for lane in range(lanes)
+            ],
+            axis=1,
+        )
+
+    def write(self, value):
+        lanes = self.wide.shape[0]
+        for row in range(ROW_BLOCK):
+            for lane in range(lanes):
+                start = (row * lanes + lane) * LANES
+                self.wide[lane, self.tokens(row), :] = value[:, start : start + LANES]
+
+
+def widen(wide, block):
+    def step(peer, carry):
+        value = block[peer].astype(F32)
+        start = pl.multiple_of(peer * CHUNK_ROWS, CHUNK_ROWS)
+        for lane in range(wide.shape[0]):
+            wide[lane, pl.ds(start, CHUNK_ROWS), :] = value[:, lane * LANES : (lane + 1) * LANES]
+        return carry
+
+    lax.fori_loop(0, block.shape[0], step, 0)
+
+
+def narrow(low, wide, chunk):
+    rows = pl.ds(pl.multiple_of(chunk * CHUNK_ROWS, CHUNK_ROWS), CHUNK_ROWS)
+
+    def step(peer, carry):
+        start = pl.multiple_of(peer * CHUNK_ROWS, CHUNK_ROWS)
+        low[peer, rows, :] = jnp.concatenate(
+            [wide[lane, pl.ds(start, CHUNK_ROWS), :] for lane in range(wide.shape[0])], axis=1
+        ).astype(low.dtype)
+        return carry
+
+    lax.fori_loop(0, low.shape[0], step, 0)
+
+
+def triangle_start(weights, mask, left_wire, right_wire, state):
+    width = state.shape[0]
+    unit, _ = unit_of(state)
+    normed = (unit * weights.gain0[...]).astype(BF16)
+    mixed = dot(weights.mix_t[...], normed)
+    for wire, base in ((left_wire, 0), (right_wire, 2 * width)):
+        gate = sigmoid(mixed[base : base + width])
+        wire.write(mask * gate * mixed[base + width : base + 2 * width])
+
+
+def triangle_finish(weights, wire, state):
+    unit, _ = unit_of(state)
+    normed = (unit * weights.gain0[...]).astype(BF16)
+    gate = sigmoid(dot(weights.gate_t[...], normed))
+    tri_unit, tri_scale = unit_of(wire.read())
+    shaped = (tri_unit * weights.gain1[...]).astype(BF16)
+    branch = dot(weights.out_t[...], shaped)
+    return (state + gate * branch, (gate, tri_unit, tri_scale, shaped, branch))
+
+
+def triangle_back_start(weights, o, wire, grad, kept):
+    gate, tri_unit, tri_scale, shaped, branch = kept
+    grad_branch = (grad * gate).astype(BF16)
+    write_rows(o.grad_gate, grad * branch * gate * (1.0 - gate))
+    o.out[...] += dot_pairs(shaped, grad_branch)
+    grad_shaped = dot(weights.out[...], grad_branch)
+    o.gain1[...] += fold(grad_shaped * tri_unit)
+    wire.write(unit_back(grad_shaped, tri_unit, tri_scale, weights.gain1[...]))
+
+
+def triangle_back_finish(weights, i, o, mask, grad, state):
+    width = state.shape[0]
+    unit, scale = unit_of(state)
+    gain = weights.gain0[...]
+    normed = (unit * gain).astype(BF16)
+    mixed = dot(weights.mix_t[...], normed)
+    parts = []
+    for wire, base in ((i.grad_left, 0), (i.grad_right, 2 * width)):
+        back = wire.read() * mask
+        gate = sigmoid(mixed[base : base + width])
+        back_gate = back * gate
+        parts.append((back_gate * mixed[base + width : base + 2 * width] * (1.0 - gate)).astype(BF16))
+        parts.append(back_gate.astype(BF16))
+    parts.append(read_rows(i.grad_gate))
+    grad_mixed = jnp.concatenate(parts, axis=0)
+    o.mix[...] += dot_pairs(normed, grad_mixed)
+    grad_normed = dot(weights.mix[...], grad_mixed)
+    o.gain0[...] += fold(grad_normed * unit)
+    return grad + unit_back(grad_normed, unit, scale, gain)
+
+
+def transition(weights, state):
+    unit, scale = unit_of(state)
+    lifted = (unit * weights.gain[...]).astype(BF16)
+    inner = dot(weights.up_t[...], lifted)
+    half = inner.shape[0] // 2
+    gate = inner[:half]
+    slope = sigmoid(gate)
+    product = (gate * slope * inner[half:]).astype(BF16)
+    return (unit, scale, lifted, inner, slope, product)
+
+
+def transition_finish(weights, state, kept):
+    return state + dot(weights.down_t[...], kept[5])
+
+
+def transition_back(weights, o, grad, kept):
+    unit, scale, lifted, inner, slope, product = kept
+    half = inner.shape[0] // 2
+    gate, up = inner[:half], inner[half:]
+    grad_low = grad.astype(BF16)
+    o.down[...] += dot_pairs(product, grad_low)
+    grad_product = dot(weights.down[...], grad_low)
+    scaled = grad_product * slope
+    grad_inner = jnp.concatenate(
+        [
+            (scaled * up * (1.0 + gate * (1.0 - slope))).astype(BF16),
+            (scaled * gate).astype(BF16),
+        ],
+        axis=0,
+    )
+    o.up[...] += dot_pairs(lifted, grad_inner)
+    grad_lifted = dot(weights.up[...], grad_inner)
+    o.gain[...] += fold(grad_lifted * unit)
+    return grad + unit_back(grad_lifted, unit, scale, weights.gain[...])
+
+
+def head_back(i, o, state):
+    unit, scale = unit_of(state)
+    gain = i.gain[...]
+    shown = (unit * gain).astype(BF16)
+    logits = dot(i.logits_t[...], shown)
+    largest = jnp.max(logits, axis=0, keepdims=True)
+    raised = jnp.exp(logits - largest)
+    total = jnp.sum(raised, axis=0, keepdims=True)
+    log_total = largest + jnp.log(total)
+    target = read_rows(i.target)
+    weight = read_rows(i.weight)
+    hot = lax.broadcasted_iota(jnp.int32, logits.shape, 0) == target
+    picked = jnp.sum(jnp.where(hot, logits, 0.0), axis=0, keepdims=True)
+    o.loss[...] += fold(weight * (log_total - picked))
+    o.count[...] += fold(weight)
+    share = raised * (1.0 / total)
+    grad_scores = (weight * (share - jnp.where(hot, 1.0, 0.0))).astype(BF16)
+    o.logits[...] += dot_pairs(grad_scores, shown)
+    grad_shown = dot(i.logits[...], grad_scores)
+    o.gain[...] += fold(grad_shown * unit)
+    return unit_back(grad_shown, unit, scale, gain)
+
+
+def bins_hot(bins, table_rows):
+    bins = read_rows(bins)
+    shape = (table_rows, bins.shape[1])
+    return jnp.where(lax.broadcasted_iota(jnp.int32, shape, 0) == bins, 1.0, 0.0).astype(BF16)
+
+
+def run_stage(body, name, rows, inputs, outputs, exchange=None):
+    args, outs = leaves_of(inputs), leaves_of(outputs)
+    steps = rows // ROW_BLOCK
+    chunks = rows // SUBLANES
+    wire_args = [index for index, arg in enumerate(args) if arg.kind == WIRE]
+    wires = exchange.wires if exchange else 0
+    chunk_scratch = []
+    if wire_args:
+        peers, _, tokens = args[wire_args[0]].array.shape
+    if exchange:
+        peers, tokens = exchange.peers, exchange.tokens
+    for _ in range(len(wire_args) + wires):
+        chunk_scratch.append(pltpu.VMEM((tokens // LANES, peers * CHUNK_ROWS, LANES), F32))
+    scratch = exchange.scratch() if exchange else []
+
+    def kernel(*refs):
+        step = pl.program_id(0)
+        phase, chunk = lax.rem(step, PHASES), lax.div(step, PHASES)
+        in_refs = [
+            ref if arg.column is None else Column(ref, arg.column) for arg, ref in zip(args, refs)
+        ]
+        out_refs = list(refs[len(args) : len(args) + len(outs)])
+        wide = list(refs[len(args) + len(outs) :][: len(chunk_scratch)])
+        held = refs[len(args) + len(outs) + len(chunk_scratch) :]
+        ring = Exchange(exchange.peers, exchange.half) if exchange else None
+
+        @pl.when(step == 0)
+        def _():
+            if exchange:
+                ring.greet()
+            for out, ref in zip(outs, out_refs):
+                if out.kind == SUM:
+                    ref[...] = jnp.zeros(out.shape, out.dtype)
+
+        @pl.when(phase == 0)
+        def _():
+            for index, target in zip(wire_args, wide):
+                widen(target, in_refs[index])
+
+        body_in = list(in_refs)
+        for index, source in zip(wire_args, wide):
+            body_in[index] = Wire(source, phase)
+        sent = wide[len(wire_args) :]
+        i, o = bag_of(inputs, iter(body_in)), bag_of(outputs, iter(out_refs))
+        body(i, o, *[Wire(target, phase) for target in sent])
+        if exchange:
+            moves = exchange.moves(held)
+
+            @pl.when(phase == PHASES - 1)
+            def _():
+                for source, move in zip(sent, moves):
+                    narrow(move[0], source, chunk)
+
+                @pl.when(chunk == 0)
+                def _():
+                    ring.meet()
+
+                ring.start(moves, chunk)
+
+            @pl.when(step == steps - 1)
+            def _():
+                def wait(index, carry):
+                    ring.wait(moves, index)
+                    return carry
+
+                lax.fori_loop(0, chunks, wait, 0)
+                exchange.finish(ring, bag_of(inputs, iter(in_refs)), o, held)
+
+    results = pl.pallas_call(
+        kernel,
+        grid=(steps,),
+        in_specs=[arg.spec() for arg in args],
+        out_specs=[out.spec() for out in outs],
+        out_shape=[jax.ShapeDtypeStruct(out.shape, out.dtype) for out in outs],
+        scratch_shapes=chunk_scratch + scratch,
+        compiler_params=pltpu.CompilerParams(
+            dimension_semantics=(pltpu.ARBITRARY,),
+            vmem_limit_bytes=VMEM_BYTES,
+            has_side_effects=exchange is not None,
+            collective_id=exchange.collective_id if exchange else None,
+        ),
+        cost_estimate=pl.CostEstimate(flops=10**11, bytes_accessed=10**6, transcendentals=0),
+        name=name,
+    )(*[arg.array for arg in args])
+    return bag_of(outputs, iter(results))
+
+
+def flip(value, step, count):
+    result, bit = 0, 1
+    while bit < count:
+        result = result + lax.rem(lax.div(value, bit) + (step // bit) % 2, 2) * bit
+        bit *= 2
+    return result
+
+
+def position(row, head, half, heads):
+    inner = half // 2 * heads
+    return (row % 2) * inner + (row // 2) * heads + head
+
+
+def place_of(position, half, heads):
+    inner = half // 2 * heads
+    rest = lax.rem(position, inner)
+    return (lax.div(rest, heads) * 2 + lax.div(position, inner), lax.rem(rest, heads))
+
+
+class Exchange:
+    def __init__(self, count, half):
+        row, head = lax.axis_index("row"), lax.axis_index("head")
+        place = lax.rem(row, half)
+        inner = count // 2
+        self.count = count
+        self.half = half
+        self.base = row - place
+        self.me = lax.rem(place, 2) * inner + lax.div(place, 2) * (count // half) + head
+        self.twin = (lax.rem(row + half, 2 * half), head)
+        self.order = []
+        for step in range(1, count):
+            for other in (step, step ^ (inner - 1)):
+                if other and other not in self.order:
+                    self.order.append(other)
+
+    def peer(self, step):
+        return flip(self.me, step, self.count)
+
+    def device(self, peer):
+        place, head = place_of(peer, self.half, self.count // self.half)
+        return (self.base + place, head)
+
+    def greet(self):
+        barrier = pltpu.get_barrier_semaphore()
+        for step in self.order:
+            pl.semaphore_signal(
+                barrier, inc=1, device_id=self.device(self.peer(step)), device_id_type=MESH
+            )
+
+    def meet(self):
+        pl.semaphore_wait(pltpu.get_barrier_semaphore(), self.count - 1)
+
+    def copies(self, moves, chunk, steps):
+        found = []
+        for step in steps:
+            peer = self.peer(step)
+            for source, target, send_sems, recv_sems in moves:
+                size = source.shape[1] // send_sems.shape[0]
+                rows = pl.ds(pl.multiple_of(chunk * size, PACKED), size)
+                if step == 0:
+                    copy = pltpu.make_async_copy(
+                        source.at[self.me, rows, :],
+                        target.at[self.me, rows, :],
+                        send_sems.at[chunk, 0],
+                    )
+                else:
+                    copy = pltpu.make_async_remote_copy(
+                        src_ref=source.at[peer, rows, :],
+                        dst_ref=target.at[self.me, rows, :],
+                        send_sem=send_sems.at[chunk, step],
+                        recv_sem=recv_sems.at[chunk, step],
+                        device_id=self.device(peer),
+                        device_id_type=MESH,
+                    )
+                found.append(copy)
+        return found
+
+    def start(self, moves, chunk):
+        for copy in self.copies(moves, chunk, self.order + [0]):
+            copy.start()
+
+    def wait(self, moves, chunk):
+        for copy in self.copies(moves, chunk, self.order + [0]):
+            copy.wait()
+
+
+def join_channels(got, pair):
+    peers, rows, _ = got.shape
+    even, odd = [], []
+    for peer in range(peers):
+        for start in range(0, rows, CHUNK_ROWS):
+            piece = got[peer, pl.ds(pl.multiple_of(start + pair * PACKED, PACKED), PACKED), :]
+            piece = piece.astype(F32)
+            even.append(piece[:SUBLANES])
+            odd.append(piece[SUBLANES:])
+    return [jnp.concatenate(pieces, axis=0).astype(BF16) for pieces in (even, odd)]
+
+
+def split_channels(low, pair, even, odd, first=0):
+    chunks = low.shape[1] // CHUNK_ROWS
+    for start in range(0, even.shape[0], SUBLANES):
+        block = (first + start) // SUBLANES
+        row = block % chunks * CHUNK_ROWS + pair * PACKED
+        low[block // chunks, pl.ds(pl.multiple_of(row, PACKED), PACKED), :] = jnp.concatenate(
+            [even[start : start + SUBLANES], odd[start : start + SUBLANES]], axis=0
+        ).astype(low.dtype)
+
+
+def each_pair(body):
+    def step(pair, carry):
+        body(pair)
+        return carry
+
+    lax.fori_loop(0, SUBLANES // 2, step, 0)
+
+
+class Forward:
+    wires = 2
+
+    def __init__(self, peers, half, rows, tokens, incoming, collective_id):
+        self.peers, self.half, self.incoming = peers, half, incoming
+        self.rows, self.tokens = rows * SUBLANES, tokens
+        self.chunks = rows // SUBLANES
+        self.collective_id = collective_id
+
+    def outs(self):
+        block = (SUBLANES, self.tokens, self.tokens)
+        return dict(
+            left=Out(block, BF16, WHOLE),
+            right=Out(block, BF16, WHOLE),
+            tri=Out((self.peers, self.rows, self.tokens), BF16, ANYWHERE),
+        )
+
+    def scratch(self):
+        low = pltpu.VMEM((self.peers, self.rows, self.tokens), BF16)
+        many = pltpu.SemaphoreType.DMA((self.chunks, self.peers))
+        once = pltpu.SemaphoreType.DMA((1, self.peers))
+        return [low] * 5 + [many] * 4 + [once] * 2
+
+    def moves(self, held):
+        return [(held[0], held[2], held[5], held[6]), (held[1], held[3], held[7], held[8])]
+
+    def finish(self, ring, i, o, held):
+        _, _, left_got, right_got, low = held[:5]
+        axis = 0 if self.incoming else 1
+        middle = self.tokens * 2 // 3 // LANES * LANES
+        tri = [(low, o.tri, held[9], held[10])]
+
+        def multiply(pair, first, last):
+            found = []
+            for channel in (2 * pair, 2 * pair + 1):
+                left, right = o.left[channel], o.right[channel]
+                part = left[:, first:last] if self.incoming else left[first:last]
+                found.append(product_of(part, right, axis, axis))
+            split_channels(low, pair, *found, first)
+
+        def join(pair):
+            for got, out in ((left_got, o.left), (right_got, o.right)):
+                for index, value in enumerate(join_channels(got, pair)):
+                    out[2 * pair + index] = value
+            multiply(pair, 0, middle)
+
+        each_pair(join)
+        self.send_to(ring, tri, 0)
+        each_pair(lambda pair: multiply(pair, middle, self.tokens))
+        self.send_to(ring, tri, 1)
+        ring.wait(tri, 0)
+
+    def send_to(self, ring, tri, part):
+        inner = self.peers // 2
+        mine = lax.div(ring.me, inner)
+
+        @pl.when(mine == part)
+        def _():
+            for copy in ring.copies(tri, 0, [step for step in ring.order if step < inner] + [0]):
+                copy.start()
+
+        @pl.when(mine != part)
+        def _():
+            for copy in ring.copies(tri, 0, [step for step in ring.order if step >= inner]):
+                copy.start()
+
+
+class Backward:
+    wires = 1
+
+    def __init__(self, peers, half, rows, tokens, incoming, collective_id):
+        self.peers, self.half, self.incoming = peers, half, incoming
+        self.rows, self.tokens = rows * SUBLANES, tokens
+        self.chunks = rows // SUBLANES
+        self.collective_id = collective_id
+
+    def outs(self):
+        wire = (self.peers, self.rows, self.tokens)
+        return dict(grad_left=Out(wire, BF16, ANYWHERE), grad_right=Out(wire, BF16, ANYWHERE))
+
+    def scratch(self):
+        low = pltpu.VMEM((self.peers, self.rows, self.tokens), BF16)
+        block = pltpu.VMEM((SUBLANES, self.tokens, self.tokens), BF16)
+        many = pltpu.SemaphoreType.DMA((self.chunks, self.peers))
+        once = pltpu.SemaphoreType.DMA((1, self.peers))
+        return [low] * 4 + [block] + [many] * 2 + [once] * 4
+
+    def moves(self, held):
+        return [(held[0], held[1], held[5], held[6])]
+
+    def finish(self, ring, i, o, held):
+        _, got, left_low, right_low, grads = held[:5]
+
+        def left_step(pair):
+            found = []
+            for index, grad in enumerate(join_channels(got, pair)):
+                channel = 2 * pair + index
+                grads[channel] = grad
+                right = i.owned.right[channel]
+                found.append(
+                    product_of(right, grad, 1, 1) if self.incoming else product_of(grad, right, 1, 0)
+                )
+            split_channels(left_low, pair, *found)
+
+        def right_step(pair):
+            found = []
+            for channel in (2 * pair, 2 * pair + 1):
+                grad, left = grads[channel], i.owned.left[channel]
+                found.append(
+                    product_of(left, grad, 1, 0) if self.incoming else product_of(grad, left, 0, 0)
+                )
+            split_channels(right_low, pair, *found)
+
+        left_moves = [(left_low, o.grad_left, held[7], held[8])]
+        right_moves = [(right_low, o.grad_right, held[9], held[10])]
+        each_pair(left_step)
+        ring.start(left_moves, 0)
+        each_pair(right_step)
+        ring.start(right_moves, 0)
+        ring.wait(left_moves, 0)
+        ring.wait(right_moves, 0)
+
+
+def prepare(triangle_input, triangle_output, expand_weight, reduce_weight, distogram_weight, norm_gains):
+    merged = [
+        triangle_input.reshape((-1,) + triangle_input.shape[2:]),
+        triangle_output.reshape((-1,) + triangle_output.shape[2:]),
+        expand_weight,
+        reduce_weight,
+        distogram_weight[None],
+    ]
+    count = len(merged)
+
+    def kernel(*refs):
+        for source, plain, turned in zip(refs[:count], refs[count + 1 :: 2], refs[count + 2 :: 2]):
+            for index in range(source.shape[0]):
+                value = source[index]
+                plain[index] = value.astype(BF16)
+                turned[index] = value.T.astype(BF16)
+        gains = refs[count][...]
+        refs[-1][...] = gains.T
+
+    shapes = []
+    for array in merged:
+        depth, rows, cols = array.shape
+        shapes.append(jax.ShapeDtypeStruct((depth, rows, cols), BF16))
+        shapes.append(jax.ShapeDtypeStruct((depth, cols, rows), BF16))
+    shapes.append(jax.ShapeDtypeStruct(norm_gains.shape[::-1], F32))
+    return pl.pallas_call(
+        kernel,
+        out_shape=shapes,
+        compiler_params=pltpu.CompilerParams(vmem_limit_bytes=VMEM_BYTES),
+        name="prepare",
+    )(*merged, norm_gains)
+
+
+def by_crop(value, rows_axis, head_axis):
+    count, heads = rows_axis, head_axis
+    half = count // 2
+    inner = half // 2 * heads
+    same, other = [], []
+    for row in range(count):
+        place = row % inner // heads * 2 + row // inner
+        for head in range(heads):
+            source = row * heads + head
+            for crop, pairs in ((head, same), (1 - head, other)):
+                pairs.append((source, (crop * half + place) * heads + row % heads))
+    head = lax.axis_index("head")
+    crop = lax.axis_index("row") // half
+    mine = lax.dynamic_index_in_dim(value, head, 0, keepdims=False)
+    rest = lax.dynamic_index_in_dim(value, 1 - head, 0, keepdims=False)
+    mine = lax.ppermute(mine, ("row", "head"), same)
+    rest = lax.ppermute(rest, ("row", "head"), other)
+    low = jnp.where(crop == 0, mine, rest)
+    high = jnp.where(crop == 0, rest, mine)
+    return jnp.concatenate([low, high], axis=-1)
+
+
+def reduce_rest(half, peers, collective_id, grids, gains, rows):
+    sizes = [grid.shape[0] * grid.shape[1] // LANES for grid in grids]
+    used = sum(sizes) + len(gains) + SUBLANES * len(rows)
+    part = -(-used // (peers * SUBLANES)) * SUBLANES
+    total = part * peers
+    starts, spot = [], 0
+    for size in sizes:
+        starts.append(spot)
+        spot += size
+    row_starts = []
+    for _ in rows:
+        row_starts.append(spot)
+        spot += SUBLANES
+    gain_start = spot
+    count = len(grids) + len(gains) + len(rows)
+
+    def kernel(*refs):
+        out, local, got, mine, other, sends, recvs, back_sends, back_recvs, twin_sems = refs[count:]
+        ring = Exchange(peers, half)
+        ring.greet()
+        barrier = pltpu.get_barrier_semaphore()
+        pl.semaphore_signal(barrier, inc=1, device_id=ring.twin, device_id_type=MESH)
+        for grid, start in zip(refs[: len(grids)], starts):
+            height, width = grid.shape
+            for column in range(width // LANES):
+                local[pl.ds(start + column * height, height), :] = grid[
+                    :, column * LANES : (column + 1) * LANES
+                ]
+        ones = jnp.ones((SUBLANES, LANES), F32)
+        for index, gain in enumerate(refs[len(grids) : len(grids) + len(gains)]):
+            folded = lax.dot_general(
+                ones,
+                gain[...],
+                (((1,), (1,)), ((), ())),
+                precision=lax.Precision.HIGHEST,
+                preferred_element_type=F32,
+            )
+            local[pl.ds(gain_start + index, 1), :] = folded[:1]
+        for row, start in zip(refs[len(grids) + len(gains) : count], row_starts):
+            local[pl.ds(start, 1), :] = row[...]
+            local[pl.ds(start + 1, SUBLANES - 1), :] = jnp.zeros((SUBLANES - 1, LANES), F32)
+        tail = gain_start + len(gains)
+        if total > tail:
+            local[pl.ds(tail, total - tail), :] = jnp.zeros((total - tail, LANES), F32)
+        pl.semaphore_wait(barrier, peers)
+
+        def block(peer):
+            return pl.ds(pl.multiple_of(peer * part, SUBLANES), part)
+
+        here = block(ring.me)
+
+        def gather(step):
+            peer = ring.peer(step)
+            return pltpu.make_async_remote_copy(
+                src_ref=local.at[block(peer), :],
+                dst_ref=got.at[here, :],
+                send_sem=sends.at[step],
+                recv_sem=recvs.at[step],
+                device_id=ring.device(peer),
+                device_id_type=MESH,
+            )
+
+        def spread(step):
+            return pltpu.make_async_remote_copy(
+                src_ref=out.at[here, :],
+                dst_ref=out.at[here, :],
+                send_sem=back_sends.at[step],
+                recv_sem=back_recvs.at[step],
+                device_id=ring.device(ring.peer(step)),
+                device_id_type=MESH,
+            )
+
+        for step in ring.order:
+            gather(step).start()
+        got[here, :] = local[here, :]
+        for step in ring.order:
+            gather(step).wait()
+        value = got[pl.ds(0, part), :]
+        for peer in range(1, peers):
+            value = value + got[pl.ds(peer * part, part), :]
+        mine[...] = value
+        copy = pltpu.make_async_remote_copy(
+            src_ref=mine,
+            dst_ref=other,
+            send_sem=twin_sems.at[0],
+            recv_sem=twin_sems.at[1],
+            device_id=ring.twin,
+            device_id_type=MESH,
+        )
+        copy.start()
+        copy.wait()
+        out[here, :] = mine[...] + other[...]
+        for step in ring.order:
+            spread(step).start()
+        for step in ring.order:
+            spread(step).wait()
+
+    inside = pl.BlockSpec(memory_space=pltpu.VMEM)
+    whole = pl.pallas_call(
+        kernel,
+        in_specs=[inside] * count,
+        out_specs=inside,
+        out_shape=jax.ShapeDtypeStruct((total, LANES), F32),
+        scratch_shapes=[pltpu.VMEM((total, LANES), F32)] * 2
+        + [pltpu.VMEM((part, LANES), F32)] * 2
+        + [pltpu.SemaphoreType.DMA((peers,))] * 4
+        + [pltpu.SemaphoreType.DMA((2,))],
+        compiler_params=pltpu.CompilerParams(
+            collective_id=collective_id, has_side_effects=True, vmem_limit_bytes=VMEM_BYTES
+        ),
+        cost_estimate=pl.CostEstimate(flops=10**10, bytes_accessed=10**6, transcendentals=0),
+        name="reduce_rest",
+    )(*grids, *gains, *rows)
+    return whole, starts, row_starts, gain_start
+
+
+def update(rest, starts, row_starts, gain_start, early, weights, firsts, seconds):
+    layers, kinds, width, mixed = weights[2].shape
+    hidden = weights[4].shape[2]
+    early_in, early_up, early_rows = early
+    given = [rest, *early_in, *early_up, early_rows]
+    count = len(given)
+
+    def kernel(*refs):
+        whole = refs[0]
+        in_refs = refs[1 : 1 + len(early_in)]
+        up_refs = refs[1 + len(early_in) : count - 1]
+        rows_ref = refs[count - 1]
+        states = [refs[count + 8 * kind : count + 8 * (kind + 1)] for kind in range(3)]
+        scalars = refs[count + 24 : count + 27]
+        results = refs[count + 27 :]
+
+        def taken(start, size):
+            return whole[pl.ds(start, size), :]
+
+        def wide(start, height, columns):
+            return jnp.concatenate(
+                [taken(start + column * height, height) for column in range(columns)], axis=1
+            )
+
+        loss = jnp.sum(taken(row_starts[0], 1), axis=1, keepdims=True)
+        valid = jnp.sum(taken(row_starts[1], 1), axis=1, keepdims=True)
+        table_rows, single_rows = weights[0].shape[0], weights[1].shape[0]
+        outs, downs = layers * kinds - 1, hidden // 2
+        grads = {}
+        grads[0, ()] = taken(starts[4], table_rows)
+        grads[1, ()] = jnp.concatenate(
+            [taken(starts[5], single_rows), taken(starts[6], single_rows)], axis=1
+        )
+        spot = 0
+        for layer in range(layers):
+            for kind in range(kinds):
+                if layer == 0:
+                    grads[2, (layer, kind)] = wide(starts[kind], width, mixed // LANES)
+                else:
+                    grads[2, (layer, kind)] = in_refs[(layer - 1) * kinds + kind][...]
+                if layer == 0 and kind == 0:
+                    grads[3, (layer, kind)] = taken(starts[2], width)
+                else:
+                    grads[3, (layer, kind)] = rows_ref[pl.ds(spot, width), :]
+                    spot += width
+        for layer in range(layers):
+            grads[4, (layer,)] = up_refs[layer][...]
+            grads[5, (layer,)] = rows_ref[pl.ds(spot, downs), :]
+            spot += downs
+        grads[6, ()] = taken(starts[3], weights[6].shape[1]).T
+        grads[7, ()] = taken(gain_start, weights[7].shape[0])
+        squares = jnp.zeros((1, 1), F32)
+        for key in grads:
+            grads[key] = grads[key] / valid
+            squares = squares + jnp.sum(grads[key] * grads[key], axis=(0, 1), keepdims=True)
+        norm = jnp.sqrt(squares)
+        factor = jnp.minimum(1.0, CLIP_NORM / (norm + 1e-06))
+        for ref, value in zip(scalars, (loss, valid, norm)):
+            ref[...] = value
+        for (index, spot), grad in grads.items():
+            rate = GAIN_RATE if index == 7 else WEIGHT_RATE
+            decay = 0.0 if index == 7 else WEIGHT_DECAY
+            new = adamw(
+                states[0][index][spot],
+                grad * factor,
+                states[1][index][spot],
+                states[2][index][spot],
+                rate,
+                decay,
+            )
+            for ref, value in zip(results[3 * index : 3 * index + 3], new):
+                ref[spot] = value
+
+    one = jax.ShapeDtypeStruct((1, 1), F32)
+    shapes = [one] * 3
+    for weight in weights:
+        shapes += [jax.ShapeDtypeStruct(weight.shape, F32)] * 3
+    found = pl.pallas_call(
+        kernel,
+        out_shape=shapes,
+        compiler_params=pltpu.CompilerParams(vmem_limit_bytes=VMEM_BYTES),
+        name="update",
+    )(*given, *weights, *firsts, *seconds)
+    return tuple(value[0, 0] for value in found[:3]) + tuple(found[3:])
+
+
+def step_by_crop(row_count, head_count, given, weights, firsts, seconds):
+    single, residue_index, chain_index, token_mask, pair_valid, target_bins = given
+    relative_table, single_weight, triangle_input, triangle_output = weights[:4]
+    expand_weight, reduce_weight, distogram_weight, norm_gains = weights[4:]
+    crops, tokens = token_mask.shape
+    width = relative_table.shape[1]
+    layers = triangle_input.shape[0]
+    half = row_count // crops
+    peers = half * head_count
+    rows = tokens // peers
+    row_index = lax.axis_index("row")
+    crop = row_index // half
+    start = position(row_index % half, lax.axis_index("head"), half, head_count) * rows
+
+    placed = by_crop(jnp.stack([pair_valid, target_bins], axis=1), row_count, head_count)
+    valid, target = placed[0], placed[1]
+
+    def of_crop(array):
+        return lax.dynamic_index_in_dim(array, crop, 0, keepdims=False)
+
+    def of_rows(array):
+        return lax.dynamic_slice_in_dim(array, start, rows, 0)
+
+    residues, chains = of_crop(residue_index), of_crop(chain_index)
+    reach = (relative_table.shape[0] - 2) // 2
+    bins = jnp.where(
+        of_rows(chains)[:, None] == chains[None, :],
+        jnp.clip(of_rows(residues)[:, None] - residues[None, :], -reach, reach) + reach,
+        2 * reach + 1,
+    )
+    present = of_crop(token_mask).astype(F32)
+    pair_mask = of_rows(present)[:, None] * present[None, :]
+    loss_weight = pair_mask * valid.astype(F32)
+    table_rows = -(-relative_table.shape[0] // PACKED) * PACKED
+    table_t = jnp.pad(relative_table, ((0, table_rows - relative_table.shape[0]), (0, 0))).T
+    tokens_single = of_crop(single)
+    proj = project(tokens_single, single_weight.astype(BF16))
+    proj_rows = of_rows(proj[:, :width])[:, :, None]
+    proj_cols = proj[:, width:].T
+    bins, pair_mask = Arg(bins[:, None, :], ROWS), Arg(pair_mask[:, None, :], ROWS)
+
+    prepared = prepare(
+        triangle_input, triangle_output, expand_weight, reduce_weight, distogram_weight, norm_gains
+    )
+    mix, mix_t, out, out_t, up, up_t, down, down_t, logits, logits_t, gains = prepared
+    hidden = up.shape[2]
+
+    def gain(index):
+        return Arg(gains, WHOLE, column=index)
+
+    def layer_of(array, index, *block):
+        shape = block or array.shape[1:]
+        return Arg(array, WHOLE, (index, 0, 0), (None,) + tuple(shape))
+
+    def triangle_weights(layer, kind, starts=False, finishes=False, back=False):
+        index = 2 * layer + kind
+        found = dict(gain0=gain(5 * layer + 2 * kind))
+        if starts:
+            found.update(mix_t=layer_of(mix_t, index, 4 * width, width))
+        if starts and back:
+            found.update(mix=layer_of(mix, index))
+        if finishes:
+            found.update(
+                gain1=gain(5 * layer + 2 * kind + 1),
+                gate_t=Arg(mix_t, WHOLE, (index, 4, 0), (None, width, width)),
+                out_t=layer_of(out_t, index),
+            )
+        if finishes and back:
+            found.update(out=layer_of(out, index))
+        return found
+
+    def transition_weights(layer, forth=True, back=False):
+        found = dict(gain=gain(5 * layer + 4), up_t=layer_of(up_t, layer))
+        if forth:
+            found.update(down_t=layer_of(down_t, layer))
+        if back:
+            found.update(up=layer_of(up, layer), down=layer_of(down, layer))
+        return found
+
+    def state_out():
+        return Out((rows, width, tokens), F32, ROWS)
+
+    def sum_out(*shape):
+        return Out(shape, F32, SUM)
+
+    def gain_out():
+        return sum_out(width, LANES)
+
+    def back_start_outs():
+        return dict(
+            grad_gate=Out((rows, width, tokens), BF16, ROWS),
+            out=sum_out(width, width),
+            gain1=gain_out(),
+        )
+
+    def back_finish_outs():
+        return dict(mix=sum_out(width, 5 * width), gain0=gain_out())
+
+    def transition_outs():
+        return dict(up=sum_out(width, hidden), down=sum_out(hidden // 2, width), gain=gain_out())
+
+    identities = iter(range(4 * layers))
+
+    def forward(incoming):
+        return Forward(peers, half, rows, tokens, incoming, next(identities))
+
+    def backward(incoming):
+        return Backward(peers, half, rows, tokens, incoming, next(identities))
+
+    def owned(kept):
+        return dict(left=Arg(kept.left, WHOLE), right=Arg(kept.right, WHOLE))
+
+    kept, states, middles, sums = {}, {}, {}, {}
+
+    def first_body(i, o, left, right):
+        state = dot(i.table_t[...], bins_hot(i.bins, table_rows))
+        cols = i.proj_cols[...]
+        state = state + jnp.concatenate(
+            [cols + i.proj_rows[row] for row in range(ROW_BLOCK)], axis=1
+        )
+        write_rows(o.state, state)
+        triangle_start(i.start, read_rows(i.mask), left, right, state)
+
+    exchange = forward(False)
+    got = run_stage(
+        first_body,
+        "first_state",
+        rows,
+        dict(
+            bins=bins,
+            proj_rows=Arg(proj_rows, ROWS),
+            proj_cols=Arg(proj_cols, WHOLE),
+            table_t=Arg(table_t.astype(BF16), WHOLE),
+            mask=pair_mask,
+            start=triangle_weights(0, 0, starts=True),
+        ),
+        dict(state=state_out(), **exchange.outs()),
+        exchange,
+    )
+    kept[0, 0], states[0, 0] = got, got.state
+
+    def between_body(i, o, left, right):
+        state, _ = triangle_finish(i.end, i.tri, read_rows(i.state))
+        write_rows(o.state, state)
+        triangle_start(i.start, read_rows(i.mask), left, right, state)
+
+    def layer_end_body(i, o, left, right):
+        state, _ = triangle_finish(i.end, i.tri, read_rows(i.state))
+        write_rows(o.middle, state)
+        state = transition_finish(i.lift, state, transition(i.lift, state))
+        write_rows(o.state, state)
+        triangle_start(i.start, read_rows(i.mask), left, right, state)
+
+    for layer in range(layers):
+        exchange = forward(True)
+        got = run_stage(
+            between_body,
+            "between_updates",
+            rows,
+            dict(
+                state=Arg(states[layer, 0], ROWS),
+                tri=Arg(kept[layer, 0].tri, WIRE),
+                mask=pair_mask,
+                end=triangle_weights(layer, 0, finishes=True),
+                start=triangle_weights(layer, 1, starts=True),
+            ),
+            dict(state=state_out(), **exchange.outs()),
+            exchange,
+        )
+        kept[layer, 1], states[layer, 1] = got, got.state
+        if layer + 1 == layers:
+            break
+        exchange = forward(False)
+        got = run_stage(
+            layer_end_body,
+            "layer_end",
+            rows,
+            dict(
+                state=Arg(states[layer, 1], ROWS),
+                tri=Arg(kept[layer, 1].tri, WIRE),
+                mask=pair_mask,
+                end=triangle_weights(layer, 1, finishes=True),
+                lift=transition_weights(layer),
+                start=triangle_weights(layer + 1, 0, starts=True),
+            ),
+            dict(middle=state_out(), state=state_out(), **exchange.outs()),
+            exchange,
+        )
+        kept[layer + 1, 0], states[layer + 1, 0] = got, got.state
+        middles[layer] = got.middle
+
+    def loss_body(i, o, wire):
+        state, kept_triangle = triangle_finish(i.end, i.tri, read_rows(i.state))
+        lifted = transition(i.lift, state)
+        grad = head_back(i.head, o.head, transition_finish(i.lift, state, lifted))
+        grad = transition_back(i.lift, o.lift, grad, lifted)
+        write_rows(o.grad, grad)
+        triangle_back_start(i.end, o.end, wire, grad, kept_triangle)
+
+    top = layers - 1
+    exchange = backward(True)
+    got = run_stage(
+        loss_body,
+        "loss",
+        rows,
+        dict(
+            state=Arg(states[top, 1], ROWS),
+            tri=Arg(kept[top, 1].tri, WIRE),
+            end=triangle_weights(top, 1, finishes=True, back=True),
+            lift=transition_weights(top, back=True),
+            head=dict(
+                gain=gain(5 * layers),
+                logits=layer_of(logits, 0),
+                logits_t=layer_of(logits_t, 0),
+                target=Arg(target[:, None, :], ROWS),
+                weight=Arg(loss_weight[:, None, :], ROWS),
+            ),
+            owned=owned(kept[top, 1]),
+        ),
+        dict(
+            grad=state_out(),
+            head=dict(
+                loss=sum_out(1, LANES),
+                count=sum_out(1, LANES),
+                logits=sum_out(distogram_weight.shape[1], width),
+                gain=gain_out(),
+            ),
+            lift=transition_outs(),
+            end=back_start_outs(),
+            **exchange.outs(),
+        ),
+        exchange,
+    )
+    head, lifts, ends, begins = got.head, {top: got.lift}, {(top, 1): got.end}, {}
+
+    def between_back_body(i, o, wire):
+        grad = triangle_back_finish(
+            i.start, i.back, o.start, read_rows(i.mask), read_rows(i.grad), read_rows(i.state)
+        )
+        write_rows(o.grad, grad)
+        _, kept_triangle = triangle_finish(i.end, i.tri, read_rows(i.before))
+        triangle_back_start(i.end, o.end, wire, grad, kept_triangle)
+
+    def layer_end_back_body(i, o, wire):
+        grad = triangle_back_finish(
+            i.start, i.back, o.start, read_rows(i.mask), read_rows(i.grad), read_rows(i.state)
+        )
+        grad = transition_back(i.lift, o.lift, grad, transition(i.lift, read_rows(i.middle)))
+        write_rows(o.grad, grad)
+        _, kept_triangle = triangle_finish(i.end, i.tri, read_rows(i.before))
+        triangle_back_start(i.end, o.end, wire, grad, kept_triangle)
+
+    def first_back_body(i, o):
+        grad = triangle_back_finish(
+            i.start, i.back, o.start, read_rows(i.mask), read_rows(i.grad), read_rows(i.state)
+        )
+        hot = bins_hot(i.bins, table_rows)
+        high = grad.astype(BF16)
+        low = (grad - high.astype(F32)).astype(BF16)
+        o.table[...] += dot_pairs(hot, high) + dot_pairs(hot, low)
+        for row in range(ROW_BLOCK):
+            part = grad[:, row * tokens : (row + 1) * tokens]
+            o.rows[row] = fold(part)
+            o.cols[...] += part
+
+    for layer in reversed(range(layers)):
+        for kind in (1, 0):
+            inputs = dict(
+                grad=Arg(got.grad, ROWS),
+                state=Arg(states[layer, kind], ROWS),
+                mask=pair_mask,
+                start=triangle_weights(layer, kind, starts=True, back=True),
+                back=dict(
+                    grad_left=Arg(got.grad_left, WIRE),
+                    grad_right=Arg(got.grad_right, WIRE),
+                    grad_gate=Arg(got.end.grad_gate, ROWS),
+                ),
+            )
+            outputs = dict(start=back_finish_outs())
+            if layer == 0 and kind == 0:
+                got = run_stage(
+                    first_back_body,
+                    "first_state_back",
+                    rows,
+                    dict(bins=bins, **inputs),
+                    dict(
+                        table=sum_out(table_rows, width),
+                        rows=Out((rows, width, LANES), F32, ROWS),
+                        cols=sum_out(width, tokens),
+                        **outputs,
+                    ),
+                )
+                begins[layer, kind] = got.start
+                break
+            before = (layer, 0) if kind == 1 else (layer - 1, 1)
+            inputs.update(
+                before=Arg(states[before], ROWS),
+                tri=Arg(kept[before].tri, WIRE),
+                end=triangle_weights(*before, finishes=True, back=True),
+                owned=owned(kept[before]),
+            )
+            outputs.update(grad=state_out(), end=back_start_outs())
+            if kind == 1:
+                exchange = backward(False)
+                body, name = between_back_body, "between_updates_back"
+            else:
+                exchange = backward(True)
+                body, name = layer_end_back_body, "layer_end_back"
+                inputs.update(
+                    middle=Arg(middles[layer - 1], ROWS),
+                    lift=transition_weights(layer - 1, forth=False, back=True),
+                )
+                outputs.update(lift=transition_outs())
+            got = run_stage(body, name, rows, inputs, dict(**outputs, **exchange.outs()), exchange)
+            begins[layer, kind], ends[before] = got.start, got.end
+            if kind == 0:
+                lifts[layer - 1] = got.lift
+
+    early = (
+        [begins[layer, kind].mix for layer in range(1, layers) for kind in range(2)],
+        [lifts[layer].up for layer in range(layers)],
+        jnp.concatenate(
+            [
+                ends[layer, kind].out
+                for layer in range(layers)
+                for kind in range(2)
+                if (layer, kind) != (0, 0)
+            ]
+            + [lifts[layer].down for layer in range(layers)],
+            axis=0,
+        ),
+    )
+    early = lax.psum(early, ("row", "head"))
+
+    wide_single = tokens_single.astype(F32)
+    row_part = jnp.einsum(
+        "is,ic->sc",
+        of_rows(wide_single),
+        jnp.sum(got.rows, axis=2),
+        precision=lax.Precision.HIGHEST,
+    )
+    col_part = jnp.einsum("js,cj->sc", wide_single, got.cols, precision=lax.Precision.HIGHEST)
+    partial_gains = []
+    for layer in range(layers):
+        for kind in range(2):
+            partial_gains += [begins[layer, kind].gain0, ends[layer, kind].gain1]
+        partial_gains.append(lifts[layer].gain)
+    partial_gains.append(head.gain)
+    grids = [
+        begins[0, 0].mix,
+        begins[0, 1].mix,
+        ends[0, 0].out,
+        head.logits,
+        got.table,
+        row_part,
+        col_part,
+    ]
+    rest, *starts = reduce_rest(
+        half, peers, 4 * layers, grids, partial_gains, [head.loss, head.count]
+    )
+    return update(rest, *starts, early, weights, firsts, seconds)
+
+
 def per_device(
+    row_count,
+    head_count,
     single,
     residue_index,
     chain_index,
@@ -280,132 +1656,25 @@
     first_gains,
     second_gains,
 ):
-    crops, rows, cols = pair_valid.shape
+    crops, tokens = token_mask.shape
     width = relative_table.shape[1]
-    layers = triangle_input.shape[0]
-    row_start = lax.axis_index("row") * rows
-    col_start = lax.axis_index("head") * cols
-
-    def take(array, start, count):
-        return lax.dynamic_slice_in_dim(array, start, count, 1)
-
-    offset = (
-        take(residue_index, row_start, rows)[:, :, None]
-        - take(residue_index, col_start, cols)[:, None, :]
-    )
-    same = (
-        take(chain_index, row_start, rows)[:, :, None]
-        == take(chain_index, col_start, cols)[:, None, :]
-    )
-    reach = (relative_table.shape[0] - 2) // 2
-    bins = jnp.where(same, jnp.clip(offset, -reach, reach) + reach, 2 * reach + 1)
-    relative_hot = (
-        bins[..., None] == jnp.arange(relative_table.shape[0])[None, None, None, :]
-    ).astype(jnp.float32)
-    token_rows = take(token_mask, row_start, rows).astype(jnp.float32)
-    token_cols = take(token_mask, col_start, cols).astype(jnp.float32)
-    pair_mask = token_rows[:, :, None] * token_cols[:, None, :]
-    loss_weight = pair_mask * pair_valid.astype(jnp.float32)
-    low_input = triangle_input.astype(jnp.bfloat16)
-    low_output = triangle_output.astype(jnp.bfloat16)
-    low_expand = expand_weight.astype(jnp.bfloat16)
-    low_reduce = reduce_weight.astype(jnp.bfloat16)
-    low_logits = distogram_weight.astype(jnp.bfloat16)
-    proj = project(single, single_weight.astype(jnp.bfloat16))
-    state = project(relative_hot.astype(jnp.bfloat16), relative_table.astype(jnp.bfloat16))
-    state = (
-        state
-        + take(proj, row_start, rows)[:, :, None, :width]
-        + take(proj, col_start, cols)[:, None, :, width:]
-    )
-    inputs = []
-    for layer in range(layers):
-        inputs.append(state)
-        state, unused = block_forward(
-            state,
-            low_input[layer],
-            low_output[layer],
-            low_expand[layer],
-            low_reduce[layer],
-            norm_gains[5 * layer : 5 * layer + 5],
-            pair_mask,
-        )
-    head_unit, head_scale = normalize(state)
-    shown = (head_unit * norm_gains[5 * layers]).astype(jnp.bfloat16)
-    logits = project(shown, low_logits)
-    largest = jnp.max(logits, axis=-1, keepdims=True)
-    log_total = largest + jnp.log(jnp.sum(jnp.exp(logits - largest), axis=-1, keepdims=True))
-    target_hot = (
-        target_bins[..., None] == jnp.arange(logits.shape[-1])[None, None, None, :]
-    ).astype(jnp.float32)
-    picked = jnp.sum(logits * target_hot, axis=-1)
-    loss_local = jnp.sum(loss_weight * (log_total[..., 0] - picked))
-    grad_scores = (loss_weight[..., None] * (jnp.exp(logits - log_total) - target_hot)).astype(
-        jnp.bfloat16
-    )
-    grad_logits = weight_grad(shown, grad_scores)
-    grad_shown = project_back(grad_scores, low_logits)
-    grad_state, gain_last = norm_back(grad_shown, head_unit, head_scale, norm_gains[5 * layers])
-    collected = []
-    for layer in reversed(range(layers)):
-        grad_state, layer_grads = block_backward(
-            grad_state,
-            inputs[layer],
-            low_input[layer],
-            low_output[layer],
-            low_expand[layer],
-            low_reduce[layer],
-            norm_gains[5 * layer : 5 * layer + 5],
-            pair_mask,
-        )
-        collected.insert(0, layer_grads)
-    grad_input = jnp.stack([entry[0] for entry in collected])
-    grad_output = jnp.stack([entry[1] for entry in collected])
-    grad_expand = jnp.stack([entry[2] for entry in collected])
-    grad_reduce = jnp.stack([entry[3] for entry in collected])
-    grad_gains = jnp.concatenate(
-        [jnp.concatenate([entry[4] for entry in collected], axis=0), gain_last[None]], axis=0
-    )
-    grad_table = jnp.einsum(
-        "bijr,bijc->rc", relative_hot, grad_state, precision=lax.Precision.HIGHEST
-    )
-    single_wide = single.astype(jnp.float32)
-    row_part = jnp.einsum(
-        "bis,bic->sc",
-        take(single_wide, row_start, rows),
-        jnp.sum(grad_state, axis=2),
-        precision=lax.Precision.HIGHEST,
-    )
-    col_part = jnp.einsum(
-        "bjs,bjc->sc",
-        take(single_wide, col_start, cols),
-        jnp.sum(grad_state, axis=1),
-        precision=lax.Precision.HIGHEST,
-    )
-    grad_single = jnp.concatenate([row_part, col_part], axis=1)
-    local_count = jnp.sum(loss_weight)
-    valid_count = lax.psum(local_count, ("row", "head"))
-    summed = lax.psum(
-        (
-            grad_table / valid_count,
-            grad_single / valid_count,
-            grad_input / valid_count,
-            grad_output / valid_count,
-            grad_expand / valid_count,
-            grad_reduce / valid_count,
-            grad_logits / valid_count,
-            grad_gains / valid_count,
-            loss_local,
-        ),
-        ("row", "head"),
-    )
-    grads = list(summed[:8])
-    loss_sum = summed[8]
-    squares = jnp.zeros((), jnp.float32)
-    for g in grads:
-        squares = squares + jnp.sum(g * g)
-    gradient_norm = jnp.sqrt(squares)
-    factor = jnp.minimum(1.0, CLIP_NORM / (gradient_norm + 1e-06))
+    peers = row_count * head_count // crops
+    given = (
+        single,
+        residue_index,
+        chain_index,
+        token_mask,
+        pair_valid,
+        target_bins,
+        relative_table,
+        single_weight,
+        triangle_input,
+        triangle_output,
+        expand_weight,
+        reduce_weight,
+        distogram_weight,
+        norm_gains,
+    )
     weights = (
         relative_table,
         single_weight,
@@ -436,6 +1705,24 @@
         second_logits,
         second_gains,
     )
+    if (
+        crops == 2
+        and head_count == 2
+        and width == LANES
+        and width == SUBLANES * peers
+        and tokens % (peers * SUBLANES) == 0
+        and tokens % (3 * LANES) == 0
+    ):
+        return step_by_crop(row_count, head_count, given[:6], weights, firsts, seconds)
+    local = gradients_by_block(*given)
+    summed = lax.psum(local, ("row", "head"))
+    loss_sum, valid_count = summed[0], summed[1]
+    grads = [grad / valid_count for grad in summed[2:]]
+    squares = jnp.zeros((), jnp.float32)
+    for g in grads:
+        squares = squares + jnp.sum(g * g)
+    gradient_norm = jnp.sqrt(squares)
+    factor = jnp.minimum(1.0, CLIP_NORM / (gradient_norm + 1e-06))
     result = []
     for index in range(8):
         rate = GAIN_RATE if index == 7 else WEIGHT_RATE
@@ -508,7 +1795,7 @@
         P(),
     )
     return jax.shard_map(
-        per_device,
+        functools.partial(per_device, mesh.shape["row"], mesh.shape["head"]),
         mesh=mesh,
         in_specs=placed,
         out_specs=(

time: 4850 us -> 1050 us (0.22)
  waiting for transfers between devices: 1610 us -> 91.9 us
  blocking collectives: 1080 us -> 0 us
  local copies, waits for them, and re-layouts: 1050 us -> 15.5 us
  Pallas kernels: 0 us -> 911 us
  matrix products: 623 us -> 3.39 us
  other arithmetic: 378 us -> 5.13 us
  starting transfers between devices: 58.8 us -> 6.05 us
    all_to_all x18 -> x0, blocking collectives: 995 us -> none  [the longest x2 212 us: triangle_backward(): lax.all_to_all(jnp.swapaxes(grad_left, 1, 2), 'row', split_axis=1, concat...]
    reduce_scatter x4 -> x0, waiting for transfers between devices: 929 us -> none  [triangle_backward(): lax.psum_scatter(jnp.einsum('bijc,bikc->jbkc', tri_cols, left_cols, prefe...]
    pallas_call x0 -> x12, Pallas kernels: none -> 911 us  [the longest x9 837 us: run_stage(): pl.pallas_call(kernel, grid=(steps,), in_specs=[arg.spec() for arg in arg...]
    convert_element_type x56 -> x1, local copies, waits for them, and re-layouts: 519 us -> 0.63 us  [step_by_crop(): table_t.astype(BF16)]
    dot_general x41 -> x2, matrix products: 513 us -> 2.14 us  [the longest x1 1.16 us: step_by_crop(): jnp.einsum('js,cj->sc', wide_single, got.cols, precision=lax.Precision.HI...]
    all_gather x4 -> x0, waiting for transfers between devices: 386 us -> none  [triangle_forward(): right_all = lax.all_gather(right_cols, 'row', axis=1, tiled=True)]
    unnamed x510 -> x35, local copies, waits for them, and re-layouts: 273 us -> 12.1 us
    all_to_all x40 -> x0, local copies, waits for them, and re-layouts: 252 us -> none  [the longest x8 55.7 us: triangle_backward(): lax.all_to_all(grad_tri.astype(jnp.bfloat16), 'head', split_axis=3, conca...]
  transfers between devices with their start and end apart: 23 -> 3, of which waited for: 21 -> 1; matrix products, arithmetic and copies ran while one was open for 12% -> 1% of each run, Pallas kernels for 0% -> 6%
where the time goes in v3:
time: 1050 us
  Pallas kernels  911 us (87%)
  waiting for transfers between devices  91.9 us (9%)
  local copies, waits for them, and re-layouts  15.5 us (1%)
  between operations  14.6 us (1%)
    pallas_call x9, Pallas kernels, run_stage(): pl.pallas_call(kernel, grid=(steps,), in_specs=[arg.spec() for arg in arg...  837 us
    psum x1, waiting for transfers between devices, step_by_crop(): early = lax.psum(early, ('row', 'head'))  91.9 us
    pallas_call x1, Pallas kernels, reduce_rest(): pl.pallas_call(kernel, in_specs=[inside] * count, out_specs=inside, out_s...  57.3 us
  transfers between devices with their start and end apart: 3, of which 1 were waited for; matrix products, arithmetic and copies ran while one was open for 1% of the time, Pallas kernels for 6%

profile of v3, /device:TPU:0, one launch (start us, length us, event | category | flops | bytes accessed | tf_op | source)
XLA Modules:
  0.0 1047.4 jit_solution(14637835832393644396)
XLA Ops:
  7.3 0.9 fusion.8
  9.0 5.4 collective-permute-start.1
  14.3 1.2 fusion.2
  16.6 0.8 compare_select_fusion.refs_0_
  17.5 1.7 copy.83.refs_1_
  19.2 0.8 copy.92
  20.0 0.7 copy.82.refs_12_
  21.4 0.7 copy.88.refs_28_
  22.2 3.8 prepare.1
  26.0 0.7 fusion.13.refs_15_
  26.8 0.8 fusion.12
  27.5 92.6 %first_state.1 = (f32[24,128,384]{2,1,0:T(8,128)}, bf16[8,384,384]{2,1,0:T(8,128)(2,1)}, bf16[8,384,384]{2,1,0:T(8,128)(2,1)}, bf16[16,192,384]{2,1,0:T(8,128)(2,1)}) custom-call(s32[24,1,384]{2,1,0:T(1,128)} %compare_select_fusion.refs_0_, f32[24,128,1]{2,1,0:T(8,128)} %copy.83.refs_1_, f32[128,384]{1,0:T(8,128)} %bitcast.52, ...), custom_call_target="tpu_custom_call" | custom-call | flops 99999997952 | bytes 1000000 | tf_op jit(solution)/shard_map/first_state/pallas_call | solution.py:747
  120.2 92.9 %between_updates.2 = (f32[24,128,384]{2,1,0:T(8,128)}, bf16[8,384,384]{2,1,0:T(8,128)(2,1)}, bf16[8,384,384]{2,1,0:T(8,128)(2,1)}, bf16[16,192,384]{2,1,0:T(8,128)(2,1)}) custom-call(f32[24,128,384]{2,1,0:T(8,128)} %get-tuple-element.129.refs_0_.refs_9_.refs_2_, bf16[16,192,384]{2,1,0:T(8,128)(2,1)} %get-tuple-element.130.refs_1_.refs_10_, ...), custom_call_target="tpu_custom_call" | custom-call | flops 99999997952 | bytes 1000000 | tf_op jit(solution)/shard_map/between_updates/pallas_call | solution.py:747
  213.1 97.2 %layer_end.1 = (f32[24,128,384]{2,1,0:T(8,128)}, f32[24,128,384]{2,1,0:T(8,128)}, bf16[8,384,384]{2,1,0:T(8,128)(2,1)}, bf16[8,384,384]{2,1,0:T(8,128)(2,1)}, bf16[16,192,384]{2,1,0:T(8,128)(2,1)}) custom-call(f32[24,128,384]{2,1,0:T(8,128)} %get-tuple-element.132.refs_0_.refs_9_.refs_1_, bf16[16,192,384]{2,1,0:T(8,128)(2,1)} %get-tuple-element.133.refs_1_.refs_10_, ...), custom_call_target="tpu_custom_call" | custom-call | flops 99999997952 | bytes 1000000 | tf_op jit(solution)/shard_map/layer_end/pallas_call | solution.py:747
  310.3 96.1 %between_updates.3 = (f32[24,128,384]{2,1,0:T(8,128)}, bf16[8,384,384]{2,1,0:T(8,128)(2,1)}, bf16[8,384,384]{2,1,0:T(8,128)(2,1)}, bf16[16,192,384]{2,1,0:T(8,128)(2,1)}) custom-call(f32[24,128,384]{2,1,0:T(8,128)} %get-tuple-element.136.refs_0_.refs_9_.refs_1_, bf16[16,192,384]{2,1,0:T(8,128)(2,1)} %get-tuple-element.137.refs_1_.refs_10_, ...), custom_call_target="tpu_custom_call" | custom-call | flops 99999997952 | bytes 1000000 | tf_op jit(solution)/shard_map/between_updates/pallas_call | solution.py:747
  406.3 120.1 %loss.1 = (f32[24,128,384]{2,1,0:T(8,128)}, f32[1,128]{1,0:T(1,128)}, f32[1,128]{1,0:T(1,128)}, f32[64,128]{1,0:T(8,128)}, f32[128,128]{1,0:T(8,128)}, /*index=5...) custom-call(f32[24,128,384]{2,1,0:T(8,128)} %get-tuple-element.138.r, ...), custom_call_target="tpu_custom_call" | custom-call | flops 99999997952 | bytes 1000000 | tf_op jit(solution)/shard_map/loss/pallas_call | solution.py:747
  526.4 98.7 %between_updates_back.2 = (f32[128,640]{1,0:T(8,128)}, f32[128,128]{1,0:T(8,128)}, f32[24,128,384]{2,1,0:T(8,128)}, bf16[24,128,384]{2,1,0:T(8,128)(2,1)}, f32[1...) custom-call(f32[24,128,384]{2,1,0:T(8,128)} %get-tuple-element.147.refs_0_, ...), custom_call_target="tpu_custom_call" | custom-call | flops 99999997952 | bytes 1000000 | tf_op jit(solution)/shard_map/between_updates_back/pallas_call | solution.py:747
  625.2 120.1 %layer_end_back.1 = (f32[128,640]{1,0:T(8,128)}, f32[128,128]{1,0:T(8,128)}, f32[24,128,384]{2,1,0:T(8,128)}, bf16[24,128,384]{2,1,0:T(8,128)(2,1)}, f32[128,128...) custom-call(f32[24,128,384]{2,1,0:T(8,128)} %get-tuple-element.154.r, ...), custom_call_target="tpu_custom_call" | custom-call | flops 99999997952 | bytes 1000000 | tf_op jit(solution)/shard_map/layer_end_back/pallas_call | solution.py:747
  745.3 1.5 constant_dynamic-update-slice_fusion.4
  748.0 1.7 constant_dynamic-update-slice_fusion.1
  749.7 0.7 constant_dynamic-update-slice_fusion
  750.4 98.7 %between_updates_back.3 = (f32[128,640]{1,0:T(8,128)}, f32[128,128]{1,0:T(8,128)}, f32[24,128,384]{2,1,0:T(8,128)}, bf16[24,128,384]{2,1,0:T(8,128)(2,1)}, f32[1...) custom-call(f32[24,128,384]{2,1,0:T(8,128)} %get-tuple-element.161.refs_0_, ...), custom_call_target="tpu_custom_call" | custom-call | flops 99999997952 | bytes 1000000 | tf_op jit(solution)/shard_map/between_updates_back/pallas_call | solution.py:747
  849.1 20.8 %first_state_back.1 = (f32[80,128]{1,0:T(8,128)}, f32[24,128,128]{2,1,0:T(8,128)}, f32[128,384]{1,0:T(8,128)}, f32[128,640]{1,0:T(8,128)}, f32[128,128]{1,0:T(8,128)}) custom-call(s32[24,1,384]{2,1,0:T(1,128)} %compare_select_fusion.refs_0_, f32[24,128,384]{2,1,0:T(8,128)} %get-tuple-element.167.refs_1_, ...), custom_call_target="tpu_custom_call" | custom-call | flops 99999997952 | bytes 1000000 | tf_op jit(solution)/shard_map/first_state_back/pallas_call | solution.py:747
  870.0 1.9 reduce_sum.9
  872.0 1.0 fusion.14.refs_5_
  873.0 1.2 fusion.refs_6_
  874.1 57.3 %reduce_rest.1.refs_0_ = f32[2432,128]{1,0:T(8,128)} custom-call(f32[128,640]{1,0:T(8,128)} %get-tuple-element.171.refs_0_, f32[128,640]{1,0:T(8,128)} %get-tuple-element.172.refs_1_, f32[128,128]{1,0:T(8,128)} %get-tuple-element.173.refs_2_, f32[64,128]{1,0:T(8,128)} %get-tuple-element.174.refs_3_, f32[80,128]{1,0:T(8,128)} %get-tuple-element.175.refs_4_, ...), custom_call_target="tpu_custom_call" | custom-call | flops 10000000000 | bytes 1000000 | tf_op jit(solution)/shard_map/reduce_rest/pallas_call | solution.py:1158
  931.4 91.9 %all-reduce.4.cloned.1.call-done = (f32[128,640]{1,0:T(8,128)}, f32[128,640]{1,0:T(8,128)}, f32[128,1024]{1,0:T(8,128)}, f32[128,1024]{1,0:T(8,128)}, f32[1408,128]{1,0:T(8,128)}) async-done(((f32[128,640]{1,0:T(8,128)}, f32[128,640]{1,0:T(8,128)}, f32[128,1024]{1,0:T(8,128)}, f32[128,1024]{1,0:T(8,128)}, f32[1408,128]{1,0:T(8,128)}), (f32[128,640]{1,0:T(8,128)}, f32[128,640]{1,0:T(8,128)}, ...) | async-done | bytes 2424848 | tf_op jit(solution)/shard_map/psum | solution.py:1594
  1023.3 12.5 %update.1 = (f32[1,1]{1,0:T(1,128)}, f32[1,1]{1,0:T(1,128)}, f32[1,1]{1,0:T(1,128)}, f32[66,128]{1,0:T(8,128)}, f32[66,128]{1,0:T(8,128)}, /*index=5*/f32[66,128...) custom-call(f32[2432,128]{1,0:T(8,128)} %reduce_rest.1.refs_0_, ...), custom_call_target="tpu_custom_call" | custom-call | tf_op jit(solution)/shard_map/update/pallas_call | solution.py:1253
  1035.7 1.5 copy.89
  1037.3 1.5 copy.90
  1038.8 1.5 copy.91
  (44 shorter events, 3.8 us)
Async XLA Ops:
  7.2 7.1 copy-start
  7.2 8.4 copy-start.11
  7.2 8.5 copy-start.3
  7.2 9.3 copy-start.10
  7.3 9.3 copy-start.9
  7.3 12.7 %copy-start.6 = (f32[128,64]{0,1:T(8,128)S(1)}, f32[128,64]{0,1:T(8,128)}, u32[]{:S(2)}) copy-start(f32[128,64]{0,1:T(8,128)} %param.42) | copy-start | bytes 98308
  7.3 1016.0 %all-reduce.4.cloned.1.call-start = ((), (), s32[]{:S(2)}) async-start(), calls=%async_computation | async-start | bytes 4849664 | tf_op jit(solution)/shard_map/psum | solution.py:1594
  7.3 13.4 %copy-start.7 = (f32[128,64]{0,1:T(8,128)S(1)}, f32[128,64]{0,1:T(8,128)}, u32[]{:S(2)}) copy-start(f32[128,64]{0,1:T(8,128)} %param.56) | copy-start | bytes 98308
  8.2 13.2 %copy-start.8 = (f32[128,64]{0,1:T(8,128)S(1)}, f32[128,64]{0,1:T(8,128)}, u32[]{:S(2)}) copy-start(f32[128,64]{0,1:T(8,128)} %param.57) | copy-start | bytes 98308
  8.3 17.7 %collective-permute-start = (s32[2,24,192]{2,0,1:T(2,128)S(1)}, s32[2,24,192]{2,0,1:T(2,128)S(1)}, u32[]{:S(2)}, u32[]{:S(2)}) collective-permute-start(s32[2,24,192]{2,0,1:T(2,128)S(1)} %bitcast.53), channel_id=1, source_target_pairs={{0,0},{1,16},{2,1},{3,17},{4,4},{5,20},{6,5},{7,21},{8,8},{9,24},{... | collective-permute-start | bytes 110600 | tf_op jit(solution)/shard_map/ppermute | solution.py:1053
  9.0 17.0 %collective-permute-start.1 = (s32[2,24,192]{2,0,1:T(2,128)S(1)}, s32[2,24,192]{2,0,1:T(2,128)S(1)}, u32[]{:S(2)}, u32[]{:S(2)}) collective-permute-start(s32[2,24,192]{2,0,1:T(2,128)S(1)} %bitcast.54), channel_id=1, source_target_pairs={{0,16},{1,0},{2,17},{3,1},{4,20},{5,4},{6,21},{7,5},{8,24},{9,8},{... | collective-permute-start | bytes 110600 | tf_op jit(solution)/shard_map/ppermute | solution.py:1054
  625.1 121.6 %copy-start.5 = (f32[128,128]{1,0:T(8,128)S(1)}, f32[128,128]{1,0:T(8,128)}, u32[]{:S(2)}) copy-start(f32[128,128]{1,0:T(8,128)} %get-tuple-element.196) | copy-start | bytes 196612
  625.1 122.3 %copy-start.4 = (f32[128,128]{1,0:T(8,128)S(1)}, f32[128,128]{1,0:T(8,128)}, u32[]{:S(2)}) copy-start(f32[128,128]{1,0:T(8,128)} %get-tuple-element.197) | copy-start | bytes 196612
  625.1 124.5 %copy-start.1 = (f32[512,128]{1,0:T(8,128)S(1)}, f32[512,128]{1,0:T(8,128)}, u32[]{:S(2)}) copy-start(f32[512,128]{1,0:T(8,128)} %get-tuple-element.199) | copy-start | bytes 786436
  870.0 3.0 copy-start.2
Sparse Core Ops, SparseCore 0:
  872.1 151.1 all-reduce.3

commit v4 on v3

--- a/solution.py
+++ b/solution.py
@@ -395,7 +395,7 @@
 CHUNK_ROWS = SUBLANES * SUBLANES
 VMEM_BYTES = 58 * 2**20
 MESH = pl.DeviceIdType.MESH
-ROWS, WIRE, WHOLE, SUM, ANYWHERE = range(5)
+ROWS, WIRE, LANDED, WHOLE, SUM, ANYWHERE = range(6)
 
 
 class Bag:
@@ -404,9 +404,9 @@
 
 
 class Arg:
-    def __init__(self, array, kind, index=None, block=None, column=None):
+    def __init__(self, array, kind, index=None, block=None, column=None, half=None):
         self.array, self.kind, self.index, self.block = array, kind, index, block
-        self.column = column
+        self.column, self.half = column, half
 
     def spec(self):
         if self.index is None:
@@ -428,13 +428,13 @@
         self.shape, self.dtype, self.kind = shape, dtype, kind
 
     def spec(self):
-        return block_spec(self.shape, self.kind)
+        return block_spec(self.shape, ANYWHERE if self.kind == LANDED else self.kind)
 
 
 def block_spec(shape, kind):
-    if kind == ANYWHERE:
+    if kind in (WIRE, ANYWHERE):
         return pl.BlockSpec(memory_space=pl.ANY)
-    if kind == WIRE:
+    if kind == LANDED:
         return pl.BlockSpec((shape[0], CHUNK_ROWS, shape[2]), lambda step: (0, step // PHASES, 0))
     if kind == ROWS:
         return pl.BlockSpec((ROW_BLOCK,) + shape[1:], lambda step: (step,) + (0,) * (len(shape) - 1))
@@ -536,15 +536,17 @@
                 self.wide[lane, self.tokens(row), :] = value[:, start : start + LANES]
 
 
-def widen(wide, block):
+def widen(wide, low, chunk):
+    rows = pl.ds(pl.multiple_of(chunk * CHUNK_ROWS, CHUNK_ROWS), CHUNK_ROWS)
+
     def step(peer, carry):
-        value = block[peer].astype(F32)
+        value = low[peer, rows, :].astype(F32)
         start = pl.multiple_of(peer * CHUNK_ROWS, CHUNK_ROWS)
         for lane in range(wide.shape[0]):
             wide[lane, pl.ds(start, CHUNK_ROWS), :] = value[:, lane * LANES : (lane + 1) * LANES]
         return carry
 
-    lax.fori_loop(0, block.shape[0], step, 0)
+    lax.fori_loop(0, low.shape[0], step, 0)
 
 
 def narrow(low, wide, chunk):
@@ -676,20 +678,29 @@
     return jnp.where(lax.broadcasted_iota(jnp.int32, shape, 0) == bins, 1.0, 0.0).astype(BF16)
 
 
-def run_stage(body, name, rows, inputs, outputs, exchange=None):
+def run_stage(body, name, collective_id, rows, inputs, outputs, exchange=None):
     args, outs = leaves_of(inputs), leaves_of(outputs)
     steps = rows // ROW_BLOCK
     chunks = rows // SUBLANES
     wire_args = [index for index, arg in enumerate(args) if arg.kind == WIRE]
+    landed_args = [index for index, arg in enumerate(args) if arg.kind == LANDED]
+    keeps = [place for place, out in enumerate(outs) if out.kind == LANDED]
     wires = exchange.wires if exchange else 0
-    chunk_scratch = []
     if wire_args:
-        peers, _, tokens = args[wire_args[0]].array.shape
+        peers, half, tokens = args[wire_args[0]].array.shape[0], args[wire_args[0]].half, 0
+        tokens = args[wire_args[0]].array.shape[2]
     if exchange:
-        peers, tokens = exchange.peers, exchange.tokens
-    for _ in range(len(wire_args) + wires):
-        chunk_scratch.append(pltpu.VMEM((tokens // LANES, peers * CHUNK_ROWS, LANES), F32))
-    scratch = exchange.scratch() if exchange else []
+        peers, half, tokens = exchange.peers, exchange.half, exchange.tokens
+    low = pltpu.VMEM((peers, rows * SUBLANES, tokens), BF16)
+    many = pltpu.SemaphoreType.DMA((chunks, peers))
+    wide = pltpu.VMEM((tokens // LANES, peers * CHUNK_ROWS, LANES), F32)
+    groups = [
+        [wide] * (len(wire_args) + len(landed_args) + wires),
+        [low] * len(wire_args),
+        [many] * (2 * len(wire_args)),
+        [pltpu.SemaphoreType.DMA((1,))] * len(keeps),
+        exchange.scratch() if exchange else [],
+    ]
 
     def kernel(*refs):
         step = pl.program_id(0)
@@ -698,29 +709,66 @@
             ref if arg.column is None else Column(ref, arg.column) for arg, ref in zip(args, refs)
         ]
         out_refs = list(refs[len(args) : len(args) + len(outs)])
-        wide = list(refs[len(args) + len(outs) :][: len(chunk_scratch)])
-        held = refs[len(args) + len(outs) + len(chunk_scratch) :]
-        ring = Exchange(exchange.peers, exchange.half) if exchange else None
+        rest, parts = list(refs[len(args) + len(outs) :]), []
+        for group in groups:
+            parts.append(rest[: len(group)])
+            rest = rest[len(group) :]
+        wides, lands, sems, keep_sems, held = parts
+        saves = [
+            pltpu.make_async_copy(land, out_refs[place], sem.at[0])
+            for land, place, sem in zip(lands, keeps, keep_sems)
+        ]
+        ring = Exchange(peers, half)
+        arrivals = [
+            (in_refs[index], land, sems[2 * place], sems[2 * place + 1])
+            for place, (index, land) in enumerate(zip(wire_args, lands))
+        ]
+        i, o = bag_of(inputs, iter(in_refs)), bag_of(outputs, iter(out_refs))
 
         @pl.when(step == 0)
         def _():
-            if exchange:
-                ring.greet()
+            ring.greet()
             for out, ref in zip(outs, out_refs):
                 if out.kind == SUM:
                     ref[...] = jnp.zeros(out.shape, out.dtype)
-
-        @pl.when(phase == 0)
-        def _():
-            for index, target in zip(wire_args, wide):
-                widen(target, in_refs[index])
+            if exchange:
+                exchange.begin(i, held)
+            if arrivals:
+                ring.meet()
+
+                def start(index, carry):
+                    ring.start(arrivals, index)
+                    return carry
+
+                lax.fori_loop(0, chunks, start, 0)
+
+        if arrivals:
+
+            @pl.when(phase == 0)
+            def _():
+                ring.wait(arrivals, chunk)
+                for target, land in zip(wides, lands):
+                    widen(target, land, chunk)
+
+        if landed_args:
+
+            @pl.when(phase == 0)
+            def _():
+                for target, index in zip(wides[len(wire_args) :], landed_args):
+                    widen(target, in_refs[index], 0)
+
+        if saves:
+
+            @pl.when(step == steps - PHASES)
+            def _():
+                for save in saves:
+                    save.start()
 
         body_in = list(in_refs)
-        for index, source in zip(wire_args, wide):
+        for index, source in zip(wire_args + landed_args, wides):
             body_in[index] = Wire(source, phase)
-        sent = wide[len(wire_args) :]
-        i, o = bag_of(inputs, iter(body_in)), bag_of(outputs, iter(out_refs))
-        body(i, o, *[Wire(target, phase) for target in sent])
+        sent = wides[len(wire_args) + len(landed_args) :]
+        body(bag_of(inputs, iter(body_in)), o, *[Wire(target, phase) for target in sent])
         if exchange:
             moves = exchange.moves(held)
 
@@ -728,10 +776,11 @@
             def _():
                 for source, move in zip(sent, moves):
                     narrow(move[0], source, chunk)
-
-                @pl.when(chunk == 0)
-                def _():
-                    ring.meet()
+                if not arrivals:
+
+                    @pl.when(chunk == 0)
+                    def _():
+                        ring.meet()
 
                 ring.start(moves, chunk)
 
@@ -742,7 +791,9 @@
                     return carry
 
                 lax.fori_loop(0, chunks, wait, 0)
-                exchange.finish(ring, bag_of(inputs, iter(in_refs)), o, held)
+                exchange.finish(i, o, held)
+                for save in saves:
+                    save.wait()
 
     results = pl.pallas_call(
         kernel,
@@ -750,14 +801,14 @@
         in_specs=[arg.spec() for arg in args],
         out_specs=[out.spec() for out in outs],
         out_shape=[jax.ShapeDtypeStruct(out.shape, out.dtype) for out in outs],
-        scratch_shapes=chunk_scratch + scratch,
+        scratch_shapes=sum(groups, []),
         compiler_params=pltpu.CompilerParams(
             dimension_semantics=(pltpu.ARBITRARY,),
             vmem_limit_bytes=VMEM_BYTES,
-            has_side_effects=exchange is not None,
-            collective_id=exchange.collective_id if exchange else None,
+            has_side_effects=True,
+            collective_id=collective_id,
         ),
-        cost_estimate=pl.CostEstimate(flops=10**11, bytes_accessed=10**6, transcendentals=0),
+        cost_estimate=pl.CostEstimate(flops=0, bytes_accessed=0, transcendentals=0),
         name=name,
     )(*[arg.array for arg in args])
     return bag_of(outputs, iter(results))
@@ -882,124 +933,94 @@
 class Forward:
     wires = 2
 
-    def __init__(self, peers, half, rows, tokens, incoming, collective_id):
+    def __init__(self, peers, half, rows, tokens, incoming):
         self.peers, self.half, self.incoming = peers, half, incoming
         self.rows, self.tokens = rows * SUBLANES, tokens
         self.chunks = rows // SUBLANES
-        self.collective_id = collective_id
 
     def outs(self):
         block = (SUBLANES, self.tokens, self.tokens)
         return dict(
             left=Out(block, BF16, WHOLE),
             right=Out(block, BF16, WHOLE),
-            tri=Out((self.peers, self.rows, self.tokens), BF16, ANYWHERE),
+            tri=Out((self.peers, self.rows, self.tokens), BF16, WHOLE),
         )
 
     def scratch(self):
         low = pltpu.VMEM((self.peers, self.rows, self.tokens), BF16)
         many = pltpu.SemaphoreType.DMA((self.chunks, self.peers))
-        once = pltpu.SemaphoreType.DMA((1, self.peers))
-        return [low] * 5 + [many] * 4 + [once] * 2
+        return [low] * 4 + [many] * 4
 
     def moves(self, held):
-        return [(held[0], held[2], held[5], held[6]), (held[1], held[3], held[7], held[8])]
-
-    def finish(self, ring, i, o, held):
-        _, _, left_got, right_got, low = held[:5]
+        return [(held[0], held[2], held[4], held[5]), (held[1], held[3], held[6], held[7])]
+
+    def begin(self, i, held):
+        pass
+
+    def finish(self, i, o, held):
         axis = 0 if self.incoming else 1
-        middle = self.tokens * 2 // 3 // LANES * LANES
-        tri = [(low, o.tri, held[9], held[10])]
-
-        def multiply(pair, first, last):
+
+        def step(pair):
+            lefts, rights = join_channels(held[2], pair), join_channels(held[3], pair)
             found = []
-            for channel in (2 * pair, 2 * pair + 1):
-                left, right = o.left[channel], o.right[channel]
-                part = left[:, first:last] if self.incoming else left[first:last]
-                found.append(product_of(part, right, axis, axis))
-            split_channels(low, pair, *found, first)
-
-        def join(pair):
-            for got, out in ((left_got, o.left), (right_got, o.right)):
-                for index, value in enumerate(join_channels(got, pair)):
-                    out[2 * pair + index] = value
-            multiply(pair, 0, middle)
-
-        each_pair(join)
-        self.send_to(ring, tri, 0)
-        each_pair(lambda pair: multiply(pair, middle, self.tokens))
-        self.send_to(ring, tri, 1)
-        ring.wait(tri, 0)
-
-    def send_to(self, ring, tri, part):
-        inner = self.peers // 2
-        mine = lax.div(ring.me, inner)
-
-        @pl.when(mine == part)
-        def _():
-            for copy in ring.copies(tri, 0, [step for step in ring.order if step < inner] + [0]):
-                copy.start()
-
-        @pl.when(mine != part)
-        def _():
-            for copy in ring.copies(tri, 0, [step for step in ring.order if step >= inner]):
-                copy.start()
+            for index in range(2):
+                o.left[2 * pair + index] = lefts[index]
+                o.right[2 * pair + index] = rights[index]
+                found.append(product_of(lefts[index], rights[index], axis, axis))
+            split_channels(o.tri, pair, *found)
+
+        each_pair(step)
 
 
 class Backward:
     wires = 1
 
-    def __init__(self, peers, half, rows, tokens, incoming, collective_id):
+    def __init__(self, peers, half, rows, tokens, incoming):
         self.peers, self.half, self.incoming = peers, half, incoming
         self.rows, self.tokens = rows * SUBLANES, tokens
         self.chunks = rows // SUBLANES
-        self.collective_id = collective_id
 
     def outs(self):
         wire = (self.peers, self.rows, self.tokens)
-        return dict(grad_left=Out(wire, BF16, ANYWHERE), grad_right=Out(wire, BF16, ANYWHERE))
+        return dict(grad_left=Out(wire, BF16, WHOLE), grad_right=Out(wire, BF16, WHOLE))
 
     def scratch(self):
         low = pltpu.VMEM((self.peers, self.rows, self.tokens), BF16)
         block = pltpu.VMEM((SUBLANES, self.tokens, self.tokens), BF16)
         many = pltpu.SemaphoreType.DMA((self.chunks, self.peers))
-        once = pltpu.SemaphoreType.DMA((1, self.peers))
-        return [low] * 4 + [block] + [many] * 2 + [once] * 4
+        return [low] * 2 + [block] * 2 + [many] * 2 + [pltpu.SemaphoreType.DMA((2,))]
 
     def moves(self, held):
-        return [(held[0], held[1], held[5], held[6])]
-
-    def finish(self, ring, i, o, held):
-        _, got, left_low, right_low, grads = held[:5]
-
-        def left_step(pair):
-            found = []
-            for index, grad in enumerate(join_channels(got, pair)):
-                channel = 2 * pair + index
-                grads[channel] = grad
-                right = i.owned.right[channel]
-                found.append(
-                    product_of(right, grad, 1, 1) if self.incoming else product_of(grad, right, 1, 0)
-                )
-            split_channels(left_low, pair, *found)
-
-        def right_step(pair):
-            found = []
-            for channel in (2 * pair, 2 * pair + 1):
-                grad, left = grads[channel], i.owned.left[channel]
-                found.append(
-                    product_of(left, grad, 1, 0) if self.incoming else product_of(grad, left, 0, 0)
-                )
-            split_channels(right_low, pair, *found)
-
-        left_moves = [(left_low, o.grad_left, held[7], held[8])]
-        right_moves = [(right_low, o.grad_right, held[9], held[10])]
-        each_pair(left_step)
-        ring.start(left_moves, 0)
-        each_pair(right_step)
-        ring.start(right_moves, 0)
-        ring.wait(left_moves, 0)
-        ring.wait(right_moves, 0)
+        return [(held[0], held[1], held[4], held[5])]
+
+    def owned(self, i, held):
+        return [
+            pltpu.make_async_copy(i.owned.left, held[2], held[6].at[0]),
+            pltpu.make_async_copy(i.owned.right, held[3], held[6].at[1]),
+        ]
+
+    def begin(self, i, held):
+        for copy in self.owned(i, held):
+            copy.start()
+
+    def finish(self, i, o, held):
+        for copy in self.owned(i, held):
+            copy.wait()
+
+        def step(pair):
+            lefts, rights = [], []
+            for index, grad in enumerate(join_channels(held[1], pair)):
+                left, right = held[2][2 * pair + index], held[3][2 * pair + index]
+                if self.incoming:
+                    lefts.append(product_of(right, grad, 1, 1))
+                    rights.append(product_of(left, grad, 1, 0))
+                else:
+                    lefts.append(product_of(grad, right, 1, 0))
+                    rights.append(product_of(grad, left, 0, 0))
+            split_channels(o.grad_left, pair, *lefts)
+            split_channels(o.grad_right, pair, *rights)
+
+        each_pair(step)
 
 
 def prepare(triangle_input, triangle_output, expand_weight, reduce_weight, distogram_weight, norm_gains):
@@ -1167,7 +1188,7 @@
         compiler_params=pltpu.CompilerParams(
             collective_id=collective_id, has_side_effects=True, vmem_limit_bytes=VMEM_BYTES
         ),
-        cost_estimate=pl.CostEstimate(flops=10**10, bytes_accessed=10**6, transcendentals=0),
+        cost_estimate=pl.CostEstimate(flops=0, bytes_accessed=0, transcendentals=0),
         name="reduce_rest",
     )(*grids, *gains, *rows)
     return whole, starts, row_starts, gain_start
@@ -1360,18 +1381,24 @@
     def transition_outs():
         return dict(up=sum_out(width, hidden), down=sum_out(hidden // 2, width), gain=gain_out())
 
-    identities = iter(range(4 * layers))
+    identities = iter(range(4 * layers + 2))
 
     def forward(incoming):
-        return Forward(peers, half, rows, tokens, incoming, next(identities))
+        return Forward(peers, half, rows, tokens, incoming)
 
     def backward(incoming):
-        return Backward(peers, half, rows, tokens, incoming, next(identities))
+        return Backward(peers, half, rows, tokens, incoming)
+
+    def wire(array):
+        return Arg(array, WIRE, half=half)
+
+    def landed_out():
+        return Out((peers, rows * SUBLANES, tokens), BF16, LANDED)
 
     def owned(kept):
-        return dict(left=Arg(kept.left, WHOLE), right=Arg(kept.right, WHOLE))
-
-    kept, states, middles, sums = {}, {}, {}, {}
+        return dict(left=Arg(kept.left, ANYWHERE), right=Arg(kept.right, ANYWHERE))
+
+    kept, states, middles, tris = {}, {}, {}, {}
 
     def first_body(i, o, left, right):
         state = dot(i.table_t[...], bins_hot(i.bins, table_rows))
@@ -1386,7 +1413,8 @@
     got = run_stage(
         first_body,
         "first_state",
-        rows,
+        next(identities),
+            rows,
         dict(
             bins=bins,
             proj_rows=Arg(proj_rows, ROWS),
@@ -1417,56 +1445,60 @@
         got = run_stage(
             between_body,
             "between_updates",
+            next(identities),
             rows,
             dict(
                 state=Arg(states[layer, 0], ROWS),
-                tri=Arg(kept[layer, 0].tri, WIRE),
+                tri=wire(kept[layer, 0].tri),
                 mask=pair_mask,
                 end=triangle_weights(layer, 0, finishes=True),
                 start=triangle_weights(layer, 1, starts=True),
             ),
-            dict(state=state_out(), **exchange.outs()),
+            dict(state=state_out(), landed=landed_out(), **exchange.outs()),
             exchange,
         )
-        kept[layer, 1], states[layer, 1] = got, got.state
+        kept[layer, 1], states[layer, 1], tris[layer, 0] = got, got.state, got.landed
         if layer + 1 == layers:
             break
         exchange = forward(False)
         got = run_stage(
             layer_end_body,
             "layer_end",
+            next(identities),
             rows,
             dict(
                 state=Arg(states[layer, 1], ROWS),
-                tri=Arg(kept[layer, 1].tri, WIRE),
+                tri=wire(kept[layer, 1].tri),
                 mask=pair_mask,
                 end=triangle_weights(layer, 1, finishes=True),
                 lift=transition_weights(layer),
                 start=triangle_weights(layer + 1, 0, starts=True),
             ),
-            dict(middle=state_out(), state=state_out(), **exchange.outs()),
+            dict(middle=state_out(), state=state_out(), landed=landed_out(), **exchange.outs()),
             exchange,
         )
+        tris[layer, 1] = got.landed
         kept[layer + 1, 0], states[layer + 1, 0] = got, got.state
         middles[layer] = got.middle
 
-    def loss_body(i, o, wire):
+    def loss_body(i, o, sent):
         state, kept_triangle = triangle_finish(i.end, i.tri, read_rows(i.state))
         lifted = transition(i.lift, state)
         grad = head_back(i.head, o.head, transition_finish(i.lift, state, lifted))
         grad = transition_back(i.lift, o.lift, grad, lifted)
         write_rows(o.grad, grad)
-        triangle_back_start(i.end, o.end, wire, grad, kept_triangle)
+        triangle_back_start(i.end, o.end, sent, grad, kept_triangle)
 
     top = layers - 1
     exchange = backward(True)
     got = run_stage(
         loss_body,
         "loss",
-        rows,
+        next(identities),
+            rows,
         dict(
             state=Arg(states[top, 1], ROWS),
-            tri=Arg(kept[top, 1].tri, WIRE),
+            tri=wire(kept[top, 1].tri),
             end=triangle_weights(top, 1, finishes=True, back=True),
             lift=transition_weights(top, back=True),
             head=dict(
@@ -1494,22 +1526,22 @@
     )
     head, lifts, ends, begins = got.head, {top: got.lift}, {(top, 1): got.end}, {}
 
-    def between_back_body(i, o, wire):
+    def between_back_body(i, o, sent):
         grad = triangle_back_finish(
             i.start, i.back, o.start, read_rows(i.mask), read_rows(i.grad), read_rows(i.state)
         )
         write_rows(o.grad, grad)
         _, kept_triangle = triangle_finish(i.end, i.tri, read_rows(i.before))
-        triangle_back_start(i.end, o.end, wire, grad, kept_triangle)
-
-    def layer_end_back_body(i, o, wire):
+        triangle_back_start(i.end, o.end, sent, grad, kept_triangle)
+
+    def layer_end_back_body(i, o, sent):
         grad = triangle_back_finish(
             i.start, i.back, o.start, read_rows(i.mask), read_rows(i.grad), read_rows(i.state)
         )
         grad = transition_back(i.lift, o.lift, grad, transition(i.lift, read_rows(i.middle)))
         write_rows(o.grad, grad)
         _, kept_triangle = triangle_finish(i.end, i.tri, read_rows(i.before))
-        triangle_back_start(i.end, o.end, wire, grad, kept_triangle)
+        triangle_back_start(i.end, o.end, sent, grad, kept_triangle)
 
     def first_back_body(i, o):
         grad = triangle_back_finish(
@@ -1532,8 +1564,8 @@
                 mask=pair_mask,
                 start=triangle_weights(layer, kind, starts=True, back=True),
                 back=dict(
-                    grad_left=Arg(got.grad_left, WIRE),
-                    grad_right=Arg(got.grad_right, WIRE),
+                    grad_left=wire(got.grad_left),
+                    grad_right=wire(got.grad_right),
                     grad_gate=Arg(got.end.grad_gate, ROWS),
                 ),
             )
@@ -1542,7 +1574,8 @@
                 got = run_stage(
                     first_back_body,
                     "first_state_back",
-                    rows,
+                    next(identities),
+            rows,
                     dict(bins=bins, **inputs),
                     dict(
                         table=sum_out(table_rows, width),
@@ -1556,7 +1589,7 @@
             before = (layer, 0) if kind == 1 else (layer - 1, 1)
             inputs.update(
                 before=Arg(states[before], ROWS),
-                tri=Arg(kept[before].tri, WIRE),
+                tri=Arg(tris[before], LANDED),
                 end=triangle_weights(*before, finishes=True, back=True),
                 owned=owned(kept[before]),
             )
@@ -1572,7 +1605,15 @@
                     lift=transition_weights(layer - 1, forth=False, back=True),
                 )
                 outputs.update(lift=transition_outs())
-            got = run_stage(body, name, rows, inputs, dict(**outputs, **exchange.outs()), exchange)
+            got = run_stage(
+                body,
+                name,
+                next(identities),
+                rows,
+                inputs,
+                dict(**outputs, **exchange.outs()),
+                exchange,
+            )
             begins[layer, kind], ends[before] = got.start, got.end
             if kind == 0:
                 lifts[layer - 1] = got.lift
@@ -1617,7 +1658,7 @@
         col_part,
     ]
     rest, *starts = reduce_rest(
-        half, peers, 4 * layers, grids, partial_gains, [head.loss, head.count]
+        half, peers, next(identities), grids, partial_gains, [head.loss, head.count]
     )
     return update(rest, *starts, early, weights, firsts, seconds)
 

time: 1050 us -> 904 us (0.86)
  waiting for transfers between devices: 91.9 us -> 0.04 us
  Pallas kernels: 911 us -> 849 us
    psum x1, waiting for transfers between devices: 91.9 us -> 0.02 us  [step_by_crop(): early = lax.psum(early, ('row', 'head'))]
    pallas_call x9, Pallas kernels: 837 us -> 792 us  [run_stage(): pl.pallas_call(kernel, grid=(steps,), in_specs=[arg.spec() for arg in arg...]
    pallas_call x1, Pallas kernels: 57.3 us -> 40.5 us  [reduce_rest(): pl.pallas_call(kernel, in_specs=[inside] * count, out_specs=inside, out_s...]
  transfers between devices with their start and end apart: 3 -> 3, of which waited for: 1 -> 0; matrix products, arithmetic and copies ran while one was open for 1% -> 1% of each run, Pallas kernels for 6% -> 26%
where the time goes in v4:
time: 904 us; the launch traced here: 893 us
  Pallas kernels  849 us (94%)
  between operations  14.9 us (2%)
  local copies, waits for them, and re-layouts  13.1 us (1%)
    pallas_call x9, Pallas kernels, run_stage(): pl.pallas_call(kernel, grid=(steps,), in_specs=[arg.spec() for arg in arg...  792 us
    pallas_call x1, Pallas kernels, reduce_rest(): pl.pallas_call(kernel, in_specs=[inside] * count, out_specs=inside, out_s...  40.5 us
  transfers between devices with their start and end apart: 3, of which 0 were waited for; matrix products, arithmetic and copies ran while one was open for 1% of the time, Pallas kernels for 26%

profile of v4, /device:TPU:0, one launch (start us, length us, event | category | flops | bytes accessed | tf_op | source)
XLA Modules:
  0.0 892.7 jit_solution(4174496569253074111)
XLA Ops:
  7.3 0.9 fusion.8
  8.9 5.4 collective-permute-start.1
  14.3 1.2 fusion.2
  16.6 0.8 compare_select_fusion.refs_0_
  17.4 1.7 copy.83.refs_1_
  19.1 0.8 copy.92
  19.9 0.7 copy.82.refs_12_
  20.6 3.8 prepare.1
  24.5 0.7 fusion.13.refs_15_
  25.2 0.8 fusion.12
  26.0 66.3 %first_state.1 = (f32[24,128,384]{2,1,0:T(8,128)}, bf16[8,384,384]{2,1,0:T(8,128)(2,1)}, bf16[8,384,384]{2,1,0:T(8,128)(2,1)}, bf16[16,192,384]{2,1,0:T(8,128)(2,1)}) custom-call(s32[24,1,384]{2,1,0:T(1,128)} %compare_select_fusion.refs_0_, f32[24,128,1]{2,1,0:T(8,128)} %copy.83.refs_1_, f32[128,384]{1,0:T(8,128)} %bitcast.47, ...), custom_call_target="tpu_custom_call" | custom-call | tf_op jit(solution)/shard_map/first_state/pallas_call | solution.py:798
  92.3 90.3 %between_updates.2 = (f32[24,128,384]{2,1,0:T(8,128)}, bf16[16,192,384]{2,1,0:T(8,128)(2,1)}, bf16[8,384,384]{2,1,0:T(8,128)(2,1)}, bf16[8,384,384]{2,1,0:T(8,128)(2,1)}, bf16[16,192,384]{2,1,0:T(8,128)(2,1)}) custom-call(f32[24,128,384]{2,1,0:T(8,128)} %get-tuple-element.132.refs_0_.refs_9_.refs_2_, bf16[16,192,384]{2,1,0:T(8,128)(2,1)} %get-tuple-element.133.refs_1_, ...), custom_call_target="tpu_custom_call" | custom-call | tf_op jit(solution)/shard_map/between_updates/pallas_call | solution.py:798
  182.7 89.6 %layer_end.1 = (f32[24,128,384]{2,1,0:T(8,128)}, f32[24,128,384]{2,1,0:T(8,128)}, bf16[16,192,384]{2,1,0:T(8,128)(2,1)}, bf16[8,384,384]{2,1,0:T(8,128)(2,1)}, b...) custom-call(f32[24,128,384]{2,1,0:T(8,128)} %get-tuple-element.135.refs_0_.refs_9_.refs_1_, ...), custom_call_target="tpu_custom_call" | custom-call | tf_op jit(solution)/shard_map/layer_end/pallas_call | solution.py:798
  272.3 91.0 %between_updates.3 = (f32[24,128,384]{2,1,0:T(8,128)}, bf16[16,192,384]{2,1,0:T(8,128)(2,1)}, bf16[8,384,384]{2,1,0:T(8,128)(2,1)}, bf16[8,384,384]{2,1,0:T(8,128)(2,1)}, bf16[16,192,384]{2,1,0:T(8,128)(2,1)}) custom-call(f32[24,128,384]{2,1,0:T(8,128)} %get-tuple-element.139.refs_0_.refs_9_.refs_1_, bf16[16,192,384]{2,1,0:T(8,128)(2,1)} %get-tuple-element.140.refs_1_, ...), custom_call_target="tpu_custom_call" | custom-call | tf_op jit(solution)/shard_map/between_updates/pallas_call | solution.py:798
  363.3 80.7 %loss.1 = (f32[24,128,384]{2,1,0:T(8,128)}, f32[1,128]{1,0:T(1,128)}, f32[1,128]{1,0:T(1,128)}, f32[64,128]{1,0:T(8,128)}, f32[128,128]{1,0:T(8,128)}, /*index=5...) custom-call(f32[24,128,384]{2,1,0:T(8,128)} %get-tuple-element.141.r, ...), custom_call_target="tpu_custom_call" | custom-call | tf_op jit(solution)/shard_map/loss/pallas_call | solution.py:798
  444.1 91.4 %between_updates_back.2 = (f32[128,640]{1,0:T(8,128)}, f32[128,128]{1,0:T(8,128)}, f32[24,128,384]{2,1,0:T(8,128)}, bf16[24,128,384]{2,1,0:T(8,128)(2,1)}, f32[1...) custom-call(f32[24,128,384]{2,1,0:T(8,128)} %get-tuple-element.150.refs_0_, ...), custom_call_target="tpu_custom_call" | custom-call | tf_op jit(solution)/shard_map/between_updates_back/pallas_call | solution.py:798
  535.6 94.3 %layer_end_back.1 = (f32[128,640]{1,0:T(8,128)}, f32[128,128]{1,0:T(8,128)}, f32[24,128,384]{2,1,0:T(8,128)}, bf16[24,128,384]{2,1,0:T(8,128)(2,1)}, f32[128,128...) custom-call(f32[24,128,384]{2,1,0:T(8,128)} %get-tuple-element.158.r, ...), custom_call_target="tpu_custom_call" | custom-call | tf_op jit(solution)/shard_map/layer_end_back/pallas_call | solution.py:798
  629.9 0.9 constant_dynamic-update-slice_fusion.4
  630.8 1.0 constant_dynamic-update-slice_fusion.1
  631.8 0.8 copy-done.1
  632.7 0.7 copy.87.refs_20_
  633.4 0.7 copy.88.refs_28_
  634.2 108.7 %between_updates_back.3 = (f32[128,640]{1,0:T(8,128)}, f32[128,128]{1,0:T(8,128)}, f32[24,128,384]{2,1,0:T(8,128)}, bf16[24,128,384]{2,1,0:T(8,128)(2,1)}, f32[1...) custom-call(f32[24,128,384]{2,1,0:T(8,128)} %get-tuple-element.166.refs_0_, ...), custom_call_target="tpu_custom_call" | custom-call | tf_op jit(solution)/shard_map/between_updates_back/pallas_call | solution.py:798
  742.8 79.9 %first_state_back.1 = (f32[80,128]{1,0:T(8,128)}, f32[24,128,128]{2,1,0:T(8,128)}, f32[128,384]{1,0:T(8,128)}, f32[128,640]{1,0:T(8,128)}, f32[128,128]{1,0:T(8,128)}) custom-call(s32[24,1,384]{2,1,0:T(1,128)} %compare_select_fusion.refs_0_, f32[24,128,384]{2,1,0:T(8,128)} %get-tuple-element.173.refs_1_, ...), custom_call_target="tpu_custom_call" | custom-call | tf_op jit(solution)/shard_map/first_state_back/pallas_call | solution.py:798
  822.7 1.9 reduce_sum.9
  824.6 1.0 fusion.14.refs_5_
  825.6 2.1 fusion.refs_6_
  827.7 40.5 %reduce_rest.1.refs_0_ = f32[2432,128]{1,0:T(8,128)} custom-call(f32[128,640]{1,0:T(8,128)} %get-tuple-element.177.refs_0_, f32[128,640]{1,0:T(8,128)} %get-tuple-element.178.refs_1_, f32[128,128]{1,0:T(8,128)} %get-tuple-element.179.refs_2_, f32[64,128]{1,0:T(8,128)} %get-tuple-element.180.refs_3_, f32[80,128]{1,0:T(8,128)} %get-tuple-element.181.refs_4_, ...), custom_call_target="tpu_custom_call" | custom-call | tf_op jit(solution)/shard_map/reduce_rest/pallas_call | solution.py:1179
  868.2 12.6 %update.1 = (f32[1,1]{1,0:T(1,128)}, f32[1,1]{1,0:T(1,128)}, f32[1,1]{1,0:T(1,128)}, f32[66,128]{1,0:T(8,128)}, f32[66,128]{1,0:T(8,128)}, /*index=5*/f32[66,128...) custom-call(f32[2432,128]{1,0:T(8,128)} %reduce_rest.1.refs_0_, ...), custom_call_target="tpu_custom_call" | custom-call | tf_op jit(solution)/shard_map/update/pallas_call | solution.py:1274
  880.9 1.5 copy.89
  882.4 1.5 copy.90
  883.9 1.5 copy.91
  (44 shorter events, 1.9 us)
Async XLA Ops:
  7.2 7.1 copy-start
  7.2 8.4 copy-start.11
  7.2 8.4 copy-start.3
  7.2 9.2 %copy-start.10 = (s32[2,384]{1,0:T(2,128)S(1)}, s32[2,384]{1,0:T(2,128)}, u32[]{:S(2)}) copy-start(s32[2,384]{1,0:T(2,128)} %param.31) | copy-start | bytes 9220
  7.3 9.2 %copy-start.9 = (s32[2,384]{1,0:T(2,128)S(1)}, s32[2,384]{1,0:T(2,128)}, u32[]{:S(2)}) copy-start(s32[2,384]{1,0:T(2,128)} %param.32) | copy-start | bytes 9220
  7.3 12.7 %copy-start.6 = (f32[128,64]{0,1:T(8,128)S(1)}, f32[128,64]{0,1:T(8,128)}, u32[]{:S(2)}) copy-start(f32[128,64]{0,1:T(8,128)} %param.42) | copy-start | bytes 98308
  7.3 861.0 %all-reduce.4.cloned.1.call-start = ((), (), s32[]{:S(2)}) async-start(), calls=%async_computation | async-start | bytes 4849664 | tf_op jit(solution)/shard_map/psum | solution.py:1635
  8.2 16.3 %collective-permute-start = (s32[2,24,192]{2,0,1:T(2,128)S(1)}, s32[2,24,192]{2,0,1:T(2,128)S(1)}, u32[]{:S(2)}, u32[]{:S(2)}) collective-permute-start(s32[2,24,192]{2,0,1:T(2,128)S(1)} %bitcast.53), channel_id=1, source_target_pairs={{0,0},{1,16},{2,1},{3,17},{4,4},{5,20},{6,5},{7,21},{8,8},{9,24},{... | collective-permute-start | bytes 110600 | tf_op jit(solution)/shard_map/ppermute | solution.py:1074
  8.9 15.6 %collective-permute-start.1 = (s32[2,24,192]{2,0,1:T(2,128)S(1)}, s32[2,24,192]{2,0,1:T(2,128)S(1)}, u32[]{:S(2)}, u32[]{:S(2)}) collective-permute-start(s32[2,24,192]{2,0,1:T(2,128)S(1)} %bitcast.54), channel_id=1, source_target_pairs={{0,16},{1,0},{2,17},{3,1},{4,20},{5,4},{6,21},{7,5},{8,24},{9,8},{... | collective-permute-start | bytes 110600 | tf_op jit(solution)/shard_map/ppermute | solution.py:1075
  535.5 95.2 %copy-start.5 = (f32[128,128]{1,0:T(8,128)S(1)}, f32[128,128]{1,0:T(8,128)}, u32[]{:S(2)}) copy-start(f32[128,128]{1,0:T(8,128)} %get-tuple-element.202) | copy-start | bytes 196612
  535.5 95.2 %copy-start.4 = (f32[128,128]{1,0:T(8,128)S(1)}, f32[128,128]{1,0:T(8,128)}, u32[]{:S(2)}) copy-start(f32[128,128]{1,0:T(8,128)} %get-tuple-element.203) | copy-start | bytes 196612
  535.6 96.2 %copy-start.2 = (f32[512,128]{1,0:T(8,128)S(1)}, f32[512,128]{1,0:T(8,128)}, u32[]{:S(2)}) copy-start(f32[512,128]{1,0:T(8,128)} %get-tuple-element.205) | copy-start | bytes 786436
  629.9 2.8 copy-start.7
  629.9 3.5 copy-start.8
  631.8 0.9 copy-start.1
Sparse Core Ops, SparseCore 0:
  632.8 163.5 all-reduce.3

commit v5 on v4

--- a/solution.py
+++ b/solution.py
@@ -390,7 +390,8 @@
 LANES = 128
 SUBLANES = 8
 PACKED = 16
-ROW_BLOCK = 2
+ROW_BLOCK = 4
+STREAM_ROWS = 2
 PHASES = SUBLANES // ROW_BLOCK
 CHUNK_ROWS = SUBLANES * SUBLANES
 VMEM_BYTES = 58 * 2**20
@@ -499,14 +500,26 @@
     return total
 
 
-def read_rows(ref):
-    return jnp.concatenate([ref[row] for row in range(ref.shape[0])], axis=1)
-
-
-def write_rows(ref, value):
+def read_rows(ref, rows):
+    return jnp.concatenate([ref[row] for row in rows], axis=1)
+
+
+def write_rows(ref, rows, value):
     cols = ref.shape[2]
-    for row in range(ref.shape[0]):
-        ref[row] = value[:, row * cols : (row + 1) * cols].astype(ref.dtype)
+    for place, row in enumerate(rows):
+        ref[row] = value[:, place * cols : (place + 1) * cols].astype(ref.dtype)
+
+
+def alternate(streams):
+    while streams:
+        going = []
+        for stream in streams:
+            try:
+                next(stream)
+                going.append(stream)
+            except StopIteration:
+                pass
+        streams = going
 
 
 class Wire:
@@ -517,22 +530,17 @@
         width = self.wide.shape[1] // SUBLANES
         return pl.ds(self.phase * ROW_BLOCK + row, width, stride=SUBLANES)
 
-    def read(self):
+    def read(self, rows):
         lanes = self.wide.shape[0]
         return jnp.concatenate(
-            [
-                self.wide[lane, self.tokens(row), :]
-                for row in range(ROW_BLOCK)
-                for lane in range(lanes)
-            ],
-            axis=1,
+            [self.wide[lane, self.tokens(row), :] for row in rows for lane in range(lanes)], axis=1
         )
 
-    def write(self, value):
+    def write(self, rows, value):
         lanes = self.wide.shape[0]
-        for row in range(ROW_BLOCK):
+        for place, row in enumerate(rows):
             for lane in range(lanes):
-                start = (row * lanes + lane) * LANES
+                start = (place * lanes + lane) * LANES
                 self.wide[lane, self.tokens(row), :] = value[:, start : start + LANES]
 
 
@@ -562,53 +570,65 @@
     lax.fori_loop(0, low.shape[0], step, 0)
 
 
-def triangle_start(weights, mask, left_wire, right_wire, state):
+def triangle_start(weights, i, rows, wires, state):
     width = state.shape[0]
     unit, _ = unit_of(state)
     normed = (unit * weights.gain0[...]).astype(BF16)
     mixed = dot(weights.mix_t[...], normed)
-    for wire, base in ((left_wire, 0), (right_wire, 2 * width)):
+    yield
+    mask = read_rows(i.mask, rows)
+    for wire, base in zip(wires, (0, 2 * width)):
         gate = sigmoid(mixed[base : base + width])
-        wire.write(mask * gate * mixed[base + width : base + 2 * width])
-
-
-def triangle_finish(weights, wire, state):
+        wire.write(rows, mask * gate * mixed[base + width : base + 2 * width])
+
+
+def triangle_finish(weights, rows, wire, state):
     unit, _ = unit_of(state)
     normed = (unit * weights.gain0[...]).astype(BF16)
-    gate = sigmoid(dot(weights.gate_t[...], normed))
-    tri_unit, tri_scale = unit_of(wire.read())
+    opened = dot(weights.gate_t[...], normed)
+    yield
+    tri_unit, tri_scale = unit_of(wire.read(rows))
     shaped = (tri_unit * weights.gain1[...]).astype(BF16)
     branch = dot(weights.out_t[...], shaped)
+    yield
+    gate = sigmoid(opened)
     return (state + gate * branch, (gate, tri_unit, tri_scale, shaped, branch))
 
 
-def triangle_back_start(weights, o, wire, grad, kept):
+def triangle_back_start(weights, o, rows, wire, grad, kept):
     gate, tri_unit, tri_scale, shaped, branch = kept
     grad_branch = (grad * gate).astype(BF16)
-    write_rows(o.grad_gate, grad * branch * gate * (1.0 - gate))
+    grad_shaped = dot(weights.out[...], grad_branch)
+    yield
     o.out[...] += dot_pairs(shaped, grad_branch)
-    grad_shaped = dot(weights.out[...], grad_branch)
+    write_rows(o.grad_gate, rows, grad * branch * gate * (1.0 - gate))
+    yield
     o.gain1[...] += fold(grad_shaped * tri_unit)
-    wire.write(unit_back(grad_shaped, tri_unit, tri_scale, weights.gain1[...]))
-
-
-def triangle_back_finish(weights, i, o, mask, grad, state):
+    wire.write(rows, unit_back(grad_shaped, tri_unit, tri_scale, weights.gain1[...]))
+
+
+def triangle_back_finish(weights, i, o, rows):
+    grad, state = read_rows(i.grad, rows), read_rows(i.state, rows)
     width = state.shape[0]
     unit, scale = unit_of(state)
     gain = weights.gain0[...]
     normed = (unit * gain).astype(BF16)
     mixed = dot(weights.mix_t[...], normed)
+    yield
+    mask = read_rows(i.mask, rows)
     parts = []
-    for wire, base in ((i.grad_left, 0), (i.grad_right, 2 * width)):
-        back = wire.read() * mask
+    for wire, base in ((i.back.grad_left, 0), (i.back.grad_right, 2 * width)):
+        back = wire.read(rows) * mask
         gate = sigmoid(mixed[base : base + width])
         back_gate = back * gate
         parts.append((back_gate * mixed[base + width : base + 2 * width] * (1.0 - gate)).astype(BF16))
         parts.append(back_gate.astype(BF16))
-    parts.append(read_rows(i.grad_gate))
+    parts.append(read_rows(i.back.grad_gate, rows))
     grad_mixed = jnp.concatenate(parts, axis=0)
+    yield
+    grad_normed = dot(weights.mix[...], grad_mixed)
     o.mix[...] += dot_pairs(normed, grad_mixed)
-    grad_normed = dot(weights.mix[...], grad_mixed)
+    yield
     o.gain0[...] += fold(grad_normed * unit)
     return grad + unit_back(grad_normed, unit, scale, gain)
 
@@ -617,6 +637,7 @@
     unit, scale = unit_of(state)
     lifted = (unit * weights.gain[...]).astype(BF16)
     inner = dot(weights.up_t[...], lifted)
+    yield
     half = inner.shape[0] // 2
     gate = inner[:half]
     slope = sigmoid(gate)
@@ -624,17 +645,14 @@
     return (unit, scale, lifted, inner, slope, product)
 
 
-def transition_finish(weights, state, kept):
-    return state + dot(weights.down_t[...], kept[5])
-
-
 def transition_back(weights, o, grad, kept):
     unit, scale, lifted, inner, slope, product = kept
     half = inner.shape[0] // 2
     gate, up = inner[:half], inner[half:]
     grad_low = grad.astype(BF16)
+    grad_product = dot(weights.down[...], grad_low)
     o.down[...] += dot_pairs(product, grad_low)
-    grad_product = dot(weights.down[...], grad_low)
+    yield
     scaled = grad_product * slope
     grad_inner = jnp.concatenate(
         [
@@ -643,37 +661,41 @@
         ],
         axis=0,
     )
+    yield
+    grad_lifted = dot(weights.up[...], grad_inner)
     o.up[...] += dot_pairs(lifted, grad_inner)
-    grad_lifted = dot(weights.up[...], grad_inner)
+    yield
     o.gain[...] += fold(grad_lifted * unit)
     return grad + unit_back(grad_lifted, unit, scale, weights.gain[...])
 
 
-def head_back(i, o, state):
+def head_back(i, o, rows, state):
     unit, scale = unit_of(state)
     gain = i.gain[...]
     shown = (unit * gain).astype(BF16)
     logits = dot(i.logits_t[...], shown)
+    yield
     largest = jnp.max(logits, axis=0, keepdims=True)
     raised = jnp.exp(logits - largest)
     total = jnp.sum(raised, axis=0, keepdims=True)
     log_total = largest + jnp.log(total)
-    target = read_rows(i.target)
-    weight = read_rows(i.weight)
+    target = read_rows(i.target, rows)
+    weight = read_rows(i.weight, rows)
     hot = lax.broadcasted_iota(jnp.int32, logits.shape, 0) == target
     picked = jnp.sum(jnp.where(hot, logits, 0.0), axis=0, keepdims=True)
     o.loss[...] += fold(weight * (log_total - picked))
     o.count[...] += fold(weight)
     share = raised * (1.0 / total)
     grad_scores = (weight * (share - jnp.where(hot, 1.0, 0.0))).astype(BF16)
+    grad_shown = dot(i.logits[...], grad_scores)
     o.logits[...] += dot_pairs(grad_scores, shown)
-    grad_shown = dot(i.logits[...], grad_scores)
+    yield
     o.gain[...] += fold(grad_shown * unit)
     return unit_back(grad_shown, unit, scale, gain)
 
 
-def bins_hot(bins, table_rows):
-    bins = read_rows(bins)
+def bins_hot(bins, rows, table_rows):
+    bins = read_rows(bins, rows)
     shape = (table_rows, bins.shape[1])
     return jnp.where(lax.broadcasted_iota(jnp.int32, shape, 0) == bins, 1.0, 0.0).astype(BF16)
 
@@ -768,7 +790,14 @@
         for index, source in zip(wire_args + landed_args, wides):
             body_in[index] = Wire(source, phase)
         sent = wides[len(wire_args) + len(landed_args) :]
-        body(bag_of(inputs, iter(body_in)), o, *[Wire(target, phase) for target in sent])
+        given = bag_of(inputs, iter(body_in))
+        out_wires = [Wire(target, phase) for target in sent]
+        alternate(
+            [
+                body(given, o, range(first, first + STREAM_ROWS), *out_wires)
+                for first in range(0, ROW_BLOCK, STREAM_ROWS)
+            ]
+        )
         if exchange:
             moves = exchange.moves(held)
 
@@ -923,11 +952,8 @@
 
 
 def each_pair(body):
-    def step(pair, carry):
+    for pair in range(SUBLANES // 2):
         body(pair)
-        return carry
-
-    lax.fori_loop(0, SUBLANES // 2, step, 0)
 
 
 class Forward:
@@ -1029,7 +1055,7 @@
         triangle_output.reshape((-1,) + triangle_output.shape[2:]),
         expand_weight,
         reduce_weight,
-        distogram_weight[None],
+        distogram_weight.T[None],
     ]
     count = len(merged)
 
@@ -1198,14 +1224,14 @@
     layers, kinds, width, mixed = weights[2].shape
     hidden = weights[4].shape[2]
     early_in, early_up, early_rows = early
-    given = [rest, *early_in, *early_up, early_rows]
+    given = [rest, *early_in, *early_up, *early_rows]
     count = len(given)
 
     def kernel(*refs):
         whole = refs[0]
         in_refs = refs[1 : 1 + len(early_in)]
-        up_refs = refs[1 + len(early_in) : count - 1]
-        rows_ref = refs[count - 1]
+        up_refs = refs[1 + len(early_in) : count - layers]
+        row_refs = refs[count - layers : count]
         states = [refs[count + 8 * kind : count + 8 * (kind + 1)] for kind in range(3)]
         scalars = refs[count + 24 : count + 27]
         results = refs[count + 27 :]
@@ -1221,14 +1247,14 @@
         loss = jnp.sum(taken(row_starts[0], 1), axis=1, keepdims=True)
         valid = jnp.sum(taken(row_starts[1], 1), axis=1, keepdims=True)
         table_rows, single_rows = weights[0].shape[0], weights[1].shape[0]
-        outs, downs = layers * kinds - 1, hidden // 2
+        downs = hidden // 2
         grads = {}
         grads[0, ()] = taken(starts[4], table_rows)
         grads[1, ()] = jnp.concatenate(
             [taken(starts[5], single_rows), taken(starts[6], single_rows)], axis=1
         )
-        spot = 0
         for layer in range(layers):
+            spot = 0
             for kind in range(kinds):
                 if layer == 0:
                     grads[2, (layer, kind)] = wide(starts[kind], width, mixed // LANES)
@@ -1237,13 +1263,11 @@
                 if layer == 0 and kind == 0:
                     grads[3, (layer, kind)] = taken(starts[2], width)
                 else:
-                    grads[3, (layer, kind)] = rows_ref[pl.ds(spot, width), :]
+                    grads[3, (layer, kind)] = row_refs[layer][pl.ds(spot, width), :]
                     spot += width
-        for layer in range(layers):
             grads[4, (layer,)] = up_refs[layer][...]
-            grads[5, (layer,)] = rows_ref[pl.ds(spot, downs), :]
-            spot += downs
-        grads[6, ()] = taken(starts[3], weights[6].shape[1]).T
+            grads[5, (layer,)] = row_refs[layer][pl.ds(spot, downs), :]
+        grads[6, ()] = taken(starts[3], weights[6].shape[0])
         grads[7, ()] = taken(gain_start, weights[7].shape[0])
         squares = jnp.zeros((1, 1), F32)
         for key in grads:
@@ -1324,7 +1348,7 @@
     prepared = prepare(
         triangle_input, triangle_output, expand_weight, reduce_weight, distogram_weight, norm_gains
     )
-    mix, mix_t, out, out_t, up, up_t, down, down_t, logits, logits_t, gains = prepared
+    mix, mix_t, out, out_t, up, up_t, down, down_t, logits_t, logits, gains = prepared
     hidden = up.shape[2]
 
     def gain(index):
@@ -1400,14 +1424,13 @@
 
     kept, states, middles, tris = {}, {}, {}, {}
 
-    def first_body(i, o, left, right):
-        state = dot(i.table_t[...], bins_hot(i.bins, table_rows))
+    def first_body(i, o, rows, *wires):
+        state = dot(i.table_t[...], bins_hot(i.bins, rows, table_rows))
+        yield
         cols = i.proj_cols[...]
-        state = state + jnp.concatenate(
-            [cols + i.proj_rows[row] for row in range(ROW_BLOCK)], axis=1
-        )
-        write_rows(o.state, state)
-        triangle_start(i.start, read_rows(i.mask), left, right, state)
+        state = state + jnp.concatenate([cols + i.proj_rows[row] for row in rows], axis=1)
+        write_rows(o.state, rows, state)
+        yield from triangle_start(i.start, i, rows, wires, state)
 
     exchange = forward(False)
     got = run_stage(
@@ -1428,17 +1451,19 @@
     )
     kept[0, 0], states[0, 0] = got, got.state
 
-    def between_body(i, o, left, right):
-        state, _ = triangle_finish(i.end, i.tri, read_rows(i.state))
-        write_rows(o.state, state)
-        triangle_start(i.start, read_rows(i.mask), left, right, state)
-
-    def layer_end_body(i, o, left, right):
-        state, _ = triangle_finish(i.end, i.tri, read_rows(i.state))
-        write_rows(o.middle, state)
-        state = transition_finish(i.lift, state, transition(i.lift, state))
-        write_rows(o.state, state)
-        triangle_start(i.start, read_rows(i.mask), left, right, state)
+    def between_body(i, o, rows, *wires):
+        state, _ = yield from triangle_finish(i.end, rows, i.tri, read_rows(i.state, rows))
+        write_rows(o.state, rows, state)
+        yield from triangle_start(i.start, i, rows, wires, state)
+
+    def layer_end_body(i, o, rows, *wires):
+        state, _ = yield from triangle_finish(i.end, rows, i.tri, read_rows(i.state, rows))
+        write_rows(o.middle, rows, state)
+        lifted = yield from transition(i.lift, state)
+        state = state + dot(i.lift.down_t[...], lifted[5])
+        yield
+        write_rows(o.state, rows, state)
+        yield from triangle_start(i.start, i, rows, wires, state)
 
     for layer in range(layers):
         exchange = forward(True)
@@ -1481,13 +1506,17 @@
         kept[layer + 1, 0], states[layer + 1, 0] = got, got.state
         middles[layer] = got.middle
 
-    def loss_body(i, o, sent):
-        state, kept_triangle = triangle_finish(i.end, i.tri, read_rows(i.state))
-        lifted = transition(i.lift, state)
-        grad = head_back(i.head, o.head, transition_finish(i.lift, state, lifted))
-        grad = transition_back(i.lift, o.lift, grad, lifted)
-        write_rows(o.grad, grad)
-        triangle_back_start(i.end, o.end, sent, grad, kept_triangle)
+    def loss_body(i, o, rows, sent):
+        state, kept_triangle = yield from triangle_finish(
+            i.end, rows, i.tri, read_rows(i.state, rows)
+        )
+        lifted = yield from transition(i.lift, state)
+        state = state + dot(i.lift.down_t[...], lifted[5])
+        yield
+        grad = yield from head_back(i.head, o.head, rows, state)
+        grad = yield from transition_back(i.lift, o.lift, grad, lifted)
+        write_rows(o.grad, rows, grad)
+        yield from triangle_back_start(i.end, o.end, rows, sent, grad, kept_triangle)
 
     top = layers - 1
     exchange = backward(True)
@@ -1526,38 +1555,49 @@
     )
     head, lifts, ends, begins = got.head, {top: got.lift}, {(top, 1): got.end}, {}
 
-    def between_back_body(i, o, sent):
-        grad = triangle_back_finish(
-            i.start, i.back, o.start, read_rows(i.mask), read_rows(i.grad), read_rows(i.state)
+    def between_back_body(i, o, rows, sent):
+        grad = yield from triangle_back_finish(i.start, i, o.start, rows)
+        write_rows(o.grad, rows, grad)
+        _, kept_triangle = yield from triangle_finish(
+            i.end, rows, i.tri, read_rows(i.before, rows)
         )
-        write_rows(o.grad, grad)
-        _, kept_triangle = triangle_finish(i.end, i.tri, read_rows(i.before))
-        triangle_back_start(i.end, o.end, sent, grad, kept_triangle)
-
-    def layer_end_back_body(i, o, sent):
-        grad = triangle_back_finish(
-            i.start, i.back, o.start, read_rows(i.mask), read_rows(i.grad), read_rows(i.state)
+        yield from triangle_back_start(i.end, o.end, rows, sent, grad, kept_triangle)
+
+    def layer_end_back_body(i, o, rows, sent):
+        grad = yield from triangle_back_finish(i.start, i, o.start, rows)
+        lifted = yield from transition(i.lift, read_rows(i.middle, rows))
+        grad = yield from transition_back(i.lift, o.lift, grad, lifted)
+        write_rows(o.grad, rows, grad)
+        _, kept_triangle = yield from triangle_finish(
+            i.end, rows, i.tri, read_rows(i.before, rows)
         )
-        grad = transition_back(i.lift, o.lift, grad, transition(i.lift, read_rows(i.middle)))
-        write_rows(o.grad, grad)
-        _, kept_triangle = triangle_finish(i.end, i.tri, read_rows(i.before))
-        triangle_back_start(i.end, o.end, sent, grad, kept_triangle)
-
-    def first_back_body(i, o):
-        grad = triangle_back_finish(
-            i.start, i.back, o.start, read_rows(i.mask), read_rows(i.grad), read_rows(i.state)
-        )
-        hot = bins_hot(i.bins, table_rows)
+        yield from triangle_back_start(i.end, o.end, rows, sent, grad, kept_triangle)
+
+    def first_back_body(i, o, rows):
+        grad = yield from triangle_back_finish(i.start, i, o.start, rows)
+        hot = bins_hot(i.bins, rows, table_rows)
         high = grad.astype(BF16)
         low = (grad - high.astype(F32)).astype(BF16)
         o.table[...] += dot_pairs(hot, high) + dot_pairs(hot, low)
-        for row in range(ROW_BLOCK):
-            part = grad[:, row * tokens : (row + 1) * tokens]
+        yield
+        for place, row in enumerate(rows):
+            part = grad[:, place * tokens : (place + 1) * tokens]
             o.rows[row] = fold(part)
             o.cols[...] += part
 
+    def layer_sums(layer):
+        kinds = (0, 1) if layer else (1,)
+        mixes = [begins[layer, 1].mix] if layer else []
+        if layer + 1 < layers:
+            mixes.append(begins[layer + 1, 0].mix)
+        outs = [ends[layer, kind].out for kind in kinds]
+        return (mixes, lifts[layer].up, jnp.concatenate(outs + [lifts[layer].down], axis=0))
+
+    early = {}
     for layer in reversed(range(layers)):
         for kind in (1, 0):
+            if (layer, kind) == (0, 0):
+                early, got.grad = lax.optimization_barrier((early, got.grad))
             inputs = dict(
                 grad=Arg(got.grad, ROWS),
                 state=Arg(states[layer, kind], ROWS),
@@ -1617,22 +1657,26 @@
             begins[layer, kind], ends[before] = got.start, got.end
             if kind == 0:
                 lifts[layer - 1] = got.lift
-
+            ready = layer if kind == 1 else layer - 1
+            if ready == 0 and kind == 1 or ready > 0 and kind == 0:
+                continue
+            group = layer_sums(ready)
+            if early:
+                group, early, got.grad = lax.optimization_barrier((group, early, got.grad))
+            early[ready] = lax.psum(group, ("row", "head"))
+
+    early_mixes = {}
+    for layer in range(layers):
+        mixes = list(early[layer][0])
+        if layer:
+            early_mixes[layer, 1] = mixes.pop(0)
+        if mixes:
+            early_mixes[layer + 1, 0] = mixes.pop(0)
     early = (
-        [begins[layer, kind].mix for layer in range(1, layers) for kind in range(2)],
-        [lifts[layer].up for layer in range(layers)],
-        jnp.concatenate(
-            [
-                ends[layer, kind].out
-                for layer in range(layers)
-                for kind in range(2)
-                if (layer, kind) != (0, 0)
-            ]
-            + [lifts[layer].down for layer in range(layers)],
-            axis=0,
-        ),
-    )
-    early = lax.psum(early, ("row", "head"))
+        [early_mixes[layer, kind] for layer in range(1, layers) for kind in range(2)],
+        [early[layer][1] for layer in range(layers)],
+        [early[layer][2] for layer in range(layers)],
+    )
 
     wide_single = tokens_single.astype(F32)
     row_part = jnp.einsum(
@@ -1657,10 +1701,14 @@
         row_part,
         col_part,
     ]
+    def turned(arrays):
+        return arrays[:6] + (arrays[6].T,) + arrays[7:]
+
     rest, *starts = reduce_rest(
         half, peers, next(identities), grids, partial_gains, [head.loss, head.count]
     )
-    return update(rest, *starts, early, weights, firsts, seconds)
+    found = update(rest, *starts, early, turned(weights), turned(firsts), turned(seconds))
+    return found[:21] + tuple(value.T for value in found[21:24]) + found[24:]
 
 
 def per_device(

time: 904 us -> 962 us (1.064)
  waiting for transfers between devices: 0.04 us -> 90.8 us
  Pallas kernels: 849 us -> 827 us
    psum x1 -> x2, waiting for transfers between devices: 0.02 us -> 90.8 us  [step_by_crop(): early[ready] = lax.psum(group, ('row', 'head'))]
    pallas_call x9, Pallas kernels: 792 us -> 769 us  [run_stage(): pl.pallas_call(kernel, grid=(steps,), in_specs=[arg.spec() for arg in arg...]
  transfers between devices with their start and end apart: 3 -> 4, of which waited for: 0 -> 2; matrix products, arithmetic and copies ran while one was open for 1% -> 1% of each run, Pallas kernels for 26% -> 22%
where the time goes in v5:
time: 962 us; the launch traced here: 955 us
  Pallas kernels  827 us (86%)
  waiting for transfers between devices  90.8 us (9%)
  between operations  14.8 us (2%)
  other arithmetic  9.8 us (1%)
    pallas_call x9, Pallas kernels, run_stage(): pl.pallas_call(kernel, grid=(steps,), in_specs=[arg.spec() for arg in arg...  769 us
    psum x2, waiting for transfers between devices, step_by_crop(): early[ready] = lax.psum(group, ('row', 'head'))  90.8 us
    pallas_call x1, Pallas kernels, reduce_rest(): pl.pallas_call(kernel, in_specs=[inside] * count, out_specs=inside, out_s...  41.1 us
  transfers between devices with their start and end apart: 4, of which 2 were waited for; matrix products, arithmetic and copies ran while one was open for 1% of the time, Pallas kernels for 22%

profile of v5, /device:TPU:0, one launch (start us, length us, event | category | flops | bytes accessed | tf_op | source)
XLA Modules:
  0.0 954.9 jit_solution(13650310691304116519)
XLA Ops:
  7.3 0.8 fusion.8
  8.2 4.1 collective-permute-start.1
  12.3 0.7 collective-permute-start
  13.0 0.7 fusion.24
  13.7 0.8 convert.4
  14.5 0.1 copy.67
  14.6 0.6 pad_bitcast_fusion.refs_3_
  15.3 1.2 fusion.2
  16.7 0.8 compare_select_fusion.refs_0_
  17.6 0.8 copy.71
  18.4 1.6 copy.68.refs_1_
  20.0 3.8 prepare.1
  23.9 0.7 fusion.13.refs_15_
  24.6 0.8 fusion.12
  25.4 65.8 %first_state.1 = (f32[24,128,384]{2,1,0:T(8,128)}, bf16[8,384,384]{2,1,0:T(8,128)(2,1)}, bf16[8,384,384]{2,1,0:T(8,128)(2,1)}, bf16[16,192,384]{2,1,0:T(8,128)(2,1)}) custom-call(s32[24,1,384]{2,1,0:T(1,128)} %compare_select_fusion.refs_0_, f32[24,128,1]{2,1,0:T(8,128)} %copy.68.refs_1_, f32[128,384]{1,0:T(8,128)} %bitcast.54, ...), custom_call_target="tpu_custom_call" | custom-call | tf_op jit(solution)/shard_map/first_state/pallas_call | solution.py:827
  91.2 90.4 %between_updates.2 = (f32[24,128,384]{2,1,0:T(8,128)}, bf16[16,192,384]{2,1,0:T(8,128)(2,1)}, bf16[8,384,384]{2,1,0:T(8,128)(2,1)}, bf16[8,384,384]{2,1,0:T(8,128)(2,1)}, bf16[16,192,384]{2,1,0:T(8,128)(2,1)}) custom-call(f32[24,128,384]{2,1,0:T(8,128)} %get-tuple-element.146.refs_0_.refs_9_.refs_2_, bf16[16,192,384]{2,1,0:T(8,128)(2,1)} %get-tuple-element.147.refs_1_, ...), custom_call_target="tpu_custom_call" | custom-call | tf_op jit(solution)/shard_map/between_updates/pallas_call | solution.py:827
  181.6 89.9 %layer_end.1 = (f32[24,128,384]{2,1,0:T(8,128)}, f32[24,128,384]{2,1,0:T(8,128)}, bf16[16,192,384]{2,1,0:T(8,128)(2,1)}, bf16[8,384,384]{2,1,0:T(8,128)(2,1)}, b...) custom-call(f32[24,128,384]{2,1,0:T(8,128)} %get-tuple-element.149.refs_0_.refs_9_.refs_1_, ...), custom_call_target="tpu_custom_call" | custom-call | tf_op jit(solution)/shard_map/layer_end/pallas_call | solution.py:827
  271.5 90.0 %between_updates.3 = (f32[24,128,384]{2,1,0:T(8,128)}, bf16[16,192,384]{2,1,0:T(8,128)(2,1)}, bf16[8,384,384]{2,1,0:T(8,128)(2,1)}, bf16[8,384,384]{2,1,0:T(8,128)(2,1)}, bf16[16,192,384]{2,1,0:T(8,128)(2,1)}) custom-call(f32[24,128,384]{2,1,0:T(8,128)} %get-tuple-element.153.refs_0_.refs_9_.refs_1_, bf16[16,192,384]{2,1,0:T(8,128)(2,1)} %get-tuple-element.154.refs_1_, ...), custom_call_target="tpu_custom_call" | custom-call | tf_op jit(solution)/shard_map/between_updates/pallas_call | solution.py:827
  361.5 72.4 %loss.1 = (f32[24,128,384]{2,1,0:T(8,128)}, f32[1,128]{1,0:T(1,128)}, f32[1,128]{1,0:T(1,128)}, f32[64,128]{1,0:T(8,128)}, f32[128,128]{1,0:T(8,128)}, /*index=5...) custom-call(f32[24,128,384]{2,1,0:T(8,128)} %get-tuple-element.155.r, ...), custom_call_target="tpu_custom_call" | custom-call | tf_op jit(solution)/shard_map/loss/pallas_call | solution.py:827
  433.9 92.1 %between_updates_back.2 = (f32[128,640]{1,0:T(8,128)}, f32[128,128]{1,0:T(8,128)}, f32[24,128,384]{2,1,0:T(8,128)}, bf16[24,128,384]{2,1,0:T(8,128)(2,1)}, f32[1...) custom-call(f32[24,128,384]{2,1,0:T(8,128)} %get-tuple-element.164.refs_0_, ...), custom_call_target="tpu_custom_call" | custom-call | tf_op jit(solution)/shard_map/between_updates_back/pallas_call | solution.py:827
  526.1 1.6 pad_maximum_fusion
  527.8 101.8 %layer_end_back.1 = (f32[128,640]{1,0:T(8,128)}, f32[128,128]{1,0:T(8,128)}, f32[24,128,384]{2,1,0:T(8,128)}, bf16[24,128,384]{2,1,0:T(8,128)(2,1)}, f32[128,128...) custom-call(f32[24,128,384]{2,1,0:T(8,128)} %get-tuple-element.172.r, ...), custom_call_target="tpu_custom_call" | custom-call | tf_op jit(solution)/shard_map/layer_end_back/pallas_call | solution.py:827
  629.5 1.7 pad_maximum_fusion.1
  631.2 39.2 %all-reduce.8.cloned.1.call-done = (f32[128,640]{1,0:T(8,128)}, f32[128,1024]{1,0:T(8,128)}, f32[768,128]{1,0:T(8,128)}) async-done(((f32[128,640]{1,0:T(8,128)}, f32[128,1024]{1,0:T(8,128)}, f32[768,128]{1,0:T(8,128)}), (f32[128,640]{1,0:T(8,128)}, f32[128,1024]{1,0:T(8,128)}, f32[768,128]{1,0:T(8,128)})) %all-reduce.8.cloned.1.call-update) | async-done | bytes 1245200 | tf_op jit(solution)/shard_map/psum | solution.py:1666
  670.4 101.4 %between_updates_back.3 = (f32[128,640]{1,0:T(8,128)}, f32[128,128]{1,0:T(8,128)}, f32[24,128,384]{2,1,0:T(8,128)}, bf16[24,128,384]{2,1,0:T(8,128)(2,1)}, f32[1...) custom-call(f32[24,128,384]{2,1,0:T(8,128)} %get-tuple-element.196.refs_0_, ...), custom_call_target="tpu_custom_call" | custom-call | tf_op jit(solution)/shard_map/between_updates_back/pallas_call | solution.py:827
  771.8 51.6 %all-reduce.6.cloned.1.call-done = (f32[128,640]{1,0:T(8,128)}, f32[128,1024]{1,0:T(8,128)}, f32[640,128]{1,0:T(8,128)}) async-done(((f32[128,640]{1,0:T(8,128)}, f32[128,1024]{1,0:T(8,128)}, f32[640,128]{1,0:T(8,128)}), (f32[128,640]{1,0:T(8,128)}, f32[128,1024]{1,0:T(8,128)}, f32[640,128]{1,0:T(8,128)})) %all-reduce.6.cloned.1.call-update) | async-done | bytes 1179664 | tf_op jit(solution)/shard_map/psum | solution.py:1666
  823.4 65.5 %first_state_back.1 = (f32[80,128]{1,0:T(8,128)}, f32[24,128,128]{2,1,0:T(8,128)}, f32[128,384]{1,0:T(8,128)}, f32[128,640]{1,0:T(8,128)}, f32[128,128]{1,0:T(8,128)}) custom-call(s32[24,1,384]{2,1,0:T(1,128)} %compare_select_fusion.refs_0_, f32[24,128,384]{2,1,0:T(8,128)} %get-tuple-element.204.refs_1_, ...), custom_call_target="tpu_custom_call" | custom-call | tf_op jit(solution)/shard_map/first_state_back/pallas_call | solution.py:827
  888.9 1.9 reduce_sum.9
  890.8 1.0 fusion.14.refs_5_
  891.8 2.1 fusion.refs_6_
  893.9 41.1 %reduce_rest.1.refs_0_ = f32[2432,128]{1,0:T(8,128)} custom-call(f32[128,640]{1,0:T(8,128)} %get-tuple-element.208.refs_0_, f32[128,640]{1,0:T(8,128)} %get-tuple-element.209.refs_1_, f32[128,128]{1,0:T(8,128)} %get-tuple-element.210.refs_2_, f32[64,128]{1,0:T(8,128)} %get-tuple-element.211.refs_3_, f32[80,128]{1,0:T(8,128)} %get-tuple-element.212.refs_4_, ...), custom_call_target="tpu_custom_call" | custom-call | tf_op jit(solution)/shard_map/reduce_rest/pallas_call | solution.py:1205
  935.0 12.6 %update.1 = (f32[1,1]{1,0:T(1,128)}, f32[1,1]{1,0:T(1,128)}, f32[1,1]{1,0:T(1,128)}, f32[66,128]{1,0:T(8,128)}, f32[66,128]{1,0:T(8,128)}, /*index=5*/f32[66,128...) custom-call(f32[2432,128]{1,0:T(8,128)} %reduce_rest.1.refs_0_, ...), custom_call_target="tpu_custom_call" | custom-call | tf_op jit(solution)/shard_map/update/pallas_call | solution.py:1298
  (24 shorter events, 0.4 us)
Async XLA Ops:
  7.2 8.1 copy-start
  7.2 9.4 copy-start.3
  7.2 9.4 copy-start.4
  7.2 663.2 %all-reduce.8.cloned.1.call-start = ((), (), s32[]{:S(2)}) async-start(), calls=%async_computation.1 | async-start | bytes 2490368 | tf_op jit(solution)/shard_map/psum | solution.py:1666
  8.2 15.7 %collective-permute-start.1 = (s32[2,24,192]{2,0,1:T(2,128)S(1)}, s32[2,24,192]{2,0,1:T(2,128)S(1)}, u32[]{:S(2)}, u32[]{:S(2)}) collective-permute-start(s32[2,24,192]{2,0,1:T(2,128)S(1)} %bitcast.61), channel_id=1, source_target_pairs={{0,16},{1,0},{2,17},{3,1},{4,20},{5,4},{6,21},{7,5},{8,24},{9,8},{... | collective-permute-start | bytes 110600 | tf_op jit(solution)/shard_map/ppermute | solution.py:1101
  12.3 11.6 %collective-permute-start = (s32[2,24,192]{2,0,1:T(2,128)S(1)}, s32[2,24,192]{2,0,1:T(2,128)S(1)}, u32[]{:S(2)}, u32[]{:S(2)}) collective-permute-start(s32[2,24,192]{2,0,1:T(2,128)S(1)} %bitcast.62), channel_id=1, source_target_pairs={{0,0},{1,16},{2,1},{3,17},{4,4},{5,20},{6,5},{7,21},{8,8},{9,24},{... | collective-permute-start | bytes 110600 | tf_op jit(solution)/shard_map/ppermute | solution.py:1100
  433.9 92.1 %copy-start.1 = (f32[512,128]{1,0:T(8,128)S(1)}, f32[512,128]{1,0:T(8,128)}, u32[]{:S(2)}) copy-start(f32[512,128]{1,0:T(8,128)} %get-tuple-element.188) | copy-start | bytes 786436
  433.9 92.1 %copy-start.2 = (f32[128,128]{1,0:T(8,128)S(1)}, f32[128,128]{1,0:T(8,128)}, u32[]{:S(2)}) copy-start(f32[128,128]{1,0:T(8,128)} %get-tuple-element.187) | copy-start | bytes 196612
  527.7 295.7 %all-reduce.6.cloned.1.call-start = ((), (), s32[]{:S(2)}) async-start(), calls=%async_computation | async-start | bytes 2359296 | tf_op jit(solution)/shard_map/psum | solution.py:1666
Sparse Core Ops, SparseCore 0:
  527.8 142.5 all-reduce.7
  676.7 146.6 all-reduce.5

commit v6 on v5

--- a/solution.py
+++ b/solution.py
@@ -844,9 +844,10 @@
 
 
 def flip(value, step, count):
+    step = jnp.int32(step)
     result, bit = 0, 1
     while bit < count:
-        result = result + lax.rem(lax.div(value, bit) + (step // bit) % 2, 2) * bit
+        result = result + lax.rem(lax.div(value, bit) + lax.div(step, bit), 2) * bit
         bit *= 2
     return result
 
@@ -872,11 +873,17 @@
         self.base = row - place
         self.me = lax.rem(place, 2) * inner + lax.div(place, 2) * (count // half) + head
         self.twin = (lax.rem(row + half, 2 * half), head)
+        core = lax.div(self.me, inner)
         self.order = []
-        for step in range(1, count):
-            for other in (step, step ^ (inner - 1)):
-                if other and other not in self.order:
-                    self.order.append(other)
+        for low in range(inner // 2):
+            for step in (low, low + inner):
+                other = step ^ (inner - 1)
+                for first, second in ((step, other), (other, step)):
+                    if first == 0 or second == 0:
+                        if first:
+                            self.order.append(first)
+                    else:
+                        self.order.append(first + core * (second - first))
 
     def peer(self, step):
         return flip(self.me, step, self.count)
@@ -897,12 +904,12 @@
 
     def copies(self, moves, chunk, steps):
         found = []
-        for step in steps:
-            peer = self.peer(step)
-            for source, target, send_sems, recv_sems in moves:
-                size = source.shape[1] // send_sems.shape[0]
-                rows = pl.ds(pl.multiple_of(chunk * size, PACKED), size)
-                if step == 0:
+        for source, target, send_sems, recv_sems in moves:
+            size = source.shape[1] // send_sems.shape[0]
+            rows = pl.ds(pl.multiple_of(chunk * size, PACKED), size)
+            for step in steps:
+                peer = self.me if step is None else self.peer(step)
+                if step is None:
                     copy = pltpu.make_async_copy(
                         source.at[self.me, rows, :],
                         target.at[self.me, rows, :],
@@ -921,11 +928,11 @@
         return found
 
     def start(self, moves, chunk):
-        for copy in self.copies(moves, chunk, self.order + [0]):
+        for copy in self.copies(moves, chunk, self.order + [None]):
             copy.start()
 
     def wait(self, moves, chunk):
-        for copy in self.copies(moves, chunk, self.order + [0]):
+        for copy in self.copies(moves, chunk, self.order + [None]):
             copy.wait()
 
 
@@ -1593,11 +1600,8 @@
         outs = [ends[layer, kind].out for kind in kinds]
         return (mixes, lifts[layer].up, jnp.concatenate(outs + [lifts[layer].down], axis=0))
 
-    early = {}
     for layer in reversed(range(layers)):
         for kind in (1, 0):
-            if (layer, kind) == (0, 0):
-                early, got.grad = lax.optimization_barrier((early, got.grad))
             inputs = dict(
                 grad=Arg(got.grad, ROWS),
                 state=Arg(states[layer, kind], ROWS),
@@ -1657,14 +1661,8 @@
             begins[layer, kind], ends[before] = got.start, got.end
             if kind == 0:
                 lifts[layer - 1] = got.lift
-            ready = layer if kind == 1 else layer - 1
-            if ready == 0 and kind == 1 or ready > 0 and kind == 0:
-                continue
-            group = layer_sums(ready)
-            if early:
-                group, early, got.grad = lax.optimization_barrier((group, early, got.grad))
-            early[ready] = lax.psum(group, ("row", "head"))
-
+
+    early = lax.psum({layer: layer_sums(layer) for layer in range(layers)}, ("row", "head"))
     early_mixes = {}
     for layer in range(layers):
         mixes = list(early[layer][0])

time: 962 us -> 890 us (0.925)
  waiting for transfers between devices: 90.8 us -> 0.04 us
  Pallas kernels: 827 us -> 844 us
    psum x2 -> x1, waiting for transfers between devices: 90.8 us -> 0.02 us  [step_by_crop(): lax.psum({layer: layer_sums(layer) for layer in range(layers)}, ('row', '...]
    pallas_call x9, Pallas kernels: 769 us -> 787 us  [run_stage(): pl.pallas_call(kernel, grid=(steps,), in_specs=[arg.spec() for arg in arg...]
  transfers between devices with their start and end apart: 4 -> 3, of which waited for: 2 -> 0; matrix products, arithmetic and copies ran while one was open for 1% -> 1% of each run, Pallas kernels for 22% -> 27%
where the time goes in v6:
time: 890 us; the launch traced here: 881 us
  Pallas kernels  844 us (95%)
  between operations  14.8 us (2%)
  other arithmetic  8.96 us (1%)
    pallas_call x9, Pallas kernels, run_stage(): pl.pallas_call(kernel, grid=(steps,), in_specs=[arg.spec() for arg in arg...  787 us
    pallas_call x1, Pallas kernels, reduce_rest(): pl.pallas_call(kernel, in_specs=[inside] * count, out_specs=inside, out_s...  40.8 us
  transfers between devices with their start and end apart: 3, of which 0 were waited for; matrix products, arithmetic and copies ran while one was open for 1% of the time, Pallas kernels for 27%

profile of v6, /device:TPU:0, one launch (start us, length us, event | category | flops | bytes accessed | tf_op | source)
XLA Modules:
  0.0 880.7 jit_solution(7505935226821533745)
XLA Ops:
  7.3 0.8 fusion.8
  8.2 4.1 collective-permute-start.1
  12.3 0.7 collective-permute-start
  13.0 0.7 fusion.24
  13.7 0.8 convert.4
  14.5 0.1 copy.67
  14.6 0.6 pad_bitcast_fusion.refs_3_
  15.3 1.2 fusion.2
  16.6 0.1 dynamic-slice_bitcast_fusion.1
  16.7 0.8 compare_select_fusion.refs_0_
  17.5 0.1 fusion.23
  17.6 0.8 copy.71
  18.4 1.7 copy.68.refs_1_
  20.1 3.8 prepare.1
  23.9 0.7 fusion.13.refs_15_
  24.7 0.8 fusion.12
  25.4 65.6 %first_state.1 = (f32[24,128,384]{2,1,0:T(8,128)}, bf16[8,384,384]{2,1,0:T(8,128)(2,1)}, bf16[8,384,384]{2,1,0:T(8,128)(2,1)}, bf16[16,192,384]{2,1,0:T(8,128)(2,1)}) custom-call(s32[24,1,384]{2,1,0:T(1,128)} %compare_select_fusion.refs_0_, f32[24,128,1]{2,1,0:T(8,128)} %copy.68.refs_1_, f32[128,384]{1,0:T(8,128)} %bitcast.54, ...), custom_call_target="tpu_custom_call" | custom-call | tf_op jit(solution)/shard_map/first_state/pallas_call | solution.py:827
  91.1 90.6 %between_updates.2 = (f32[24,128,384]{2,1,0:T(8,128)}, bf16[16,192,384]{2,1,0:T(8,128)(2,1)}, bf16[8,384,384]{2,1,0:T(8,128)(2,1)}, bf16[8,384,384]{2,1,0:T(8,128)(2,1)}, bf16[16,192,384]{2,1,0:T(8,128)(2,1)}) custom-call(f32[24,128,384]{2,1,0:T(8,128)} %get-tuple-element.132.refs_0_.refs_9_.refs_2_, bf16[16,192,384]{2,1,0:T(8,128)(2,1)} %get-tuple-element.133.refs_1_, ...), custom_call_target="tpu_custom_call" | custom-call | tf_op jit(solution)/shard_map/between_updates/pallas_call | solution.py:827
  181.7 90.1 %layer_end.1 = (f32[24,128,384]{2,1,0:T(8,128)}, f32[24,128,384]{2,1,0:T(8,128)}, bf16[16,192,384]{2,1,0:T(8,128)(2,1)}, bf16[8,384,384]{2,1,0:T(8,128)(2,1)}, b...) custom-call(f32[24,128,384]{2,1,0:T(8,128)} %get-tuple-element.135.refs_0_.refs_9_.refs_1_, ...), custom_call_target="tpu_custom_call" | custom-call | tf_op jit(solution)/shard_map/layer_end/pallas_call | solution.py:827
  271.8 89.9 %between_updates.3 = (f32[24,128,384]{2,1,0:T(8,128)}, bf16[16,192,384]{2,1,0:T(8,128)(2,1)}, bf16[8,384,384]{2,1,0:T(8,128)(2,1)}, bf16[8,384,384]{2,1,0:T(8,128)(2,1)}, bf16[16,192,384]{2,1,0:T(8,128)(2,1)}) custom-call(f32[24,128,384]{2,1,0:T(8,128)} %get-tuple-element.139.refs_0_.refs_9_.refs_1_, bf16[16,192,384]{2,1,0:T(8,128)(2,1)} %get-tuple-element.140.refs_1_, ...), custom_call_target="tpu_custom_call" | custom-call | tf_op jit(solution)/shard_map/between_updates/pallas_call | solution.py:827
  361.7 73.2 %loss.1 = (f32[24,128,384]{2,1,0:T(8,128)}, f32[1,128]{1,0:T(1,128)}, f32[1,128]{1,0:T(1,128)}, f32[64,128]{1,0:T(8,128)}, f32[128,128]{1,0:T(8,128)}, /*index=5...) custom-call(f32[24,128,384]{2,1,0:T(8,128)} %get-tuple-element.141.r, ...), custom_call_target="tpu_custom_call" | custom-call | tf_op jit(solution)/shard_map/loss/pallas_call | solution.py:827
  434.9 93.5 %between_updates_back.2 = (f32[128,640]{1,0:T(8,128)}, f32[128,128]{1,0:T(8,128)}, f32[24,128,384]{2,1,0:T(8,128)}, bf16[24,128,384]{2,1,0:T(8,128)(2,1)}, f32[1...) custom-call(f32[24,128,384]{2,1,0:T(8,128)} %get-tuple-element.150.refs_0_, ...), custom_call_target="tpu_custom_call" | custom-call | tf_op jit(solution)/shard_map/between_updates_back/pallas_call | solution.py:827
  528.5 93.3 %layer_end_back.1 = (f32[128,640]{1,0:T(8,128)}, f32[128,128]{1,0:T(8,128)}, f32[24,128,384]{2,1,0:T(8,128)}, bf16[24,128,384]{2,1,0:T(8,128)(2,1)}, f32[128,128...) custom-call(f32[24,128,384]{2,1,0:T(8,128)} %get-tuple-element.158.r, ...), custom_call_target="tpu_custom_call" | custom-call | tf_op jit(solution)/shard_map/layer_end_back/pallas_call | solution.py:827
  621.9 1.7 pad_maximum_fusion.1
  623.6 0.8 pad_maximum_fusion
  624.4 108.3 %between_updates_back.3 = (f32[128,640]{1,0:T(8,128)}, f32[128,128]{1,0:T(8,128)}, f32[24,128,384]{2,1,0:T(8,128)}, bf16[24,128,384]{2,1,0:T(8,128)(2,1)}, f32[1...) custom-call(f32[24,128,384]{2,1,0:T(8,128)} %get-tuple-element.166.refs_0_, ...), custom_call_target="tpu_custom_call" | custom-call | tf_op jit(solution)/shard_map/between_updates_back/pallas_call | solution.py:827
  732.6 82.4 %first_state_back.1 = (f32[80,128]{1,0:T(8,128)}, f32[24,128,128]{2,1,0:T(8,128)}, f32[128,384]{1,0:T(8,128)}, f32[128,640]{1,0:T(8,128)}, f32[128,128]{1,0:T(8,128)}) custom-call(s32[24,1,384]{2,1,0:T(1,128)} %compare_select_fusion.refs_0_, f32[24,128,384]{2,1,0:T(8,128)} %get-tuple-element.173.refs_1_, ...), custom_call_target="tpu_custom_call" | custom-call | tf_op jit(solution)/shard_map/first_state_back/pallas_call | solution.py:827
  815.1 1.9 reduce_sum.9
  817.0 1.0 fusion.14.refs_5_
  818.0 2.1 fusion.refs_6_
  820.0 40.8 %reduce_rest.1.refs_0_ = f32[2432,128]{1,0:T(8,128)} custom-call(f32[128,640]{1,0:T(8,128)} %get-tuple-element.177.refs_0_, f32[128,640]{1,0:T(8,128)} %get-tuple-element.178.refs_1_, f32[128,128]{1,0:T(8,128)} %get-tuple-element.179.refs_2_, f32[64,128]{1,0:T(8,128)} %get-tuple-element.180.refs_3_, f32[80,128]{1,0:T(8,128)} %get-tuple-element.181.refs_4_, ...), custom_call_target="tpu_custom_call" | custom-call | tf_op jit(solution)/shard_map/reduce_rest/pallas_call | solution.py:1212
  860.8 12.6 %update.1 = (f32[1,1]{1,0:T(1,128)}, f32[1,1]{1,0:T(1,128)}, f32[1,1]{1,0:T(1,128)}, f32[66,128]{1,0:T(8,128)}, f32[66,128]{1,0:T(8,128)}, /*index=5*/f32[66,128...) custom-call(f32[2432,128]{1,0:T(8,128)} %reduce_rest.1.refs_0_, ...), custom_call_target="tpu_custom_call" | custom-call | tf_op jit(solution)/shard_map/update/pallas_call | solution.py:1305
  (23 shorter events, 0.2 us)
Async XLA Ops:
  7.2 8.1 copy-start
  7.2 9.4 %copy-start.4 = (s32[2,384]{1,0:T(2,128)S(1)}, s32[2,384]{1,0:T(2,128)}, u32[]{:S(2)}) copy-start(s32[2,384]{1,0:T(2,128)} %param.32) | copy-start | bytes 9220
  7.2 9.4 %copy-start.5 = (s32[2,384]{1,0:T(2,128)S(1)}, s32[2,384]{1,0:T(2,128)}, u32[]{:S(2)}) copy-start(s32[2,384]{1,0:T(2,128)} %param.31) | copy-start | bytes 9220
  7.2 853.6 %all-reduce.4.cloned.1.call-start = ((), (), s32[]{:S(2)}) async-start(), calls=%async_computation | async-start | bytes 4849664 | tf_op jit(solution)/shard_map/psum | solution.py:1665
  8.2 15.7 %collective-permute-start.1 = (s32[2,24,192]{2,0,1:T(2,128)S(1)}, s32[2,24,192]{2,0,1:T(2,128)S(1)}, u32[]{:S(2)}, u32[]{:S(2)}) collective-permute-start(s32[2,24,192]{2,0,1:T(2,128)S(1)} %bitcast.61), channel_id=1, source_target_pairs={{0,16},{1,0},{2,17},{3,1},{4,20},{5,4},{6,21},{7,5},{8,24},{9,8},{... | collective-permute-start | bytes 110600 | tf_op jit(solution)/shard_map/ppermute | solution.py:1108
  12.3 11.6 %collective-permute-start = (s32[2,24,192]{2,0,1:T(2,128)S(1)}, s32[2,24,192]{2,0,1:T(2,128)S(1)}, u32[]{:S(2)}, u32[]{:S(2)}) collective-permute-start(s32[2,24,192]{2,0,1:T(2,128)S(1)} %bitcast.62), channel_id=1, source_target_pairs={{0,0},{1,16},{2,1},{3,17},{4,4},{5,20},{6,5},{7,21},{8,8},{9,24},{... | collective-permute-start | bytes 110600 | tf_op jit(solution)/shard_map/ppermute | solution.py:1107
  528.5 95.1 %copy-start.1 = (f32[512,128]{1,0:T(8,128)S(1)}, f32[512,128]{1,0:T(8,128)}, u32[]{:S(2)}) copy-start(f32[512,128]{1,0:T(8,128)} %get-tuple-element.205) | copy-start | bytes 786436
  528.5 95.1 %copy-start.2 = (f32[128,128]{1,0:T(8,128)S(1)}, f32[128,128]{1,0:T(8,128)}, u32[]{:S(2)}) copy-start(f32[128,128]{1,0:T(8,128)} %get-tuple-element.204) | copy-start | bytes 196612
  528.5 95.1 %copy-start.3 = (f32[128,128]{1,0:T(8,128)S(1)}, f32[128,128]{1,0:T(8,128)}, u32[]{:S(2)}) copy-start(f32[128,128]{1,0:T(8,128)} %get-tuple-element.203) | copy-start | bytes 196612
Sparse Core Ops, SparseCore 0:
  624.5 166.3 all-reduce.3

commit v7 on v6

--- a/solution.py
+++ b/solution.py
@@ -396,7 +396,7 @@
 CHUNK_ROWS = SUBLANES * SUBLANES
 VMEM_BYTES = 58 * 2**20
 MESH = pl.DeviceIdType.MESH
-ROWS, WIRE, LANDED, WHOLE, SUM, ANYWHERE = range(6)
+ROWS, LANDED, WHOLE, SUM, ANYWHERE = range(5)
 
 
 class Bag:
@@ -405,9 +405,9 @@
 
 
 class Arg:
-    def __init__(self, array, kind, index=None, block=None, column=None, half=None):
+    def __init__(self, array, kind, index=None, block=None, column=None):
         self.array, self.kind, self.index, self.block = array, kind, index, block
-        self.column, self.half = column, half
+        self.column = column
 
     def spec(self):
         if self.index is None:
@@ -433,7 +433,7 @@
 
 
 def block_spec(shape, kind):
-    if kind in (WIRE, ANYWHERE):
+    if kind == ANYWHERE:
         return pl.BlockSpec(memory_space=pl.ANY)
     if kind == LANDED:
         return pl.BlockSpec((shape[0], CHUNK_ROWS, shape[2]), lambda step: (0, step // PHASES, 0))
@@ -447,18 +447,19 @@
 
 
 def bag_of(tree, leaves):
-    return Bag(
-        **{
-            key: next(leaves) if is_leaf(value) else bag_of(value, leaves)
-            for key, value in tree.items()
-        }
-    )
+    if is_leaf(tree):
+        return next(leaves)
+    if isinstance(tree, list):
+        return [bag_of(value, leaves) for value in tree]
+    return Bag(**{key: bag_of(value, leaves) for key, value in tree.items()})
 
 
 def leaves_of(tree):
+    if is_leaf(tree):
+        return [tree]
     found = []
-    for value in tree.values():
-        found.extend([value] if is_leaf(value) else leaves_of(value))
+    for value in tree if isinstance(tree, list) else tree.values():
+        found.extend(leaves_of(value))
     return found
 
 
@@ -607,7 +608,7 @@
     wire.write(rows, unit_back(grad_shaped, tri_unit, tri_scale, weights.gain1[...]))
 
 
-def triangle_back_finish(weights, i, o, rows):
+def triangle_back_finish(weights, i, o, rows, wires):
     grad, state = read_rows(i.grad, rows), read_rows(i.state, rows)
     width = state.shape[0]
     unit, scale = unit_of(state)
@@ -617,13 +618,13 @@
     yield
     mask = read_rows(i.mask, rows)
     parts = []
-    for wire, base in ((i.back.grad_left, 0), (i.back.grad_right, 2 * width)):
+    for wire, base in zip(wires, (0, 2 * width)):
         back = wire.read(rows) * mask
         gate = sigmoid(mixed[base : base + width])
         back_gate = back * gate
         parts.append((back_gate * mixed[base + width : base + 2 * width] * (1.0 - gate)).astype(BF16))
         parts.append(back_gate.astype(BF16))
-    parts.append(read_rows(i.back.grad_gate, rows))
+    parts.append(read_rows(i.grad_gate, rows))
     grad_mixed = jnp.concatenate(parts, axis=0)
     yield
     grad_normed = dot(weights.mix[...], grad_mixed)
@@ -700,28 +701,25 @@
     return jnp.where(lax.broadcasted_iota(jnp.int32, shape, 0) == bins, 1.0, 0.0).astype(BF16)
 
 
-def run_stage(body, name, collective_id, rows, inputs, outputs, exchange=None):
+def run_stage(body, name, collective_id, group, inputs, outputs, products=None, wires=0):
+    peers, half, rows, tokens = group
     args, outs = leaves_of(inputs), leaves_of(outputs)
     steps = rows // ROW_BLOCK
     chunks = rows // SUBLANES
-    wire_args = [index for index, arg in enumerate(args) if arg.kind == WIRE]
+    arriving = products.results if products else 0
     landed_args = [index for index, arg in enumerate(args) if arg.kind == LANDED]
     keeps = [place for place, out in enumerate(outs) if out.kind == LANDED]
-    wires = exchange.wires if exchange else 0
-    if wire_args:
-        peers, half, tokens = args[wire_args[0]].array.shape[0], args[wire_args[0]].half, 0
-        tokens = args[wire_args[0]].array.shape[2]
-    if exchange:
-        peers, half, tokens = exchange.peers, exchange.half, exchange.tokens
     low = pltpu.VMEM((peers, rows * SUBLANES, tokens), BF16)
     many = pltpu.SemaphoreType.DMA((chunks, peers))
     wide = pltpu.VMEM((tokens // LANES, peers * CHUNK_ROWS, LANES), F32)
     groups = [
-        [wide] * (len(wire_args) + len(landed_args) + wires),
-        [low] * len(wire_args),
-        [many] * (2 * len(wire_args)),
+        [wide] * (arriving + len(landed_args) + wires),
+        [low] * arriving,
+        [many] * (2 * arriving),
+        [low] * wires,
+        [many] * (2 * wires),
         [pltpu.SemaphoreType.DMA((1,))] * len(keeps),
-        exchange.scratch() if exchange else [],
+        products.scratch(low) if products else [],
     ]
 
     def kernel(*refs):
@@ -732,30 +730,31 @@
         ]
         out_refs = list(refs[len(args) : len(args) + len(outs)])
         rest, parts = list(refs[len(args) + len(outs) :]), []
-        for group in groups:
-            parts.append(rest[: len(group)])
-            rest = rest[len(group) :]
-        wides, lands, sems, keep_sems, held = parts
+        for part in groups:
+            parts.append(rest[: len(part)])
+            rest = rest[len(part) :]
+        wides, lands, land_sems, sends, send_sems, keep_sems, held = parts
         saves = [
             pltpu.make_async_copy(land, out_refs[place], sem.at[0])
             for land, place, sem in zip(lands, keeps, keep_sems)
         ]
         ring = Exchange(peers, half)
+        i, o = bag_of(inputs, iter(in_refs)), bag_of(outputs, iter(out_refs))
         arrivals = [
-            (in_refs[index], land, sems[2 * place], sems[2 * place + 1])
-            for place, (index, land) in enumerate(zip(wire_args, lands))
+            (result, land, land_sems[2 * place], land_sems[2 * place + 1])
+            for place, (result, land) in enumerate(zip(held, lands))
         ]
-        i, o = bag_of(inputs, iter(in_refs)), bag_of(outputs, iter(out_refs))
 
         @pl.when(step == 0)
         def _():
             ring.greet()
+            if products:
+                products.load(i, held)
             for out, ref in zip(outs, out_refs):
                 if out.kind == SUM:
                     ref[...] = jnp.zeros(out.shape, out.dtype)
-            if exchange:
-                exchange.begin(i, held)
-            if arrivals:
+            if products:
+                products.multiply(i, o, held)
                 ring.meet()
 
                 def start(index, carry):
@@ -764,7 +763,7 @@
 
                 lax.fori_loop(0, chunks, start, 0)
 
-        if arrivals:
+        if products:
 
             @pl.when(phase == 0)
             def _():
@@ -776,7 +775,7 @@
 
             @pl.when(phase == 0)
             def _():
-                for target, index in zip(wides[len(wire_args) :], landed_args):
+                for target, index in zip(wides[arriving:], landed_args):
                     widen(target, in_refs[index], 0)
 
         if saves:
@@ -787,25 +786,29 @@
                     save.start()
 
         body_in = list(in_refs)
-        for index, source in zip(wire_args + landed_args, wides):
+        for index, source in zip(landed_args, wides[arriving:]):
             body_in[index] = Wire(source, phase)
-        sent = wides[len(wire_args) + len(landed_args) :]
         given = bag_of(inputs, iter(body_in))
-        out_wires = [Wire(target, phase) for target in sent]
+        arrived = [Wire(source, phase) for source in wides[:arriving]]
+        written = wides[arriving + len(landed_args) :]
+        sent = [Wire(target, phase) for target in written]
         alternate(
             [
-                body(given, o, range(first, first + STREAM_ROWS), *out_wires)
+                body(given, o, range(first, first + STREAM_ROWS), arrived, sent)
                 for first in range(0, ROW_BLOCK, STREAM_ROWS)
             ]
         )
-        if exchange:
-            moves = exchange.moves(held)
+        moves = [
+            (send, land, send_sems[2 * place], send_sems[2 * place + 1])
+            for place, (send, land) in enumerate(zip(sends, o.got if wires else []))
+        ]
+        if wires:
 
             @pl.when(phase == PHASES - 1)
             def _():
-                for source, move in zip(sent, moves):
-                    narrow(move[0], source, chunk)
-                if not arrivals:
+                for source, send in zip(written, sends):
+                    narrow(send, source, chunk)
+                if not products:
 
                     @pl.when(chunk == 0)
                     def _():
@@ -813,16 +816,19 @@
 
                 ring.start(moves, chunk)
 
-            @pl.when(step == steps - 1)
-            def _():
+        @pl.when(step == steps - 1)
+        def _():
+            if wires:
+
                 def wait(index, carry):
                     ring.wait(moves, index)
                     return carry
 
                 lax.fori_loop(0, chunks, wait, 0)
-                exchange.finish(i, o, held)
-                for save in saves:
-                    save.wait()
+            for save in saves:
+                save.wait()
+            if products:
+                products.end(o, held)
 
     results = pl.pallas_call(
         kernel,
@@ -964,96 +970,98 @@
 
 
 class Forward:
-    wires = 2
-
-    def __init__(self, peers, half, rows, tokens, incoming):
-        self.peers, self.half, self.incoming = peers, half, incoming
-        self.rows, self.tokens = rows * SUBLANES, tokens
-        self.chunks = rows // SUBLANES
-
-    def outs(self):
-        block = (SUBLANES, self.tokens, self.tokens)
-        return dict(
-            left=Out(block, BF16, WHOLE),
-            right=Out(block, BF16, WHOLE),
-            tri=Out((self.peers, self.rows, self.tokens), BF16, WHOLE),
-        )
-
-    def scratch(self):
-        low = pltpu.VMEM((self.peers, self.rows, self.tokens), BF16)
-        many = pltpu.SemaphoreType.DMA((self.chunks, self.peers))
-        return [low] * 4 + [many] * 4
-
-    def moves(self, held):
-        return [(held[0], held[2], held[4], held[5]), (held[1], held[3], held[6], held[7])]
-
-    def begin(self, i, held):
-        pass
-
-    def finish(self, i, o, held):
+    results = 1
+
+    def __init__(self, tokens, incoming):
+        self.tokens, self.incoming = tokens, incoming
+
+    def scratch(self, low):
+        block = pltpu.VMEM((SUBLANES, self.tokens, self.tokens), BF16)
+        return [low] * 3 + [block] * 2 + [pltpu.SemaphoreType.DMA((4,))]
+
+    def loads(self, i, held):
+        return [
+            pltpu.make_async_copy(i.got[place], held[1 + place], held[5].at[place])
+            for place in range(2)
+        ]
+
+    def saves(self, o, held):
+        return [
+            pltpu.make_async_copy(held[3], o.left, held[5].at[2]),
+            pltpu.make_async_copy(held[4], o.right, held[5].at[3]),
+        ]
+
+    def load(self, i, held):
+        for copy in self.loads(i, held):
+            copy.start()
+
+    def multiply(self, i, o, held):
+        tri, left_got, right_got, left_block, right_block = held[:5]
+        for copy in self.loads(i, held):
+            copy.wait()
         axis = 0 if self.incoming else 1
 
         def step(pair):
-            lefts, rights = join_channels(held[2], pair), join_channels(held[3], pair)
+            lefts, rights = join_channels(left_got, pair), join_channels(right_got, pair)
             found = []
             for index in range(2):
-                o.left[2 * pair + index] = lefts[index]
-                o.right[2 * pair + index] = rights[index]
+                left_block[2 * pair + index] = lefts[index]
+                right_block[2 * pair + index] = rights[index]
                 found.append(product_of(lefts[index], rights[index], axis, axis))
-            split_channels(o.tri, pair, *found)
+            split_channels(tri, pair, *found)
 
         each_pair(step)
+        for copy in self.saves(o, held):
+            copy.start()
+
+    def end(self, o, held):
+        for copy in self.saves(o, held):
+            copy.wait()
 
 
 class Backward:
-    wires = 1
-
-    def __init__(self, peers, half, rows, tokens, incoming):
-        self.peers, self.half, self.incoming = peers, half, incoming
-        self.rows, self.tokens = rows * SUBLANES, tokens
-        self.chunks = rows // SUBLANES
-
-    def outs(self):
-        wire = (self.peers, self.rows, self.tokens)
-        return dict(grad_left=Out(wire, BF16, WHOLE), grad_right=Out(wire, BF16, WHOLE))
-
-    def scratch(self):
-        low = pltpu.VMEM((self.peers, self.rows, self.tokens), BF16)
+    results = 2
+
+    def __init__(self, tokens, incoming):
+        self.tokens, self.incoming = tokens, incoming
+
+    def scratch(self, low):
         block = pltpu.VMEM((SUBLANES, self.tokens, self.tokens), BF16)
-        many = pltpu.SemaphoreType.DMA((self.chunks, self.peers))
-        return [low] * 2 + [block] * 2 + [many] * 2 + [pltpu.SemaphoreType.DMA((2,))]
-
-    def moves(self, held):
-        return [(held[0], held[1], held[4], held[5])]
-
-    def owned(self, i, held):
+        return [low] * 3 + [block] * 2 + [pltpu.SemaphoreType.DMA((3,))]
+
+    def loads(self, i, held):
+        sources = (i.got[0], i.owned.left, i.owned.right)
         return [
-            pltpu.make_async_copy(i.owned.left, held[2], held[6].at[0]),
-            pltpu.make_async_copy(i.owned.right, held[3], held[6].at[1]),
+            pltpu.make_async_copy(source, held[2 + place], held[5].at[place])
+            for place, source in enumerate(sources)
         ]
 
-    def begin(self, i, held):
-        for copy in self.owned(i, held):
+    def load(self, i, held):
+        for copy in self.loads(i, held):
             copy.start()
 
-    def finish(self, i, o, held):
-        for copy in self.owned(i, held):
+    def multiply(self, i, o, held):
+        grad_left, grad_right, got, left_block, right_block = held[:5]
+        for copy in self.loads(i, held):
             copy.wait()
 
         def step(pair):
             lefts, rights = [], []
-            for index, grad in enumerate(join_channels(held[1], pair)):
-                left, right = held[2][2 * pair + index], held[3][2 * pair + index]
+            for index, grad in enumerate(join_channels(got, pair)):
+                left, right = left_block[2 * pair + index], right_block[2 * pair + index]
                 if self.incoming:
                     lefts.append(product_of(right, grad, 1, 1))
                     rights.append(product_of(left, grad, 1, 0))
                 else:
                     lefts.append(product_of(grad, right, 1, 0))
                     rights.append(product_of(grad, left, 0, 0))
-            split_channels(o.grad_left, pair, *lefts)
-            split_channels(o.grad_right, pair, *rights)
+            split_channels(grad_left, pair, *lefts)
+            split_channels(grad_right, pair, *rights)
 
         each_pair(step)
+
+    def end(self, o, held):
+        pass
 
 
 def prepare(triangle_input, triangle_output, expand_weight, reduce_weight, distogram_weight, norm_gains):
@@ -1414,14 +1422,14 @@
 
     identities = iter(range(4 * layers + 2))
 
-    def forward(incoming):
-        return Forward(peers, half, rows, tokens, incoming)
-
-    def backward(incoming):
-        return Backward(peers, half, rows, tokens, incoming)
-
-    def wire(array):
-        return Arg(array, WIRE, half=half)
+    group = (peers, half, rows, tokens)
+    block_out = Out((SUBLANES, tokens, tokens), BF16, ANYWHERE)
+
+    def got_out(count):
+        return [Out((peers, rows * SUBLANES, tokens), BF16, ANYWHERE)] * count
+
+    def got_in(stage):
+        return [Arg(array, ANYWHERE) for array in stage.got]
 
     def landed_out():
         return Out((peers, rows * SUBLANES, tokens), BF16, LANDED)
@@ -1431,20 +1439,19 @@
 
     kept, states, middles, tris = {}, {}, {}, {}
 
-    def first_body(i, o, rows, *wires):
+    def first_body(i, o, rows, arrived, sent):
         state = dot(i.table_t[...], bins_hot(i.bins, rows, table_rows))
         yield
         cols = i.proj_cols[...]
         state = state + jnp.concatenate([cols + i.proj_rows[row] for row in rows], axis=1)
         write_rows(o.state, rows, state)
-        yield from triangle_start(i.start, i, rows, wires, state)
-
-    exchange = forward(False)
+        yield from triangle_start(i.start, i, rows, sent, state)
+
     got = run_stage(
         first_body,
         "first_state",
         next(identities),
-            rows,
+        group,
         dict(
             bins=bins,
             proj_rows=Arg(proj_rows, ROWS),
@@ -1453,69 +1460,85 @@
             mask=pair_mask,
             start=triangle_weights(0, 0, starts=True),
         ),
-        dict(state=state_out(), **exchange.outs()),
-        exchange,
-    )
-    kept[0, 0], states[0, 0] = got, got.state
-
-    def between_body(i, o, rows, *wires):
-        state, _ = yield from triangle_finish(i.end, rows, i.tri, read_rows(i.state, rows))
+        dict(state=state_out(), got=got_out(2)),
+        wires=2,
+    )
+    states[0, 0] = got.state
+
+    def between_body(i, o, rows, arrived, sent):
+        state, _ = yield from triangle_finish(
+            i.end, rows, arrived[0], read_rows(i.state, rows)
+        )
         write_rows(o.state, rows, state)
-        yield from triangle_start(i.start, i, rows, wires, state)
-
-    def layer_end_body(i, o, rows, *wires):
-        state, _ = yield from triangle_finish(i.end, rows, i.tri, read_rows(i.state, rows))
+        yield from triangle_start(i.start, i, rows, sent, state)
+
+    def layer_end_body(i, o, rows, arrived, sent):
+        state, _ = yield from triangle_finish(
+            i.end, rows, arrived[0], read_rows(i.state, rows)
+        )
         write_rows(o.middle, rows, state)
         lifted = yield from transition(i.lift, state)
         state = state + dot(i.lift.down_t[...], lifted[5])
         yield
         write_rows(o.state, rows, state)
-        yield from triangle_start(i.start, i, rows, wires, state)
+        yield from triangle_start(i.start, i, rows, sent, state)
 
     for layer in range(layers):
-        exchange = forward(True)
         got = run_stage(
             between_body,
             "between_updates",
             next(identities),
-            rows,
+            group,
             dict(
+                got=got_in(got),
                 state=Arg(states[layer, 0], ROWS),
-                tri=wire(kept[layer, 0].tri),
                 mask=pair_mask,
                 end=triangle_weights(layer, 0, finishes=True),
                 start=triangle_weights(layer, 1, starts=True),
             ),
-            dict(state=state_out(), landed=landed_out(), **exchange.outs()),
-            exchange,
+            dict(
+                state=state_out(),
+                landed=landed_out(),
+                left=block_out,
+                right=block_out,
+                got=got_out(2),
+            ),
+            Forward(tokens, False),
+            wires=2,
         )
-        kept[layer, 1], states[layer, 1], tris[layer, 0] = got, got.state, got.landed
+        kept[layer, 0], states[layer, 1], tris[layer, 0] = got, got.state, got.landed
         if layer + 1 == layers:
             break
-        exchange = forward(False)
         got = run_stage(
             layer_end_body,
             "layer_end",
             next(identities),
-            rows,
+            group,
             dict(
+                got=got_in(got),
                 state=Arg(states[layer, 1], ROWS),
-                tri=wire(kept[layer, 1].tri),
                 mask=pair_mask,
                 end=triangle_weights(layer, 1, finishes=True),
                 lift=transition_weights(layer),
                 start=triangle_weights(layer + 1, 0, starts=True),
             ),
-            dict(middle=state_out(), state=state_out(), landed=landed_out(), **exchange.outs()),
-            exchange,
+            dict(
+                middle=state_out(),
+                state=state_out(),
+                landed=landed_out(),
+                left=block_out,
+                right=block_out,
+                got=got_out(2),
+            ),
+            Forward(tokens, True),
+            wires=2,
         )
-        tris[layer, 1] = got.landed
-        kept[layer + 1, 0], states[layer + 1, 0] = got, got.state
+        kept[layer, 1], states[layer + 1, 0], tris[layer, 1] = got, got.state, got.landed
         middles[layer] = got.middle
 
-    def loss_body(i, o, rows, sent):
+    def loss_body(i, o, rows, arrived, sent):
         state, kept_triangle = yield from triangle_finish(
-            i.end, rows, i.tri, read_rows(i.state, rows)
+            i.end, rows, arrived[0], read_rows(i.state, rows)
         )
         lifted = yield from transition(i.lift, state)
         state = state + dot(i.lift.down_t[...], lifted[5])
@@ -1523,18 +1546,17 @@
         grad = yield from head_back(i.head, o.head, rows, state)
         grad = yield from transition_back(i.lift, o.lift, grad, lifted)
         write_rows(o.grad, rows, grad)
-        yield from triangle_back_start(i.end, o.end, rows, sent, grad, kept_triangle)
+        yield from triangle_back_start(i.end, o.end, rows, sent[0], grad, kept_triangle)
 
     top = layers - 1
-    exchange = backward(True)
     got = run_stage(
         loss_body,
         "loss",
         next(identities),
-            rows,
+        group,
         dict(
+            got=got_in(got),
             state=Arg(states[top, 1], ROWS),
-            tri=wire(kept[top, 1].tri),
             end=triangle_weights(top, 1, finishes=True, back=True),
             lift=transition_weights(top, back=True),
             head=dict(
@@ -1544,7 +1566,6 @@
                 target=Arg(target[:, None, :], ROWS),
                 weight=Arg(loss_weight[:, None, :], ROWS),
             ),
-            owned=owned(kept[top, 1]),
         ),
         dict(
             grad=state_out(),
@@ -1556,32 +1577,36 @@
             ),
             lift=transition_outs(),
             end=back_start_outs(),
-            **exchange.outs(),
+            left=block_out,
+            right=block_out,
+            got=got_out(1),
         ),
-        exchange,
-    )
+        Forward(tokens, True),
+        wires=1,
+    )
+    kept[top, 1] = got
     head, lifts, ends, begins = got.head, {top: got.lift}, {(top, 1): got.end}, {}
 
-    def between_back_body(i, o, rows, sent):
-        grad = yield from triangle_back_finish(i.start, i, o.start, rows)
+    def between_back_body(i, o, rows, arrived, sent):
+        grad = yield from triangle_back_finish(i.start, i, o.start, rows, arrived)
         write_rows(o.grad, rows, grad)
         _, kept_triangle = yield from triangle_finish(
             i.end, rows, i.tri, read_rows(i.before, rows)
         )
-        yield from triangle_back_start(i.end, o.end, rows, sent, grad, kept_triangle)
-
-    def layer_end_back_body(i, o, rows, sent):
-        grad = yield from triangle_back_finish(i.start, i, o.start, rows)
+        yield from triangle_back_start(i.end, o.end, rows, sent[0], grad, kept_triangle)
+
+    def layer_end_back_body(i, o, rows, arrived, sent):
+        grad = yield from triangle_back_finish(i.start, i, o.start, rows, arrived)
         lifted = yield from transition(i.lift, read_rows(i.middle, rows))
         grad = yield from transition_back(i.lift, o.lift, grad, lifted)
         write_rows(o.grad, rows, grad)
         _, kept_triangle = yield from triangle_finish(
             i.end, rows, i.tri, read_rows(i.before, rows)
         )
-        yield from triangle_back_start(i.end, o.end, rows, sent, grad, kept_triangle)
-
-    def first_back_body(i, o, rows):
-        grad = yield from triangle_back_finish(i.start, i, o.start, rows)
+        yield from triangle_back_start(i.end, o.end, rows, sent[0], grad, kept_triangle)
+
+    def first_back_body(i, o, rows, arrived, sent):
+        grad = yield from triangle_back_finish(i.start, i, o.start, rows, arrived)
         hot = bins_hot(i.bins, rows, table_rows)
         high = grad.astype(BF16)
         low = (grad - high.astype(F32)).astype(BF16)
@@ -1603,23 +1628,22 @@
     for layer in reversed(range(layers)):
         for kind in (1, 0):
             inputs = dict(
+                got=got_in(got),
+                owned=owned(kept[layer, kind]),
                 grad=Arg(got.grad, ROWS),
+                grad_gate=Arg(got.end.grad_gate, ROWS),
                 state=Arg(states[layer, kind], ROWS),
                 mask=pair_mask,
                 start=triangle_weights(layer, kind, starts=True, back=True),
-                back=dict(
-                    grad_left=wire(got.grad_left),
-                    grad_right=wire(got.grad_right),
-                    grad_gate=Arg(got.end.grad_gate, ROWS),
-                ),
             )
             outputs = dict(start=back_finish_outs())
+            products = Backward(tokens, kind == 1)
             if layer == 0 and kind == 0:
                 got = run_stage(
                     first_back_body,
                     "first_state_back",
                     next(identities),
-            rows,
+                    group,
                     dict(bins=bins, **inputs),
                     dict(
                         table=sum_out(table_rows, width),
@@ -1627,6 +1651,7 @@
                         cols=sum_out(width, tokens),
                         **outputs,
                     ),
+                    products,
                 )
                 begins[layer, kind] = got.start
                 break
@@ -1635,14 +1660,11 @@
                 before=Arg(states[before], ROWS),
                 tri=Arg(tris[before], LANDED),
                 end=triangle_weights(*before, finishes=True, back=True),
-                owned=owned(kept[before]),
             )
-            outputs.update(grad=state_out(), end=back_start_outs())
+            outputs.update(grad=state_out(), end=back_start_outs(), got=got_out(1))
             if kind == 1:
-                exchange = backward(False)
                 body, name = between_back_body, "between_updates_back"
             else:
-                exchange = backward(True)
                 body, name = layer_end_back_body, "layer_end_back"
                 inputs.update(
                     middle=Arg(middles[layer - 1], ROWS),
@@ -1650,13 +1672,7 @@
                 )
                 outputs.update(lift=transition_outs())
             got = run_stage(
-                body,
-                name,
-                next(identities),
-                rows,
-                inputs,
-                dict(**outputs, **exchange.outs()),
-                exchange,
+                body, name, next(identities), group, inputs, outputs, products, wires=1
             )
             begins[layer, kind], ends[before] = got.start, got.end
             if kind == 0:

time: 890 us -> 888 us (level)
  no operation moved by 1% of the time
where the time goes in v7:
time: 888 us; the launch traced here: 880 us
  Pallas kernels  843 us (95%)
  between operations  14.8 us (2%)
  other arithmetic  8.96 us (1%)
    pallas_call x9, Pallas kernels, run_stage(): pl.pallas_call(kernel, grid=(steps,), in_specs=[arg.spec() for arg in arg...  784 us
    pallas_call x1, Pallas kernels, reduce_rest(): pl.pallas_call(kernel, in_specs=[inside] * count, out_specs=inside, out_s...  43.2 us
  transfers between devices with their start and end apart: 3, of which 0 were waited for; matrix products, arithmetic and copies ran while one was open for 1% of the time, Pallas kernels for 27%

profile of v7, /device:TPU:0, one launch (start us, length us, event | category | flops | bytes accessed | tf_op | source)
XLA Modules:
  0.0 879.7 jit_solution(8170790348638428734)
XLA Ops:
  7.3 0.8 fusion.8
  8.2 4.1 collective-permute-start.1
  12.3 0.7 collective-permute-start
  13.0 0.7 fusion.24
  13.7 0.8 convert.4
  14.5 0.1 copy.67
  14.6 0.6 pad_bitcast_fusion.refs_3_
  15.3 1.2 fusion.2
  16.6 0.1 dynamic-slice_bitcast_fusion.1
  16.7 0.8 compare_select_fusion.refs_0_
  17.5 0.1 fusion.23
  17.6 0.8 copy.71
  18.4 1.7 copy.68.refs_1_
  20.1 3.8 prepare.1
  23.9 0.7 fusion.13.refs_16_
  24.7 0.8 fusion.12
  25.4 61.8 %first_state.1 = (f32[24,128,384]{2,1,0:T(8,128)}, bf16[16,192,384]{2,1,0:T(8,128)(2,1)}, bf16[16,192,384]{2,1,0:T(8,128)(2,1)}) custom-call(s32[24,1,384]{2,1,0:T(1,128)} %compare_select_fusion.refs_0_, f32[24,128,1]{2,1,0:T(8,128)} %copy.68.refs_1_, f32[128,384]{1,0:T(8,128)} %bitcast.54, bf16[128,80]{1,0:T(8,128)(2,1)} %pad_bitcast_fusion.refs_3_, ...), custom_call_target="tpu_custom_call" | custom-call | tf_op jit(solution)/shard_map/first_state/pallas_call | solution.py:833
  87.3 89.6 %between_updates.2 = (f32[24,128,384]{2,1,0:T(8,128)}, bf16[16,192,384]{2,1,0:T(8,128)(2,1)}, bf16[8,384,384]{2,1,0:T(8,128)(2,1)}, bf16[8,384,384]{2,1,0:T(8,12...) custom-call(bf16[16,192,384]{2,1,0:T(8,128)(2,1)} %get-tuple-element.132.refs_0_, ...), custom_call_target="tpu_custom_call" | custom-call | tf_op jit(solution)/shard_map/between_updates/pallas_call | solution.py:833
  176.8 87.8 %layer_end.1 = (f32[24,128,384]{2,1,0:T(8,128)}, f32[24,128,384]{2,1,0:T(8,128)}, bf16[16,192,384]{2,1,0:T(8,128)(2,1)}, bf16[8,384,384]{2,1,0:T(8,128)(2,1)}, b...) custom-call(bf16[16,192,384]{2,1,0:T(8,128)(2,1)} %get-tuple-element.136.refs_0_, ...), custom_call_target="tpu_custom_call" | custom-call | tf_op jit(solution)/shard_map/layer_end/pallas_call | solution.py:833
  264.7 91.6 %between_updates.3 = (f32[24,128,384]{2,1,0:T(8,128)}, bf16[16,192,384]{2,1,0:T(8,128)(2,1)}, bf16[8,384,384]{2,1,0:T(8,128)(2,1)}, bf16[8,384,384]{2,1,0:T(8,12...) custom-call(bf16[16,192,384]{2,1,0:T(8,128)(2,1)} %get-tuple-element.141.refs_0_, ...), custom_call_target="tpu_custom_call" | custom-call | tf_op jit(solution)/shard_map/between_updates/pallas_call | solution.py:833
  356.3 74.1 %loss.1 = (f32[24,128,384]{2,1,0:T(8,128)}, f32[1,128]{1,0:T(1,128)}, f32[1,128]{1,0:T(1,128)}, f32[64,128]{1,0:T(8,128)}, f32[128,128]{1,0:T(8,128)}, /*index=5...) custom-call(bf16[16,192,384]{2,1,0:T(8,128)(2,1)} %get-tuple-element, ...), custom_call_target="tpu_custom_call" | custom-call | tf_op jit(solution)/shard_map/loss/pallas_call | solution.py:833
  430.5 94.0 %between_updates_back.2 = (f32[128,640]{1,0:T(8,128)}, f32[128,128]{1,0:T(8,128)}, f32[24,128,384]{2,1,0:T(8,128)}, bf16[24,128,384]{2,1,0:T(8,128)(2,1)}, f32[1...) custom-call(bf16[16,192,384]{2,1,0:T(8,128)(2,1)} %get-tuple-element.152.refs_0_, ...), custom_call_target="tpu_custom_call" | custom-call | tf_op jit(solution)/shard_map/between_updates_back/pallas_call | solution.py:833
  524.5 95.0 %layer_end_back.1 = (f32[128,640]{1,0:T(8,128)}, f32[128,128]{1,0:T(8,128)}, f32[24,128,384]{2,1,0:T(8,128)}, bf16[24,128,384]{2,1,0:T(8,128)(2,1)}, f32[128,128...) custom-call(bf16[16,192,384]{2,1,0:T(8,128)(2,1)} %get-tuple-element, ...), custom_call_target="tpu_custom_call" | custom-call | tf_op jit(solution)/shard_map/layer_end_back/pallas_call | solution.py:833
  619.6 1.7 pad_maximum_fusion.1
  621.3 0.8 pad_maximum_fusion
  622.1 107.6 %between_updates_back.3 = (f32[128,640]{1,0:T(8,128)}, f32[128,128]{1,0:T(8,128)}, f32[24,128,384]{2,1,0:T(8,128)}, bf16[24,128,384]{2,1,0:T(8,128)(2,1)}, f32[1...) custom-call(bf16[16,192,384]{2,1,0:T(8,128)(2,1)} %get-tuple-element.166.refs_0_, ...), custom_call_target="tpu_custom_call" | custom-call | tf_op jit(solution)/shard_map/between_updates_back/pallas_call | solution.py:833
  729.7 81.9 %first_state_back.1 = (f32[80,128]{1,0:T(8,128)}, f32[24,128,128]{2,1,0:T(8,128)}, f32[128,384]{1,0:T(8,128)}, f32[128,640]{1,0:T(8,128)}, f32[128,128]{1,0:T(8,128)}) custom-call(s32[24,1,384]{2,1,0:T(1,128)} %compare_select_fusion.refs_0_, bf16[16,192,384]{2,1,0:T(8,128)(2,1)} %get-tuple-element.172.refs_1_, ...), custom_call_target="tpu_custom_call" | custom-call | tf_op jit(solution)/shard_map/first_state_back/pallas_call | solution.py:833
  811.7 1.9 reduce_sum.9
  813.5 1.0 fusion.14.refs_5_
  814.5 2.1 fusion.refs_6_
  816.6 43.2 %reduce_rest.1.refs_0_ = f32[2432,128]{1,0:T(8,128)} custom-call(f32[128,640]{1,0:T(8,128)} %get-tuple-element.177.refs_0_, f32[128,640]{1,0:T(8,128)} %get-tuple-element.178.refs_1_, f32[128,128]{1,0:T(8,128)} %get-tuple-element.179.refs_2_, f32[64,128]{1,0:T(8,128)} %get-tuple-element.180.refs_3_, f32[80,128]{1,0:T(8,128)} %get-tuple-element.181.refs_4_, ...), custom_call_target="tpu_custom_call" | custom-call | tf_op jit(solution)/shard_map/reduce_rest/pallas_call | solution.py:1220
  859.9 12.6 %update.1 = (f32[1,1]{1,0:T(1,128)}, f32[1,1]{1,0:T(1,128)}, f32[1,1]{1,0:T(1,128)}, f32[66,128]{1,0:T(8,128)}, f32[66,128]{1,0:T(8,128)}, /*index=5*/f32[66,128...) custom-call(f32[2432,128]{1,0:T(8,128)} %reduce_rest.1.refs_0_, ...), custom_call_target="tpu_custom_call" | custom-call | tf_op jit(solution)/shard_map/update/pallas_call | solution.py:1313
  (23 shorter events, 0.2 us)
Async XLA Ops:
  7.2 8.1 copy-start
  7.2 9.4 %copy-start.4 = (s32[2,384]{1,0:T(2,128)S(1)}, s32[2,384]{1,0:T(2,128)}, u32[]{:S(2)}) copy-start(s32[2,384]{1,0:T(2,128)} %param.32) | copy-start | bytes 9220
  7.2 9.4 %copy-start.5 = (s32[2,384]{1,0:T(2,128)S(1)}, s32[2,384]{1,0:T(2,128)}, u32[]{:S(2)}) copy-start(s32[2,384]{1,0:T(2,128)} %param.31) | copy-start | bytes 9220
  7.2 852.6 %all-reduce.4.cloned.1.call-start = ((), (), s32[]{:S(2)}) async-start(), calls=%async_computation | async-start | bytes 4849664 | tf_op jit(solution)/shard_map/psum | solution.py:1681
  8.2 15.7 %collective-permute-start.1 = (s32[2,24,192]{2,0,1:T(2,128)S(1)}, s32[2,24,192]{2,0,1:T(2,128)S(1)}, u32[]{:S(2)}, u32[]{:S(2)}) collective-permute-start(s32[2,24,192]{2,0,1:T(2,128)S(1)} %bitcast.61), channel_id=1, source_target_pairs={{0,16},{1,0},{2,17},{3,1},{4,20},{5,4},{6,21},{7,5},{8,24},{9,8},{... | collective-permute-start | bytes 110600 | tf_op jit(solution)/shard_map/ppermute | solution.py:1116
  12.3 11.6 %collective-permute-start = (s32[2,24,192]{2,0,1:T(2,128)S(1)}, s32[2,24,192]{2,0,1:T(2,128)S(1)}, u32[]{:S(2)}, u32[]{:S(2)}) collective-permute-start(s32[2,24,192]{2,0,1:T(2,128)S(1)} %bitcast.62), channel_id=1, source_target_pairs={{0,0},{1,16},{2,1},{3,17},{4,4},{5,20},{6,5},{7,21},{8,8},{9,24},{... | collective-permute-start | bytes 110600 | tf_op jit(solution)/shard_map/ppermute | solution.py:1115
  524.5 96.8 %copy-start.1 = (f32[512,128]{1,0:T(8,128)S(1)}, f32[512,128]{1,0:T(8,128)}, u32[]{:S(2)}) copy-start(f32[512,128]{1,0:T(8,128)} %get-tuple-element.205) | copy-start | bytes 786436
  524.5 96.8 %copy-start.2 = (f32[128,128]{1,0:T(8,128)S(1)}, f32[128,128]{1,0:T(8,128)}, u32[]{:S(2)}) copy-start(f32[128,128]{1,0:T(8,128)} %get-tuple-element.204) | copy-start | bytes 196612
  524.5 96.8 %copy-start.3 = (f32[128,128]{1,0:T(8,128)S(1)}, f32[128,128]{1,0:T(8,128)}, u32[]{:S(2)}) copy-start(f32[128,128]{1,0:T(8,128)} %get-tuple-element.203) | copy-start | bytes 196612
Sparse Core Ops, SparseCore 0:
  622.2 167.9 all-reduce.3

commit v8 on v7

--- a/solution.py
+++ b/solution.py
@@ -395,6 +395,8 @@
 PHASES = SUBLANES // ROW_BLOCK
 CHUNK_ROWS = SUBLANES * SUBLANES
 VMEM_BYTES = 58 * 2**20
+UPDATE_BYTES = 40 * 2**20
+REDUCE_BYTES = 16 * 2**20
 MESH = pl.DeviceIdType.MESH
 ROWS, LANDED, WHOLE, SUM, ANYWHERE = range(5)
 
@@ -1227,7 +1229,7 @@
         + [pltpu.SemaphoreType.DMA((peers,))] * 4
         + [pltpu.SemaphoreType.DMA((2,))],
         compiler_params=pltpu.CompilerParams(
-            collective_id=collective_id, has_side_effects=True, vmem_limit_bytes=VMEM_BYTES
+            collective_id=collective_id, has_side_effects=True, vmem_limit_bytes=REDUCE_BYTES
         ),
         cost_estimate=pl.CostEstimate(flops=0, bytes_accessed=0, transcendentals=0),
         name="reduce_rest",
@@ -1313,7 +1315,7 @@
     found = pl.pallas_call(
         kernel,
         out_shape=shapes,
-        compiler_params=pltpu.CompilerParams(vmem_limit_bytes=VMEM_BYTES),
+        compiler_params=pltpu.CompilerParams(vmem_limit_bytes=UPDATE_BYTES),
         name="update",
     )(*given, *weights, *firsts, *seconds)
     return tuple(value[0, 0] for value in found[:3]) + tuple(found[3:])
@@ -1627,6 +1629,9 @@
 
     for layer in reversed(range(layers)):
         for kind in (1, 0):
+            if (layer, kind) == (0, 0):
+                first = lax.psum(layer_sums(top), ("row", "head"))
+                first, got.grad = lax.optimization_barrier((first, got.grad))
             inputs = dict(
                 got=got_in(got),
                 owned=owned(kept[layer, kind]),
@@ -1678,7 +1683,9 @@
             if kind == 0:
                 lifts[layer - 1] = got.lift
 
-    early = lax.psum({layer: layer_sums(layer) for layer in range(layers)}, ("row", "head"))
+    early = {layer: layer_sums(layer) for layer in range(top)}
+    early = lax.psum(early, ("head", "row"))
+    early[top] = first
     early_mixes = {}
     for layer in range(layers):
         mixes = list(early[layer][0])

time: 888 us -> 917 us (1.033)
  local copies, waits for them, and re-layouts: 3.58 us -> 44.1 us
  Pallas kernels: 843 us -> 829 us
    unnamed x13 -> x107, local copies, waits for them, and re-layouts: 0.84 us -> 41.3 us
  transfers between devices with their start and end apart: 3 -> 4, of which waited for: 0 -> 0; matrix products, arithmetic and copies ran while one was open for 1% -> 1% of each run, Pallas kernels for 27% -> 35%
where the time goes in v8:
time: 917 us; the launch traced here: 906 us
  Pallas kernels  829 us (90%)
  local copies, waits for them, and re-layouts  44.1 us (5%)
  between operations  15 us (2%)
  other arithmetic  9.84 us (1%)
    pallas_call x9, Pallas kernels, run_stage(): pl.pallas_call(kernel, grid=(steps,), in_specs=[arg.spec() for arg in arg...  777 us
    unnamed x107, local copies, waits for them, and re-layouts  41.3 us
    pallas_call x1, Pallas kernels, reduce_rest(): pl.pallas_call(kernel, in_specs=[inside] * count, out_specs=inside, out_s...  40.2 us
  transfers between devices with their start and end apart: 4, of which 0 were waited for; matrix products, arithmetic and copies ran while one was open for 1% of the time, Pallas kernels for 35%

profile of v8, /device:TPU:0, one launch (start us, length us, event | category | flops | bytes accessed | tf_op | source)
XLA Modules:
  0.0 905.6 jit_solution(4833041672944128988)
XLA Ops:
  8.2 4.1 collective-permute-start.1
  15.3 1.2 fusion.2
  18.4 1.7 copy.68.refs_1_
  20.1 3.8 prepare.1
  25.4 61.8 %first_state.1 = (f32[24,128,384]{2,1,0:T(8,128)}, bf16[16,192,384]{2,1,0:T(8,128)(2,1)}, bf16[16,192,384]{2,1,0:T(8,128)(2,1)}) custom-call(s32[24,1,384]{2,1,0:T(1,128)} %compare_select_fusion.refs_0_, f32[24,128,1]{2,1,0:T(8,128)} %copy.68.refs_1_, f32[128,384]{1,0:T(8,128)} %bitcast.58, bf16[128,80]{1,0:T(8,128)(2,1)} %pad_bitcast_fusion.refs_3_, ...), custom_call_target="tpu_custom_call" | custom-call | tf_op jit(solution)/shard_map/first_state/pallas_call | solution.py:835
  87.3 89.5 %between_updates.2 = (f32[24,128,384]{2,1,0:T(8,128)}, bf16[16,192,384]{2,1,0:T(8,128)(2,1)}, bf16[8,384,384]{2,1,0:T(8,128)(2,1)}, bf16[8,384,384]{2,1,0:T(8,12...) custom-call(bf16[16,192,384]{2,1,0:T(8,128)(2,1)} %get-tuple-element.136.refs_0_, ...), custom_call_target="tpu_custom_call" | custom-call | tf_op jit(solution)/shard_map/between_updates/pallas_call | solution.py:835
  176.8 87.9 %layer_end.1 = (f32[24,128,384]{2,1,0:T(8,128)}, f32[24,128,384]{2,1,0:T(8,128)}, bf16[16,192,384]{2,1,0:T(8,128)(2,1)}, bf16[8,384,384]{2,1,0:T(8,128)(2,1)}, b...) custom-call(bf16[16,192,384]{2,1,0:T(8,128)(2,1)} %get-tuple-element.140.refs_0_, ...), custom_call_target="tpu_custom_call" | custom-call | tf_op jit(solution)/shard_map/layer_end/pallas_call | solution.py:835
  264.6 91.6 %between_updates.3 = (f32[24,128,384]{2,1,0:T(8,128)}, bf16[16,192,384]{2,1,0:T(8,128)(2,1)}, bf16[8,384,384]{2,1,0:T(8,128)(2,1)}, bf16[8,384,384]{2,1,0:T(8,12...) custom-call(bf16[16,192,384]{2,1,0:T(8,128)(2,1)} %get-tuple-element.145.refs_0_, ...), custom_call_target="tpu_custom_call" | custom-call | tf_op jit(solution)/shard_map/between_updates/pallas_call | solution.py:835
  356.3 74.2 %loss.1 = (f32[24,128,384]{2,1,0:T(8,128)}, f32[1,128]{1,0:T(1,128)}, f32[1,128]{1,0:T(1,128)}, f32[64,128]{1,0:T(8,128)}, f32[128,128]{1,0:T(8,128)}, /*index=5...) custom-call(bf16[16,192,384]{2,1,0:T(8,128)(2,1)} %get-tuple-element, ...), custom_call_target="tpu_custom_call" | custom-call | tf_op jit(solution)/shard_map/loss/pallas_call | solution.py:835
  430.5 96.3 %between_updates_back.2 = (f32[128,640]{1,0:T(8,128)}, f32[128,128]{1,0:T(8,128)}, f32[24,128,384]{2,1,0:T(8,128)}, bf16[24,128,384]{2,1,0:T(8,128)(2,1)}, f32[1...) custom-call(bf16[16,192,384]{2,1,0:T(8,128)(2,1)} %get-tuple-element.156.refs_0_, ...), custom_call_target="tpu_custom_call" | custom-call | tf_op jit(solution)/shard_map/between_updates_back/pallas_call | solution.py:835
  526.9 1.6 pad_maximum_fusion
  528.5 99.3 %layer_end_back.1 = (f32[128,640]{1,0:T(8,128)}, f32[128,128]{1,0:T(8,128)}, f32[24,128,384]{2,1,0:T(8,128)}, bf16[24,128,384]{2,1,0:T(8,128)(2,1)}, f32[128,128...) custom-call(bf16[16,192,384]{2,1,0:T(8,128)(2,1)} %get-tuple-element, ...), custom_call_target="tpu_custom_call" | custom-call | tf_op jit(solution)/shard_map/layer_end_back/pallas_call | solution.py:835
  627.9 1.7 pad_maximum_fusion.1
  629.6 106.0 %between_updates_back.3 = (f32[128,640]{1,0:T(8,128)}, f32[128,128]{1,0:T(8,128)}, f32[24,128,384]{2,1,0:T(8,128)}, bf16[24,128,384]{2,1,0:T(8,128)(2,1)}, f32[1...) custom-call(bf16[16,192,384]{2,1,0:T(8,128)(2,1)} %get-tuple-element.170.refs_0_, ...), custom_call_target="tpu_custom_call" | custom-call | tf_op jit(solution)/shard_map/between_updates_back/pallas_call | solution.py:835
  735.6 70.7 %first_state_back.1 = (f32[80,128]{1,0:T(8,128)}, f32[24,128,128]{2,1,0:T(8,128)}, f32[128,384]{1,0:T(8,128)}, f32[128,640]{1,0:T(8,128)}, f32[128,128]{1,0:T(8,128)}) custom-call(s32[24,1,384]{2,1,0:T(1,128)} %compare_select_fusion.refs_0_, bf16[16,192,384]{2,1,0:T(8,128)(2,1)} %get-tuple-element.176.refs_1_, ...), custom_call_target="tpu_custom_call" | custom-call | tf_op jit(solution)/shard_map/first_state_back/pallas_call | solution.py:835
  806.3 1.9 reduce_sum.9
  808.6 1.6 fusion.refs_6_
  823.8 40.2 %reduce_rest.1.refs_0_ = f32[2432,128]{1,0:T(8,128)S(1)} custom-call(f32[128,640]{1,0:T(8,128)S(1)} %copy-done.18, f32[128,640]{1,0:T(8,128)S(1)} %copy-done.17, f32[128,128]{1,0:T(8,128)S(1)} %copy-done.35, f32[64,128]{1,0:T(8,128)S(1)} %copy-done.43, f32[80,128]{1,0:T(8,128)S(1)} %copy-done.38, f32[384,128]{1,0:T(8,128)S(1)} %fusion.14.refs_5_, ...), custom_call_target="tpu_custom_call" | custom-call | tf_op jit(solution)/shard_map/reduce_rest/pallas_call | solution.py:1222
  864.1 1.2 copy-done.2
  865.3 1.0 copy-done.3
  866.3 1.3 copy-done.5
  867.6 1.3 copy-done.6
  869.9 1.2 copy-done.8
  871.1 1.2 copy-done.9
  872.4 1.0 copy-done.10
  873.4 1.0 copy-done.11
  874.4 1.0 copy-done.12
  875.5 1.0 copy-done.13
  876.5 1.0 copy-done.14
  877.5 1.0 copy-done.15
  878.5 1.0 copy-done.16
  891.0 7.3 update.1
  (120 shorter events, 33.6 us)
Async XLA Ops:
  7.2 8.1 copy-start
  7.2 9.4 %copy-start.51 = (s32[2,384]{1,0:T(2,128)S(1)}, s32[2,384]{1,0:T(2,128)}, u32[]{:S(2)}) copy-start(s32[2,384]{1,0:T(2,128)} %param.32) | copy-start | bytes 9220
  7.2 9.4 %copy-start.52 = (s32[2,384]{1,0:T(2,128)S(1)}, s32[2,384]{1,0:T(2,128)}, u32[]{:S(2)}) copy-start(s32[2,384]{1,0:T(2,128)} %param.31) | copy-start | bytes 9220
  7.2 728.4 %all-reduce.6.cloned.1.call-start = ((), (), s32[]{:S(2)}) async-start(), calls=%async_computation | async-start | bytes 2490368 | tf_op jit(solution)/shard_map/psum | solution.py:1633
  8.2 15.7 %collective-permute-start.1 = (s32[2,24,192]{2,0,1:T(2,128)S(1)}, s32[2,24,192]{2,0,1:T(2,128)S(1)}, u32[]{:S(2)}, u32[]{:S(2)}) collective-permute-start(s32[2,24,192]{2,0,1:T(2,128)S(1)} %bitcast.63), channel_id=1, source_target_pairs={{0,16},{1,0},{2,17},{3,1},{4,20},{5,4},{6,21},{7,5},{8,24},{9,8},{... | collective-permute-start | bytes 110600 | tf_op jit(solution)/shard_map/ppermute | solution.py:1118
  12.3 11.6 %collective-permute-start = (s32[2,24,192]{2,0,1:T(2,128)S(1)}, s32[2,24,192]{2,0,1:T(2,128)S(1)}, u32[]{:S(2)}, u32[]{:S(2)}) collective-permute-start(s32[2,24,192]{2,0,1:T(2,128)S(1)} %bitcast.64), channel_id=1, source_target_pairs={{0,0},{1,16},{2,1},{3,17},{4,4},{5,20},{6,5},{7,21},{8,8},{9,24},{... | collective-permute-start | bytes 110600 | tf_op jit(solution)/shard_map/ppermute | solution.py:1117
  430.5 96.4 %copy-start.49 = (f32[512,128]{1,0:T(8,128)S(1)}, f32[512,128]{1,0:T(8,128)}, u32[]{:S(2)}) copy-start(f32[512,128]{1,0:T(8,128)} %get-tuple-element.183) | copy-start | bytes 786436
  430.5 96.4 %copy-start.50 = (f32[128,128]{1,0:T(8,128)S(1)}, f32[128,128]{1,0:T(8,128)}, u32[]{:S(2)}) copy-start(f32[128,128]{1,0:T(8,128)} %get-tuple-element.182) | copy-start | bytes 196612
  528.5 335.5 %all-reduce.8.cloned.1.call-start = ((), (), s32[]{:S(2)}) async-start(), calls=%async_computation.1 | async-start | bytes 2359296 | tf_op jit(solution)/shard_map/psum | solution.py:1687
  806.3 3.9 copy-start.47
  806.3 3.9 copy-start.48
  808.3 55.8 %copy-start.1 = (f32[2,2,128,640]{3,2,1,0:T(8,128)S(1)}, f32[2,2,128,640]{3,2,1,0:T(8,128)}, u32[]{:S(2)}) copy-start(f32[2,2,128,640]{3,2,1,0:T(8,128)} %refs_9_.1) | copy-start | bytes 3932164
  808.3 55.7 %copy-start.4 = (f32[384,256]{1,0:T(8,128)S(1)}, f32[384,256]{1,0:T(8,128)}, u32[]{:S(2)}) copy-start(f32[384,256]{1,0:T(8,128)} %refs_8_.1) | copy-start | bytes 1179652
  810.2 1.0 copy-start.17
  811.2 1.0 copy-start.18
  864.0 1.2 copy-start.2
  865.3 1.0 copy-start.3
  866.3 1.3 copy-start.5
  867.6 1.3 copy-start.6
  868.9 0.9 copy-start.7
  869.9 1.2 copy-start.8
  871.1 1.2 copy-start.9
  872.4 1.0 copy-start.10
  873.4 1.0 copy-start.11
  874.4 1.0 copy-start.12
  875.5 1.0 copy-start.13
  876.5 1.0 copy-start.14
  877.5 1.0 copy-start.15
  878.5 1.0 copy-start.16
  879.5 1.0 copy-start.19
  880.5 1.0 copy-start.20
  881.5 1.0 copy-start.21
  (25 other events, 20.2 us)
Sparse Core Ops, SparseCore 0:
  528.6 147.4 all-reduce.5
  682.5 149.9 all-reduce.7

commit v9 on v8

--- a/solution.py
+++ b/solution.py
@@ -395,8 +395,8 @@
 PHASES = SUBLANES // ROW_BLOCK
 CHUNK_ROWS = SUBLANES * SUBLANES
 VMEM_BYTES = 58 * 2**20
-UPDATE_BYTES = 40 * 2**20
-REDUCE_BYTES = 16 * 2**20
+UPDATE_BYTES = VMEM_BYTES
+REDUCE_BYTES = VMEM_BYTES
 MESH = pl.DeviceIdType.MESH
 ROWS, LANDED, WHOLE, SUM, ANYWHERE = range(5)
 

time: 917 us -> 888 us (0.968)
  local copies, waits for them, and re-layouts: 44.1 us -> 3.57 us
  Pallas kernels: 829 us -> 843 us
    unnamed x107 -> x11, local copies, waits for them, and re-layouts: 41.3 us -> 0.84 us
  transfers between devices with their start and end apart: 4 -> 4, of which waited for: 0 -> 0; matrix products, arithmetic and copies ran while one was open for 1% -> 2% of each run, Pallas kernels for 35% -> 38%
where the time goes in v9:
time: 888 us; the launch traced here: 880 us
  Pallas kernels  843 us (95%)
  between operations  14.8 us (2%)
  other arithmetic  9.84 us (1%)
    pallas_call x9, Pallas kernels, run_stage(): pl.pallas_call(kernel, grid=(steps,), in_specs=[arg.spec() for arg in arg...  780 us
    pallas_call x1, Pallas kernels, reduce_rest(): pl.pallas_call(kernel, in_specs=[inside] * count, out_specs=inside, out_s...  46.2 us
  transfers between devices with their start and end apart: 4, of which 0 were waited for; matrix products, arithmetic and copies ran while one was open for 2% of the time, Pallas kernels for 38%

profile of v9, /device:TPU:0, one launch (start us, length us, event | category | flops | bytes accessed | tf_op | source)
XLA Modules:
  0.0 880.3 jit_solution(549516868405316825)
XLA Ops:
  7.3 0.8 fusion.8
  8.2 4.1 collective-permute-start.1
  12.3 0.7 collective-permute-start
  13.0 0.7 fusion.24
  13.7 0.8 convert.4
  14.5 0.1 copy.67
  14.6 0.6 pad_bitcast_fusion.refs_3_
  15.3 1.2 fusion.2
  16.6 0.1 dynamic-slice_bitcast_fusion.1
  16.7 0.8 compare_select_fusion.refs_0_
  17.5 0.1 fusion.23
  17.6 0.8 copy.71
  18.4 1.7 copy.68.refs_1_
  20.1 3.8 prepare.1
  23.9 0.7 fusion.13.refs_16_
  24.7 0.8 fusion.12
  25.4 61.8 %first_state.1 = (f32[24,128,384]{2,1,0:T(8,128)}, bf16[16,192,384]{2,1,0:T(8,128)(2,1)}, bf16[16,192,384]{2,1,0:T(8,128)(2,1)}) custom-call(s32[24,1,384]{2,1,0:T(1,128)} %compare_select_fusion.refs_0_, f32[24,128,1]{2,1,0:T(8,128)} %copy.68.refs_1_, f32[128,384]{1,0:T(8,128)} %bitcast.54, bf16[128,80]{1,0:T(8,128)(2,1)} %pad_bitcast_fusion.refs_3_, ...), custom_call_target="tpu_custom_call" | custom-call | tf_op jit(solution)/shard_map/first_state/pallas_call | solution.py:835
  87.2 89.4 %between_updates.2 = (f32[24,128,384]{2,1,0:T(8,128)}, bf16[16,192,384]{2,1,0:T(8,128)(2,1)}, bf16[8,384,384]{2,1,0:T(8,128)(2,1)}, bf16[8,384,384]{2,1,0:T(8,12...) custom-call(bf16[16,192,384]{2,1,0:T(8,128)(2,1)} %get-tuple-element.136.refs_0_, ...), custom_call_target="tpu_custom_call" | custom-call | tf_op jit(solution)/shard_map/between_updates/pallas_call | solution.py:835
  176.7 87.9 %layer_end.1 = (f32[24,128,384]{2,1,0:T(8,128)}, f32[24,128,384]{2,1,0:T(8,128)}, bf16[16,192,384]{2,1,0:T(8,128)(2,1)}, bf16[8,384,384]{2,1,0:T(8,128)(2,1)}, b...) custom-call(bf16[16,192,384]{2,1,0:T(8,128)(2,1)} %get-tuple-element.140.refs_0_, ...), custom_call_target="tpu_custom_call" | custom-call | tf_op jit(solution)/shard_map/layer_end/pallas_call | solution.py:835
  264.6 91.7 %between_updates.3 = (f32[24,128,384]{2,1,0:T(8,128)}, bf16[16,192,384]{2,1,0:T(8,128)(2,1)}, bf16[8,384,384]{2,1,0:T(8,128)(2,1)}, bf16[8,384,384]{2,1,0:T(8,12...) custom-call(bf16[16,192,384]{2,1,0:T(8,128)(2,1)} %get-tuple-element.145.refs_0_, ...), custom_call_target="tpu_custom_call" | custom-call | tf_op jit(solution)/shard_map/between_updates/pallas_call | solution.py:835
  356.3 74.5 %loss.1 = (f32[24,128,384]{2,1,0:T(8,128)}, f32[1,128]{1,0:T(1,128)}, f32[1,128]{1,0:T(1,128)}, f32[64,128]{1,0:T(8,128)}, f32[128,128]{1,0:T(8,128)}, /*index=5...) custom-call(bf16[16,192,384]{2,1,0:T(8,128)(2,1)} %get-tuple-element, ...), custom_call_target="tpu_custom_call" | custom-call | tf_op jit(solution)/shard_map/loss/pallas_call | solution.py:835
  430.8 93.6 %between_updates_back.2 = (f32[128,640]{1,0:T(8,128)}, f32[128,128]{1,0:T(8,128)}, f32[24,128,384]{2,1,0:T(8,128)}, bf16[24,128,384]{2,1,0:T(8,128)(2,1)}, f32[1...) custom-call(bf16[16,192,384]{2,1,0:T(8,128)(2,1)} %get-tuple-element.156.refs_0_, ...), custom_call_target="tpu_custom_call" | custom-call | tf_op jit(solution)/shard_map/between_updates_back/pallas_call | solution.py:835
  524.4 1.6 pad_maximum_fusion
  526.1 102.3 %layer_end_back.1 = (f32[128,640]{1,0:T(8,128)}, f32[128,128]{1,0:T(8,128)}, f32[24,128,384]{2,1,0:T(8,128)}, bf16[24,128,384]{2,1,0:T(8,128)(2,1)}, f32[128,128...) custom-call(bf16[16,192,384]{2,1,0:T(8,128)(2,1)} %get-tuple-element, ...), custom_call_target="tpu_custom_call" | custom-call | tf_op jit(solution)/shard_map/layer_end_back/pallas_call | solution.py:835
  628.5 1.7 pad_maximum_fusion.1
  630.2 105.4 %between_updates_back.3 = (f32[128,640]{1,0:T(8,128)}, f32[128,128]{1,0:T(8,128)}, f32[24,128,384]{2,1,0:T(8,128)}, bf16[24,128,384]{2,1,0:T(8,128)(2,1)}, f32[1...) custom-call(bf16[16,192,384]{2,1,0:T(8,128)(2,1)} %get-tuple-element.170.refs_0_, ...), custom_call_target="tpu_custom_call" | custom-call | tf_op jit(solution)/shard_map/between_updates_back/pallas_call | solution.py:835
  735.6 73.6 %first_state_back.1 = (f32[80,128]{1,0:T(8,128)}, f32[24,128,128]{2,1,0:T(8,128)}, f32[128,384]{1,0:T(8,128)}, f32[128,640]{1,0:T(8,128)}, f32[128,128]{1,0:T(8,128)}) custom-call(s32[24,1,384]{2,1,0:T(1,128)} %compare_select_fusion.refs_0_, bf16[16,192,384]{2,1,0:T(8,128)(2,1)} %get-tuple-element.176.refs_1_, ...), custom_call_target="tpu_custom_call" | custom-call | tf_op jit(solution)/shard_map/first_state_back/pallas_call | solution.py:835
  809.2 1.9 reduce_sum.9
  811.2 1.0 fusion.14.refs_5_
  812.1 2.1 fusion.refs_6_
  814.2 46.2 %reduce_rest.1.refs_0_ = f32[2432,128]{1,0:T(8,128)} custom-call(f32[128,640]{1,0:T(8,128)} %get-tuple-element.187.refs_0_, f32[128,640]{1,0:T(8,128)} %get-tuple-element.188.refs_1_, f32[128,128]{1,0:T(8,128)} %get-tuple-element.189.refs_2_, f32[64,128]{1,0:T(8,128)} %get-tuple-element.190.refs_3_, f32[80,128]{1,0:T(8,128)} %get-tuple-element.191.refs_4_, ...), custom_call_target="tpu_custom_call" | custom-call | tf_op jit(solution)/shard_map/reduce_rest/pallas_call | solution.py:1222
  860.4 12.6 %update.1 = (f32[1,1]{1,0:T(1,128)}, f32[1,1]{1,0:T(1,128)}, f32[1,1]{1,0:T(1,128)}, f32[66,128]{1,0:T(8,128)}, f32[66,128]{1,0:T(8,128)}, /*index=5*/f32[66,128...) custom-call(f32[2432,128]{1,0:T(8,128)} %reduce_rest.1.refs_0_, ...), custom_call_target="tpu_custom_call" | custom-call | tf_op jit(solution)/shard_map/update/pallas_call | solution.py:1315
  (24 shorter events, 0.3 us)
Async XLA Ops:
  7.2 8.1 copy-start
  7.2 9.4 %copy-start.3 = (s32[2,384]{1,0:T(2,128)S(1)}, s32[2,384]{1,0:T(2,128)}, u32[]{:S(2)}) copy-start(s32[2,384]{1,0:T(2,128)} %param.32) | copy-start | bytes 9220
  7.2 9.4 %copy-start.4 = (s32[2,384]{1,0:T(2,128)S(1)}, s32[2,384]{1,0:T(2,128)}, u32[]{:S(2)}) copy-start(s32[2,384]{1,0:T(2,128)} %param.31) | copy-start | bytes 9220
  7.2 728.4 %all-reduce.6.cloned.1.call-start = ((), (), s32[]{:S(2)}) async-start(), calls=%async_computation | async-start | bytes 2490368 | tf_op jit(solution)/shard_map/psum | solution.py:1633
  8.2 15.7 %collective-permute-start.1 = (s32[2,24,192]{2,0,1:T(2,128)S(1)}, s32[2,24,192]{2,0,1:T(2,128)S(1)}, u32[]{:S(2)}, u32[]{:S(2)}) collective-permute-start(s32[2,24,192]{2,0,1:T(2,128)S(1)} %bitcast.61), channel_id=1, source_target_pairs={{0,16},{1,0},{2,17},{3,1},{4,20},{5,4},{6,21},{7,5},{8,24},{9,8},{... | collective-permute-start | bytes 110600 | tf_op jit(solution)/shard_map/ppermute | solution.py:1118
  12.3 11.6 %collective-permute-start = (s32[2,24,192]{2,0,1:T(2,128)S(1)}, s32[2,24,192]{2,0,1:T(2,128)S(1)}, u32[]{:S(2)}, u32[]{:S(2)}) collective-permute-start(s32[2,24,192]{2,0,1:T(2,128)S(1)} %bitcast.62), channel_id=1, source_target_pairs={{0,0},{1,16},{2,1},{3,17},{4,4},{5,20},{6,5},{7,21},{8,8},{9,24},{... | collective-permute-start | bytes 110600 | tf_op jit(solution)/shard_map/ppermute | solution.py:1117
  430.8 93.6 %copy-start.1 = (f32[512,128]{1,0:T(8,128)S(1)}, f32[512,128]{1,0:T(8,128)}, u32[]{:S(2)}) copy-start(f32[512,128]{1,0:T(8,128)} %get-tuple-element.183) | copy-start | bytes 786436
  430.8 93.6 %copy-start.2 = (f32[128,128]{1,0:T(8,128)S(1)}, f32[128,128]{1,0:T(8,128)}, u32[]{:S(2)}) copy-start(f32[128,128]{1,0:T(8,128)} %get-tuple-element.182) | copy-start | bytes 196612
  526.1 334.3 %all-reduce.8.cloned.1.call-start = ((), (), s32[]{:S(2)}) async-start(), calls=%async_computation.1 | async-start | bytes 2359296 | tf_op jit(solution)/shard_map/psum | solution.py:1687
Sparse Core Ops, SparseCore 0:
  526.2 153.0 all-reduce.5
  685.6 149.9 all-reduce.7
